TPU v7x, 32 devices: a whole 2x2x4 slice. The times are simulated.
32 devices in a mesh: section: 2 (over y), dp: 4 (over x, core), expert: 4 (over z).
Axes of the slice: x: 2, y: 2, z: 4, core: 2. Of those that a mesh axis runs over, the one named last changes fastest.
Arguments:
- activations: bfloat16 [2, 256, 4096], P('section', 'expert'), may hold values from -6 to 6
- routes: int32 [2, 256, 8], P('section', 'expert'), may hold values from 0 to 31, all different within a row; in each aligned block of 64 rows (0 to 63, 64 to 127, ..., all dimensions but the last counted through in order) at most 16 rows name the same one
- gate_weights: float32 [2, 256, 8], P('section', 'expert'), may hold values from 0.05 to 0.5
- norm_gain: bfloat16 [4096], replicated, may hold values from 0.099609375 to 1.8984375
- gate_up_weights: bfloat16 [32, 2, 1536, 4096], P('expert', None, 'dp'), may hold values from -0.09375 to 0.09375
- down_weights: bfloat16 [32, 1536, 4096], P('expert', None, 'dp'), may hold values from -0.15625 to 0.15625
Outputs:
- arrived: bfloat16 [2, 256, 4096], P('section', 'expert', 'dp')
Inputs may be any that keep to these rules, and one draw needn't show every extreme that they name: `routes`: each token names 8 different experts. Among the 64 tokens of one device (aligned blocks of 64 tokens), no expert is named more than 16 times, and in some blocks one expert is named exactly 16 times.
All inputs are finite; a program needn't handle non-finite values.
Results may differ from a plain program's by a relative error of at most 0.005.
Values may be sent and summed in bfloat16 or wider, within the bound.
No kernel may reach another device: no remote copies, remote signals or barrier semaphores. Data moves between devices by JAX's collectives and lax.ppermute only.
A program may use at most 128 MiB of HBM per device.

v0:
```python
import jax
import jax.numpy as jnp
from jax import lax
from jax.sharding import PartitionSpec as P


def passed_along(block, axis, distance):
    devices = range(lax.axis_size(axis))
    route = [((i - distance) % len(devices), i) for i in devices]
    return lax.ppermute(block, axis, route)


def body(activations, routes, gate_weights, norm_gain, gate_up_weights, down_weights):
    tokens_here = activations[0]
    token_count, feature_count = tokens_here.shape
    top_count = routes.shape[2]
    local_experts = gate_up_weights.shape[0]
    expert_devices = lax.axis_size("expert")
    dp_devices = lax.axis_size("dp")
    total_experts = local_experts * expert_devices
    window = max(1, token_count * top_count // (total_experts * dp_devices))
    capacity = window * dp_devices
    slice_width = feature_count // dp_devices
    dp_place = lax.axis_index("dp")
    widened = tokens_here.astype(jnp.float32)
    mean_square = jnp.mean(widened * widened, axis=-1, keepdims=True)
    normed = (widened * lax.rsqrt(mean_square + 1e-06) * norm_gain.astype(jnp.float32)).astype(
        jnp.bfloat16
    )
    flat_routes = routes[0].reshape(-1)
    experts_iota = jnp.arange(total_experts, dtype=jnp.int32)
    onehot = (flat_routes[:, None] == experts_iota[None, :]).astype(jnp.int32)
    slot_ranks = jnp.sum((jnp.cumsum(onehot, axis=0) - onehot) * onehot, axis=1)
    targets = flat_routes * capacity + slot_ranks
    contract_rows = (((0,), (0,)), ((), ()))
    slot_iota = jnp.arange(total_experts * capacity, dtype=jnp.int32)
    matches = (targets[:, None] == slot_iota[None, :]).reshape(
        token_count, top_count, total_experts * capacity
    )
    placing = jnp.any(matches, axis=1).astype(jnp.bfloat16)
    normed_slice = lax.dynamic_slice_in_dim(normed, dp_place * slice_width, slice_width, 1)
    outgoing = lax.dot_general(
        placing, normed_slice, contract_rows, preferred_element_type=jnp.float32
    )
    outgoing = outgoing.astype(jnp.bfloat16).reshape(total_experts, capacity, slice_width)
    arriving = lax.all_to_all(outgoing, "expert", split_axis=0, concat_axis=0, tiled=True)
    arriving = arriving.reshape(expert_devices, local_experts, capacity, slice_width)
    weights_part = gate_up_weights
    gate_up = jnp.einsum(
        "seck,ejhk->jsech",
        lax.all_gather(arriving, "dp", axis=3, tiled=True),
        weights_part,
        preferred_element_type=jnp.float32,
    )
    hidden_act = (jax.nn.silu(gate_up[0]) * gate_up[1]).astype(jnp.bfloat16)
    weights_part = down_weights
    summed = jnp.einsum(
        "sech,ehf->secf",
        lax.all_gather(hidden_act, "dp", axis=3, tiled=True),
        weights_part,
        preferred_element_type=jnp.float32,
    )
    expert_out = summed.astype(jnp.bfloat16)
    returned = lax.all_to_all(expert_out, "expert", split_axis=0, concat_axis=0, tiled=True)
    returned_flat = returned.reshape(total_experts * capacity, slice_width)
    picked = jnp.take(returned_flat, targets, axis=0).reshape(token_count, top_count, slice_width)
    branch = jnp.sum(picked.astype(jnp.float32) * gate_weights[0][:, :, None], axis=1)
    residual = lax.dynamic_slice_in_dim(widened, dp_place * slice_width, slice_width, 1)
    finished = (residual + branch).astype(jnp.bfloat16)
    arrived = passed_along(finished, "section", 1)
    return arrived[None]


def solution(mesh):
    placed = (
        P("section", "expert", None),
        P("section", "expert", None),
        P("section", "expert", None),
        P(),
        P("expert", None, "dp", None),
        P("expert", None, "dp"),
    )
    return jax.shard_map(
        body, mesh=mesh, in_specs=placed, out_specs=P("section", "expert", "dp"), check_vma=False
    )
```

profile of v0, /device:TPU:0, one launch (start us, length us, event | category | flops | bytes accessed | tf_op | source)
XLA Modules:
  0.0 184.4 jit_solution(1469341054795439052)
XLA Ops:
  6.5 0.8 copy.35
  7.3 0.1 eq.40
  7.4 0.1 reshape_squeeze.3
  7.5 1.2 fusion.30
  8.7 1.2 multiply_reduce_fusion.1
  9.9 1.2 reduce-window.6
  11.1 0.2 slice_reduce_fusion
  11.4 0.1 fusion.27
  11.5 0.1 reduce_sum.32
  11.6 0.7 compare_and_fusion
  12.4 0.4 fusion.16
  12.8 0.7 dynamic-slice.1
  13.5 0.5 convolution_convert_fusion
  14.0 31.8 %all_to_all.10 = bf16[32,16,1024]{2,1,0:T(8,128)(2,1)S(1)} all-to-all(bf16[32,16,1024]{2,1,0:T(8,128)(2,1)S(1)} %bitcast.83), channel_id=1, replica_groups=mesh['section'=2,'dp'=4,'expert'=4] {'expert'}, dimensions={0} | all-to-all | bytes 2097152 | tf_op jit(solution)/shard_map/all_to_all | solution.py:46
  45.9 1.1 copy.41
  47.0 33.7 %all-gather.3.cloned.1.call-done = bf16[4,8,16,4096]{3,2,0,1:T(8,128)(2,1)} async-done(((bf16[4,8,16,1024]{3,2,0,1:T(8,128)(2,1)}), bf16[4,8,16,4096]{3,2,0,1:T(8,128)(2,1)}) %all-gather.3.cloned.1.call-update) | async-done | bytes 4194320 | tf_op jit(solution)/shard_map/all_gather | solution.py:51
  80.7 22.5 %fusion.8 = f32[2,4,8,16,384]{4,3,0,1,2:T(8,128)S(1)} fusion(bf16[8,2,384,4096]{3,2,1,0:T(8,128)(2,1)} %param.10, bf16[4,8,16,4096]{3,2,0,1:T(8,128)(2,1)} %all-gather.3.cloned.1.call-done), kind=kOutput, calls=%fused_computation.9 | convolution fusion | flops 3221225472 | bytes 56098816 | tf_op jit(solution)/shard_map/seck,ejhk->jsech/dot_general | solution.py:49
  103.2 1.0 fusion.18
  104.2 19.8 %all-gather.5.cloned.1.call-done = bf16[4,8,16,1536]{3,2,0,1:T(8,128)(2,1)} async-done(((bf16[4,8,16,384]{3,2,0,1:T(8,128)(2,1)}), bf16[4,8,16,1536]{3,2,0,1:T(8,128)(2,1)}) %all-gather.5.cloned.1.call-update) | async-done | bytes 1572880 | tf_op jit(solution)/shard_map/all_gather | solution.py:59
  124.0 13.1 %fusion.13 = bf16[4,8,16,1024]{3,2,0,1:T(8,128)(2,1)S(1)} fusion(bf16[4,8,16,1536]{3,2,0,1:T(8,128)(2,1)} %all-gather.5.cloned.1.call-done, bf16[8,1536,1024]{2,1,0:T(8,128)(2,1)} %param.11), kind=kOutput, calls=%fused_computation.10 | convolution fusion | flops 1611137024 | bytes 27787264 | tf_op jit(solution)/shard_map/sech,ehf->secf/dot_general | solution.py:57
  137.2 1.1 copy.43
  138.2 4.6 %all-to-all-start.1 = ((bf16[4,8,16,1024]{3,2,1,0:T(8,128)(2,1)}), bf16[4,8,16,1024]{3,2,1,0:T(8,128)(2,1)S(1)}, u32[]{:S(2)}, u32[]{:S(2)}) async-start(bf16[4,8,16,1024]{3,2,1,0:T(8,128)(2,1)} %copy.43), calls=%async_computation.1 | async-start | bytes 2097152 | tf_op jit(solution)/shard_map/all_to_all | solution.py:64
  142.8 0.1 copy.44
  142.9 0.1 mul.80
  143.0 0.1 copy.39
  143.1 0.1 copy.45
  143.2 25.7 %all-to-all-done.1 = bf16[4,8,16,1024]{3,2,1,0:T(8,128)(2,1)S(1)} async-done(((bf16[4,8,16,1024]{3,2,1,0:T(8,128)(2,1)}), bf16[4,8,16,1024]{3,2,1,0:T(8,128)(2,1)S(1)}, u32[]{:S(2)}, u32[]{:S(2)}) %all-to-all-start.1) | async-done | bytes 1048608 | tf_op jit(solution)/shard_map/all_to_all | solution.py:64
  168.9 2.0 %gather_fusion = bf16[512,1024]{1,0:T(8,128)(2,1)S(1)} fusion(bf16[512,1024]{1,0:T(8,128)(2,1)S(1)} %bitcast.82, s32[1024]{0:T(1024)S(1)} %pad_clamp_fusion), kind=kCustom, calls=%fused_computation | custom fusion | bytes 2099200 | tf_op jit(solution)/shard_map/jit(_take)/gather | solution.py:66
  171.0 0.8 multiply_reduce_fusion
  171.9 1.5 collective-permute-start
  173.4 3.5 %collective-permute-done = bf16[64,1024]{1,0:T(8,128)(2,1)S(1)} collective-permute-done((bf16[64,1024]{1,0:T(8,128)(2,1)S(1)}, bf16[64,1024]{1,0:T(8,128)(2,1)S(1)}, u32[]{:S(2)}, u32[]{:S(2)}) %collective-permute-start) | collective-permute-done | bytes 131104 | tf_op jit(solution)/shard_map/ppermute | solution.py:10
  176.9 0.7 copy.53
  (18 shorter events, 0.3 us)
Async XLA Ops:
  6.5 74.2 %all-gather.3.cloned.1.call-start = ((), (), s32[]{:S(2)}) async-start(), calls=%async_computation.2 | async-start | bytes 5242880 | tf_op jit(solution)/shard_map/all_gather | solution.py:51
  47.0 77.0 %all-gather.5.cloned.1.call-start = ((), (), s32[]{:S(2)}) async-start(), calls=%async_computation.3 | async-start | bytes 1966080 | tf_op jit(solution)/shard_map/all_gather | solution.py:59
  137.1 5.7 %copy-start = (s32[1,64,8]{1,2,0:T(8,128)S(1)}, s32[1,64,8]{1,2,0:T(8,128)}, u32[]{:S(2)}) copy-start(s32[1,64,8]{1,2,0:T(8,128)} %param.7) | copy-start | bytes 6148
  137.1 6.0 %copy-start.1 = (f32[1,64,8]{1,2,0:T(8,128)S(1)}, f32[1,64,8]{1,2,0:T(8,128)}, u32[]{:S(2)}) copy-start(f32[1,64,8]{1,2,0:T(8,128)} %param.8) | copy-start | bytes 6148
  138.2 30.7 %all-to-all-start.1 = ((bf16[4,8,16,1024]{3,2,1,0:T(8,128)(2,1)}), bf16[4,8,16,1024]{3,2,1,0:T(8,128)(2,1)S(1)}, u32[]{:S(2)}, u32[]{:S(2)}) async-start(bf16[4,8,16,1024]{3,2,1,0:T(8,128)(2,1)} %copy.43), calls=%async_computation.1 | async-start | bytes 2097152 | tf_op jit(solution)/shard_map/all_to_all | solution.py:64
  171.9 5.0 %collective-permute-start = (bf16[64,1024]{1,0:T(8,128)(2,1)S(1)}, bf16[64,1024]{1,0:T(8,128)(2,1)S(1)}, u32[]{:S(2)}, u32[]{:S(2)}) collective-permute-start(bf16[64,1024]{1,0:T(8,128)(2,1)S(1)} %fusion.21), channel_id=1, source_target_pairs={{16,0},{0,16},{17,1},{1,17},{18,2},{2,18},{19,3},{3,19},{20,4},{4,... | collective-permute-start | bytes 393224 | tf_op jit(solution)/shard_map/ppermute | solution.py:10
Sparse Core Ops, SparseCore 0:
  47.1 33.5 all-gather.2
  104.3 19.6 all-gather.4
where the time goes:
time: 185 us; the launch traced here: 184 us
  waiting for transfers between devices  82.7 us (45%)
  matrix products  36.1 us (20%)
  blocking collectives  31.8 us (17%)
  between operations  13.5 us (7%)
  local copies, waits for them, and re-layouts  7.31 us (4%)
  other arithmetic  6.67 us (4%)
  starting transfers between devices  6.18 us (3%)
    all_gather x1, waiting for transfers between devices, body(): lax.all_gather(arriving, 'dp', axis=3, tiled=True)  33.7 us
    all_to_all x1, blocking collectives, body(): lax.all_to_all(outgoing, 'expert', split_axis=0, concat_axis=0, tiled=True)  31.8 us
    all_to_all x1, waiting for transfers between devices, body(): lax.all_to_all(expert_out, 'expert', split_axis=0, concat_axis=0, tiled=T...  25.7 us
    dot_general x1, matrix products, body(): jnp.einsum('seck,ejhk->jsech', lax.all_gather(arriving, 'dp', axis=3, til...  22.5 us
    all_gather x1, waiting for transfers between devices, body(): lax.all_gather(hidden_act, 'dp', axis=3, tiled=True)  19.8 us
    dot_general x1, matrix products, body(): jnp.einsum('sech,ehf->secf', lax.all_gather(hidden_act, 'dp', axis=3, til...  13.1 us
    all_to_all x1, starting transfers between devices, body(): lax.all_to_all(expert_out, 'expert', split_axis=0, concat_axis=0, tiled=T...  4.6 us
  transfers between devices with their start and end apart: 4, of which 4 were waited for; matrix products, arithmetic and copies ran while one was open for 0% of the time, Pallas kernels for 0%

commit v1 on v0

--- a/solution.py
+++ b/solution.py
@@ -1,16 +1,404 @@
+import functools
+
 import jax
 import jax.numpy as jnp
 from jax import lax
+from jax.experimental import pallas as pl
+from jax.experimental.pallas import tpu as pltpu
 from jax.sharding import PartitionSpec as P
 
-
-def passed_along(block, axis, distance):
-    devices = range(lax.axis_size(axis))
-    route = [((i - distance) % len(devices), i) for i in devices]
-    return lax.ppermute(block, axis, route)
-
-
-def body(activations, routes, gate_weights, norm_gain, gate_up_weights, down_weights):
+CONTRACT_LAST = (((1,), (1,)), ((), ()))
+IN_VMEM = pl.BlockSpec(memory_space=pltpu.VMEM)
+IN_SMEM = pl.BlockSpec(memory_space=pltpu.SMEM)
+ANYWHERE = pl.BlockSpec(memory_space=pl.ANY)
+MIB = 1 << 20
+
+
+def params(mib):
+    return pltpu.CompilerParams(vmem_limit_bytes=mib * MIB)
+
+
+def cost(flops, moved):
+    return pl.CostEstimate(flops=int(flops), bytes_accessed=int(moved), transcendentals=0)
+
+
+def pinned(array):
+    return pltpu.with_memory_space_constraint(array, pltpu.VMEM)
+
+
+def shifted(block, axis, distance):
+    count = lax.axis_size(axis)
+    return lax.ppermute(block, axis, [((i - distance) % count, i) for i in range(count)])
+
+
+def flipped(block, axis, bit):
+    return lax.ppermute(block, axis, [(i, i ^ bit) for i in range(lax.axis_size(axis))])
+
+
+def norm_kernel(place, tokens, gain, normed, own):
+    widened = tokens[...].astype(jnp.float32)
+    mean_square = jnp.mean(widened * widened, axis=-1, keepdims=True)
+    rows = widened * lax.rsqrt(mean_square + 1e-06) * gain[...].astype(jnp.float32)
+    normed[...] = rows.astype(jnp.bfloat16)
+    width = own.shape[1]
+    start = pl.multiple_of(place[0] * width, width)
+    own[...] = normed[:, pl.ds(start, width)]
+
+
+def normalize(place, tokens, gain, width):
+    count, features = tokens.shape
+    return pl.pallas_call(
+        norm_kernel,
+        out_shape=(
+            jax.ShapeDtypeStruct((count, features), jnp.bfloat16),
+            jax.ShapeDtypeStruct((count, width), jnp.bfloat16),
+        ),
+        in_specs=[IN_SMEM, IN_VMEM, IN_VMEM],
+        out_specs=(IN_VMEM, IN_VMEM),
+        compiler_params=params(6),
+    )(place, tokens, gain)
+
+
+def plan_kernel(capacity, blocks, *refs):
+    first = refs[0]
+    routes = refs[1 : 1 + blocks]
+    weights = refs[1 + blocks : 1 + 2 * blocks]
+    placing, high, low = refs[1 + 2 * blocks :]
+    tokens, top = routes[0].shape
+    slots = placing.shape[1]
+    lane = lax.broadcasted_iota(jnp.int32, (tokens, slots), 1)
+    expert = first[0] + lane // capacity
+    rank_of_lane = lane % capacity
+    row = lax.broadcasted_iota(jnp.int32, (tokens, tokens), 0)
+    column = lax.broadcasted_iota(jnp.int32, (tokens, tokens), 1)
+    earlier = jnp.where(column < row, 1.0, 0.0).astype(jnp.bfloat16)
+    for block in range(blocks):
+        named = jnp.zeros((tokens, slots), jnp.float32)
+        weight = jnp.zeros((tokens, slots), jnp.float32)
+        for k in range(top):
+            hit = routes[block][:, k : k + 1] == expert
+            named = jnp.where(hit, 1.0, named)
+            weight = jnp.where(hit, weights[block][:, k : k + 1], weight)
+        ranks = jnp.dot(earlier, named.astype(jnp.bfloat16), preferred_element_type=jnp.float32)
+        here = jnp.where((named > 0.5) & (ranks.astype(jnp.int32) == rank_of_lane), 1.0, 0.0)
+        placing[block] = here.T.astype(jnp.bfloat16)
+        scaled = here * weight
+        coarse = scaled.astype(jnp.bfloat16)
+        high[block] = coarse
+        low[block] = (scaled - coarse.astype(jnp.float32)).astype(jnp.bfloat16)
+
+
+def plan(first, routes, weights, slots, capacity):
+    blocks, tokens = len(routes), routes[0].shape[0]
+    return pl.pallas_call(
+        functools.partial(plan_kernel, capacity, blocks),
+        out_shape=(
+            jax.ShapeDtypeStruct((blocks, slots, tokens), jnp.bfloat16),
+            jax.ShapeDtypeStruct((blocks, tokens, slots), jnp.bfloat16),
+            jax.ShapeDtypeStruct((blocks, tokens, slots), jnp.bfloat16),
+        ),
+        in_specs=[IN_SMEM] + [IN_VMEM] * (2 * blocks),
+        out_specs=(IN_VMEM,) * 3,
+        compiler_params=params(6),
+    )(first, *routes, *weights)
+
+
+def up_part(weights, target, semaphore, place, quarter):
+    width = target.shape[-1]
+    start = pl.multiple_of((place ^ quarter) * width, width)
+    return pltpu.make_async_copy(weights.at[:, :, :, pl.ds(start, width)], target, semaphore)
+
+
+def down_part(weights, target, semaphore, place, quarter):
+    rows = target.shape[1]
+    start = pl.multiple_of((place ^ quarter) * rows, rows)
+    return pltpu.make_async_copy(weights.at[:, pl.ds(start, rows), :], target, semaphore)
+
+
+def stage_kernel(quarters, place, weights, *refs):
+    targets, semaphores = refs[: len(quarters)], refs[-1]
+    copies = [
+        up_part(weights, targets[i], semaphores.at[i], place[0], quarter)
+        for i, quarter in enumerate(quarters)
+    ]
+    for copy in copies:
+        copy.start()
+    for copy in copies:
+        copy.wait()
+
+
+def stage(place, weights, quarters, width):
+    shape = weights.shape[:-1] + (width,)
+    count = len(quarters)
+    return pl.pallas_call(
+        functools.partial(stage_kernel, quarters),
+        out_shape=(pltpu.VMEM(shape, weights.dtype),) * count,
+        in_specs=[IN_SMEM, ANYWHERE],
+        out_specs=(IN_VMEM,) * count,
+        scratch_shapes=[pltpu.SemaphoreType.DMA((count,))],
+        compiler_params=params(4),
+        cost_estimate=cost(0, 2 * count * weights.size // 2),
+    )(place, weights)
+
+
+def up_kernel(opts, place, placing, normed, arrived, weights, *refs):
+    quarter, has_total, finish, fetch_up, fetch_down, experts = opts
+    refs = list(refs)
+    total_in = refs.pop(0) if has_total else None
+    up_source = refs.pop(0) if fetch_up else None
+    down_source = refs.pop(0) if fetch_down else None
+    result = refs.pop(0)
+    up_targets = [refs.pop(0) for _ in fetch_up]
+    down_targets = [refs.pop(0) for _ in fetch_down]
+    gathered, rows = refs.pop(0), refs.pop(0)
+    copies = []
+    if fetch_up or fetch_down:
+        semaphores = refs.pop(0)
+        for i, part in enumerate(fetch_up):
+            copies.append(up_part(up_source, up_targets[i], semaphores.at[i], place[0], part))
+        for i, part in enumerate(fetch_down):
+            at = semaphores.at[len(fetch_up) + i]
+            copies.append(down_part(down_source, down_targets[i], at, place[0], part))
+    for copy in copies:
+        copy.start()
+    blocks, slots, tokens = placing.shape
+    local_experts, _, hidden, width = weights.shape
+    capacity = slots // local_experts
+    start = pl.multiple_of((place[0] ^ quarter) * width, width)
+    rows[0:tokens] = normed[:, pl.ds(start, width)]
+    rows[tokens:] = arrived[...]
+    for block in range(blocks):
+        picked = jnp.dot(
+            placing[block],
+            rows[block * tokens : (block + 1) * tokens],
+            preferred_element_type=jnp.float32,
+        ).astype(jnp.bfloat16)
+        gathered[:, block * capacity : (block + 1) * capacity, :] = picked.reshape(
+            local_experts, capacity, width
+        )
+
+    def one(expert, carry):
+        own = gathered[expert]
+        parts = []
+        for side in range(2):
+            value = lax.dot_general(
+                own, weights[expert, side], CONTRACT_LAST, preferred_element_type=jnp.float32
+            )
+            if has_total:
+                value = value + total_in[expert, side]
+            parts.append(value)
+        if finish:
+            gate, up = parts
+            result[expert - experts[0]] = (gate / (1.0 + jnp.exp(-gate)) * up).astype(jnp.bfloat16)
+        else:
+            result[expert, 0] = parts[0]
+            result[expert, 1] = parts[1]
+        return carry
+
+    lax.fori_loop(experts[0], experts[1], one, 0)
+    for copy in copies:
+        copy.wait()
+
+
+def up_step(place, placing, normed, arrived, weights, total, quarter, finish, experts, up=None, down=None):
+    fetch_up, up_source = up if up else ((), None)
+    fetch_down, down_source = down if down else ((), None)
+    blocks, slots, tokens = placing.shape
+    local_experts, _, hidden, width = weights.shape
+    depth = blocks * (slots // local_experts)
+    operands = [place, placing, normed, arrived, pinned(weights)]
+    in_specs = [IN_SMEM] + [IN_VMEM] * 4
+    if total is not None:
+        operands.append(pinned(total))
+        in_specs.append(IN_VMEM)
+    if fetch_up:
+        operands.append(up_source)
+        in_specs.append(ANYWHERE)
+    if fetch_down:
+        operands.append(down_source)
+        in_specs.append(ANYWHERE)
+    count = experts[1] - experts[0]
+    if finish:
+        shapes = [jax.ShapeDtypeStruct((count, depth, hidden), jnp.bfloat16)]
+    else:
+        shapes = [pltpu.VMEM((local_experts, 2, depth, hidden), jnp.float32)]
+    shapes += [pltpu.VMEM(weights.shape, weights.dtype) for _ in fetch_up]
+    if fetch_down:
+        shapes += [
+            pltpu.VMEM((local_experts, hidden, down_source.shape[2]), down_source.dtype)
+            for _ in fetch_down
+        ]
+    scratch = [
+        pltpu.VMEM((local_experts, depth, width), jnp.bfloat16),
+        pltpu.VMEM((blocks * tokens, width), jnp.bfloat16),
+    ]
+    copies = len(fetch_up) + len(fetch_down)
+    if copies:
+        scratch.append(pltpu.SemaphoreType.DMA((copies,)))
+    return pl.pallas_call(
+        functools.partial(
+            up_kernel, (quarter, total is not None, finish, fetch_up, fetch_down, experts)
+        ),
+        out_shape=tuple(shapes),
+        in_specs=in_specs,
+        out_specs=(IN_VMEM,) * len(shapes),
+        scratch_shapes=scratch,
+        compiler_params=params(8),
+        cost_estimate=cost(2 * count * 256 * 2 * hidden * width, 2 * weights.size),
+    )(*operands)
+
+
+def down_kernel(opts, *refs):
+    has_total, last, pieces, local_experts = opts
+    refs = list(refs)
+    acts = [refs.pop(0) for _ in range(pieces)]
+    weights = [refs.pop(0) for _ in range(pieces)]
+    total_in = refs.pop(0) if has_total else None
+    if last:
+        high, low, tokens, place = [refs.pop(0) for _ in range(4)]
+        results = [refs.pop(0) for _ in range(high.shape[0])]
+        slots_out = refs.pop(0)
+    else:
+        result = refs.pop(0)
+
+    def one(expert, carry):
+        value = None
+        for i in range(pieces):
+            part = jnp.dot(acts[i][expert], weights[i][expert], preferred_element_type=jnp.float32)
+            value = part if value is None else value + part
+        if has_total:
+            value = value + total_in[expert]
+        if last:
+            blocks = slots_out.shape[0]
+            capacity = value.shape[0] // blocks
+            rounded = value.astype(jnp.bfloat16)
+            for block in range(blocks):
+                at = pl.ds(pl.multiple_of(expert * capacity, capacity), capacity)
+                slots_out[block, at, :] = rounded[block * capacity : (block + 1) * capacity]
+        else:
+            result[expert] = value
+        return carry
+
+    lax.fori_loop(0, local_experts, one, 0)
+    if last:
+        width = tokens.shape[1] // (tokens.shape[1] // slots_out.shape[2])
+        start = pl.multiple_of(place[0] * width, width)
+        for block in range(len(results)):
+            value = jnp.dot(
+                high[block], slots_out[block], preferred_element_type=jnp.float32
+            ) + jnp.dot(low[block], slots_out[block], preferred_element_type=jnp.float32)
+            if block == 0:
+                value = value + tokens[:, pl.ds(start, width)].astype(jnp.float32)
+            results[block][...] = value.astype(jnp.bfloat16)
+
+
+def down_step(acts, weights, total, finish=None):
+    pieces = len(acts)
+    local_experts, depth, hidden = acts[0].shape
+    width = weights[0].shape[2]
+    operands = list(acts) + [pinned(w) for w in weights]
+    if total is not None:
+        operands.append(pinned(total))
+    in_specs = [IN_VMEM] * len(operands)
+    scratch = []
+    if finish:
+        high, low, tokens, place = finish
+        operands += [high, low, tokens, place]
+        in_specs += [IN_VMEM] * 3 + [IN_SMEM]
+        blocks, count, slots = high.shape
+        shapes = (jax.ShapeDtypeStruct((count, width), jnp.bfloat16),) * blocks
+        scratch = [pltpu.VMEM((blocks, slots, width), jnp.bfloat16)]
+    else:
+        shapes = pltpu.VMEM((local_experts, depth, width), jnp.float32)
+    return pl.pallas_call(
+        functools.partial(
+            down_kernel, (total is not None, finish is not None, pieces, local_experts)
+        ),
+        out_shape=shapes,
+        in_specs=in_specs,
+        out_specs=(IN_VMEM,) * len(shapes) if finish else IN_VMEM,
+        scratch_shapes=scratch,
+        compiler_params=params(8),
+        cost_estimate=cost(
+            2 * pieces * local_experts * 256 * hidden * width, 2 * pieces * weights[0].size
+        ),
+    )(*operands)
+
+
+def sum_kernel(*refs):
+    *parts, result = refs
+    value = parts[0][...].astype(jnp.float32)
+    for part in parts[1:]:
+        value = value + part[...].astype(jnp.float32)
+    result[0] = value.astype(jnp.bfloat16)
+
+
+def gathered_tokens(activations, routes, gate_weights, norm_gain, gate_up_weights, down_weights):
+    tokens = activations[0]
+    token_count, features = tokens.shape
+    local_experts = gate_up_weights.shape[0]
+    rows = lax.axis_size("expert")
+    dp_devices = lax.axis_size("dp")
+    sections = lax.axis_size("section")
+    capacity = token_count * routes.shape[2] // (local_experts * rows)
+    slots = local_experts * capacity
+    width = features // dp_devices
+    place = lax.axis_index("dp").astype(jnp.int32).reshape(1)
+    first = (lax.axis_index("expert") * local_experts).astype(jnp.int32).reshape(1)
+
+    all_routes = [routes[0]] + [shifted(routes[0], "expert", j) for j in range(1, rows)]
+    all_weights = [gate_weights[0]] + [
+        shifted(gate_weights[0], "expert", j) for j in range(1, rows)
+    ]
+    normed, own = normalize(place, tokens, norm_gain.reshape(1, features), width)
+    blocks = [shifted(own, "expert", j) for j in range(1, rows)]
+    placing, high, low = plan(first, all_routes, all_weights, slots, capacity)
+    staged_0, staged_1 = stage(place, gate_up_weights, (0, 1), width)
+
+    mine = jnp.concatenate(blocks, axis=0)
+    across = flipped(mine, "dp", 2)
+    beside = flipped(mine, "dp", 1)
+    everyone = (0, local_experts)
+    half = local_experts // 2
+    step = functools.partial(up_step, place, placing, normed)
+    total, staged_2 = step(
+        mine, staged_0, None, 0, False, everyone, up=((2,), gate_up_weights)
+    )
+    total, staged_3 = step(
+        beside, staged_1, total, 1, False, everyone, up=((3,), gate_up_weights)
+    )
+    total, down_0, down_1 = step(
+        across, staged_2, total, 2, False, everyone, down=((0, 1), down_weights)
+    )
+    far = flipped(across, "dp", 1)
+    act, down_2, down_3 = step(
+        far, staged_3, total, 3, True, everyone, down=((2, 3), down_weights)
+    )
+
+    act_across = flipped(act, "dp", 2)
+    act_beside = flipped(act, "dp", 1)
+    act_far = flipped(act_across, "dp", 1)
+    summed = down_step([act, act_beside], [down_0, down_1], None)
+    partial = down_step(
+        [act_across, act_far], [down_2, down_3], summed, (high, low, tokens, place)
+    )
+    received = []
+    for j in range(rows):
+        route = [
+            (s * rows + e, ((s + 1) % sections) * rows + (e - j) % rows)
+            for s in range(sections)
+            for e in range(rows)
+        ]
+        received.append(lax.ppermute(partial[j], ("section", "expert"), route))
+    return pl.pallas_call(
+        sum_kernel,
+        out_shape=jax.ShapeDtypeStruct((1, token_count, width), jnp.bfloat16),
+        in_specs=[IN_VMEM] * rows,
+        out_specs=IN_VMEM,
+        compiler_params=params(6),
+    )(*received)
+
+def routed_rows(activations, routes, gate_weights, norm_gain, gate_up_weights, down_weights):
     tokens_here = activations[0]
     token_count, feature_count = tokens_here.shape
     top_count = routes.shape[2]
@@ -67,8 +455,21 @@
     branch = jnp.sum(picked.astype(jnp.float32) * gate_weights[0][:, :, None], axis=1)
     residual = lax.dynamic_slice_in_dim(widened, dp_place * slice_width, slice_width, 1)
     finished = (residual + branch).astype(jnp.bfloat16)
-    arrived = passed_along(finished, "section", 1)
+    arrived = shifted(finished, "section", 1)
     return arrived[None]
+
+
+def body(activations, routes, gate_weights, norm_gain, gate_up_weights, down_weights):
+    token_count, top_count = routes.shape[1], routes.shape[2]
+    local_experts = gate_up_weights.shape[0]
+    rows = lax.axis_size("expert")
+    capacity = token_count * top_count // (local_experts * rows)
+    few = token_count <= local_experts * capacity
+    aligned = capacity % 16 == 0 and token_count % 16 == 0
+    form = gathered_tokens if few and aligned and lax.axis_size("dp") == 4 else routed_rows
+    return form(
+        activations, routes, gate_weights, norm_gain, gate_up_weights, down_weights
+    )
 
 
 def solution(mesh):

time: 185 us -> 114 us (0.62)
  waiting for transfers between devices: 82.7 us -> 28.3 us
  Pallas kernels: 0 us -> 38.4 us
  matrix products: 36.1 us -> 0 us
  blocking collectives: 31.8 us -> 0 us
  starting transfers between devices: 6.18 us -> 24.6 us
  local copies, waits for them, and re-layouts: 7.31 us -> 21.6 us
  between operations: 13.5 us -> 0.22 us
  other arithmetic: 6.67 us -> 0.01 us
    all_gather x2 -> x0, waiting for transfers between devices: 53.5 us -> none  [the longest x1 33.7 us: body(): lax.all_gather(arriving, 'dp', axis=3, tiled=True)]
    pallas_call x0 -> x10, Pallas kernels: none -> 38.4 us  [the longest x4 21.2 us: up_step(): pl.pallas_call(functools.partial(up_kernel, (quarter, total is not None,...]
    dot_general x3 -> x0, matrix products: 36.1 us -> none  [the longest x1 22.5 us: body(): jnp.einsum('seck,ejhk->jsech', lax.all_gather(arriving, 'dp', axis=3, til...]
    all_to_all x1 -> x0, blocking collectives: 31.8 us -> none  [body(): lax.all_to_all(outgoing, 'expert', split_axis=0, concat_axis=0, tiled=True)]
    all_to_all x1 -> x0, waiting for transfers between devices: 25.7 us -> none  [body(): lax.all_to_all(expert_out, 'expert', split_axis=0, concat_axis=0, tiled=T...]
    ppermute x1 -> x19, waiting for transfers between devices: 3.49 us -> 28.3 us  [the longest x4 10.7 us: gathered_tokens(): received.append(lax.ppermute(partial[j], ('section', 'expert'), route))]
    ppermute x1 -> x19, starting transfers between devices: 1.54 us -> 24.6 us  [the longest x9 17.1 us: shifted(): lax.ppermute(block, axis, [((i - distance) % count, i) for i in range(cou...]
    unnamed x6 -> x24, local copies, waits for them, and re-layouts: 1.44 us -> 20.9 us
  transfers between devices with their start and end apart: 4 -> 19, of which waited for: 4 -> 6; matrix products, arithmetic and copies ran while one was open for 0% -> 1% of each run, Pallas kernels for 0% -> 25%
where the time goes in v1:
time: 114 us; the launch traced here: 113 us
  Pallas kernels  38.4 us (34%)
  waiting for transfers between devices  28.3 us (25%)
  starting transfers between devices  24.6 us (22%)
  local copies, waits for them, and re-layouts  21.6 us (19%)
    pallas_call x4, Pallas kernels, up_step(): pl.pallas_call(functools.partial(up_kernel, (quarter, total is not None,...  21.2 us
    unnamed x24, local copies, waits for them, and re-layouts  20.9 us
    ppermute x9, starting transfers between devices, shifted(): lax.ppermute(block, axis, [((i - distance) % count, i) for i in range(cou...  17.1 us
    ppermute x4, waiting for transfers between devices, gathered_tokens(): received.append(lax.ppermute(partial[j], ('section', 'expert'), route))  10.7 us
    ppermute x6, waiting for transfers between devices, flipped(): lax.ppermute(block, axis, [(i, i ^ bit) for i in range(lax.axis_size(axis...  9.65 us
    pallas_call x1, Pallas kernels, stage(): pl.pallas_call(functools.partial(stage_kernel, quarters), out_shape=(pltp...  8.19 us
    ppermute x9, waiting for transfers between devices, shifted(): lax.ppermute(block, axis, [((i - distance) % count, i) for i in range(cou...  7.95 us
    pallas_call x2, Pallas kernels, down_step(): pl.pallas_call(functools.partial(down_kernel, (total is not None, finish...  6.9 us
  transfers between devices with their start and end apart: 19, of which 6 were waited for; matrix products, arithmetic and copies ran while one was open for 1% of the time, Pallas kernels for 25%

profile of v1, /device:TPU:0, one launch (start us, length us, event | category | flops | bytes accessed | tf_op | source)
XLA Modules:
  0.0 113.2 jit_solution(6907411791391647701)
XLA Ops:
  0.7 1.0 copy-done.5
  2.1 3.1 %collective-permute-start.6 = (bf16[64,1024]{1,0:T(8,128)(2,1)S(1)}, bf16[64,1024]{1,0:T(8,128)(2,1)S(1)}, u32[]{:S(2)}, u32[]{:S(2)}) collective-permute-start(bf16[64,1024]{1,0:T(8,128)(2,1)S(1)} %get-tuple-element.28), channel_id=1, source_target_pairs={{3,0},{0,1},{1,2},{2,3},{7,4},{4,5},{5,6},{6,7},{11,8},{8,9},{9,10... | collective-permute-start | bytes 393224 | tf_op jit(solution)/shard_map/ppermute | solution.py:31
  5.1 2.6 %collective-permute-start.7 = (bf16[64,1024]{1,0:T(8,128)(2,1)S(1)}, bf16[64,1024]{1,0:T(8,128)(2,1)S(1)}, u32[]{:S(2)}, u32[]{:S(2)}) collective-permute-start(bf16[64,1024]{1,0:T(8,128)(2,1)S(1)} %get-tuple-element.28), channel_id=1, source_target_pairs={{2,0},{3,1},{0,2},{1,3},{6,4},{7,5},{4,6},{5,7},{10,8},{11,9},{8,1... | collective-permute-start | bytes 393224 | tf_op jit(solution)/shard_map/ppermute | solution.py:31
  7.7 1.3 %collective-permute-start.8 = (bf16[64,1024]{1,0:T(8,128)(2,1)S(1)}, bf16[64,1024]{1,0:T(8,128)(2,1)S(1)}, u32[]{:S(2)}, u32[]{:S(2)}) collective-permute-start(bf16[64,1024]{1,0:T(8,128)(2,1)S(1)} %get-tuple-element.28), channel_id=1, source_target_pairs={{1,0},{2,1},{3,2},{0,3},{5,4},{6,5},{7,6},{4,7},{9,8},{10,9},{11,1... | collective-permute-start | bytes 393224 | tf_op jit(solution)/shard_map/ppermute | solution.py:31
  9.1 2.5 %collective-permute-done.6 = bf16[64,1024]{1,0:T(8,128)(2,1)S(1)} collective-permute-done((bf16[64,1024]{1,0:T(8,128)(2,1)S(1)}, bf16[64,1024]{1,0:T(8,128)(2,1)S(1)}, u32[]{:S(2)}, u32[]{:S(2)}) %collective-permute-start.6) | collective-permute-done | bytes 131104 | tf_op jit(solution)/shard_map/ppermute | solution.py:31
  11.6 4.8 %collective-permute-done.7 = bf16[64,1024]{1,0:T(8,128)(2,1)S(1)} collective-permute-done((bf16[64,1024]{1,0:T(8,128)(2,1)S(1)}, bf16[64,1024]{1,0:T(8,128)(2,1)S(1)}, u32[]{:S(2)}, u32[]{:S(2)}) %collective-permute-start.7) | collective-permute-done | bytes 131104 | tf_op jit(solution)/shard_map/ppermute | solution.py:31
  16.4 1.6 %collective-permute-start.9 = (bf16[192,1024]{1,0:T(8,128)(2,1)S(1)}, bf16[192,1024]{1,0:T(8,128)(2,1)S(1)}, u32[]{:S(2)}, u32[]{:S(2)}) collective-permute-start(bf16[192,1024]{1,0:T(8,128)(2,1)S(1)} %constant_dynamic-update-slice_fusion.arrived), channel_id=1, source_target_pairs={{0,8},{4,12},{8,0},{12,4},{1,9},{5,13},{9,1},{13,5},{2,10},{6,14},... | collective-permute-start | bytes 1179656 | tf_op jit(solution)/shard_map/ppermute | solution.py:35
  18.7 3.3 %collective-permute-start = (s32[64,8]{1,0:T(8,128)S(1)}, s32[64,8]{1,0:T(8,128)S(1)}, u32[]{:S(2)}, u32[]{:S(2)}) collective-permute-start(s32[64,8]{1,0:T(8,128)S(1)} %bitcast.9), channel_id=1, source_target_pairs={{3,0},{0,1},{1,2},{2,3},{7,4},{4,5},{5,6},{6,7},{11,8},{8,9},{9,10... | collective-permute-start | bytes 6152 | tf_op jit(solution)/shard_map/ppermute | solution.py:31
  22.0 1.7 %collective-permute-start.1 = (s32[64,8]{1,0:T(8,128)S(1)}, s32[64,8]{1,0:T(8,128)S(1)}, u32[]{:S(2)}, u32[]{:S(2)}) collective-permute-start(s32[64,8]{1,0:T(8,128)S(1)} %bitcast.10), channel_id=1, source_target_pairs={{2,0},{3,1},{0,2},{1,3},{6,4},{7,5},{4,6},{5,7},{10,8},{11,9},{8,1... | collective-permute-start | bytes 6152 | tf_op jit(solution)/shard_map/ppermute | solution.py:31
  25.2 1.3 %collective-permute-start.3 = (f32[64,8]{1,0:T(8,128)S(1)}, f32[64,8]{1,0:T(8,128)S(1)}, u32[]{:S(2)}, u32[]{:S(2)}) collective-permute-start(f32[64,8]{1,0:T(8,128)S(1)} %bitcast.13), channel_id=1, source_target_pairs={{3,0},{0,1},{1,2},{2,3},{7,4},{4,5},{5,6},{6,7},{11,8},{8,9},{9,10... | collective-permute-start | bytes 6152 | tf_op jit(solution)/shard_map/ppermute | solution.py:31
  27.2 1.6 %collective-permute-start.4 = (f32[64,8]{1,0:T(8,128)S(1)}, f32[64,8]{1,0:T(8,128)S(1)}, u32[]{:S(2)}, u32[]{:S(2)}) collective-permute-start(f32[64,8]{1,0:T(8,128)S(1)} %bitcast.14), channel_id=1, source_target_pairs={{2,0},{3,1},{0,2},{1,3},{6,4},{7,5},{4,6},{5,7},{10,8},{11,9},{8,1... | collective-permute-start | bytes 6152 | tf_op jit(solution)/shard_map/ppermute | solution.py:31
  28.8 1.4 %collective-permute-start.5 = (f32[64,8]{1,0:T(8,128)S(1)}, f32[64,8]{1,0:T(8,128)S(1)}, u32[]{:S(2)}, u32[]{:S(2)}) collective-permute-start(f32[64,8]{1,0:T(8,128)S(1)} %bitcast.15), channel_id=1, source_target_pairs={{1,0},{2,1},{3,2},{0,3},{5,4},{6,5},{7,6},{4,7},{9,8},{10,9},{11,1... | collective-permute-start | bytes 6152 | tf_op jit(solution)/shard_map/ppermute | solution.py:31
  30.3 8.2 %shard_map.66 = (bf16[8,2,384,1024]{3,2,1,0:T(8,128)(2,1)S(1)}, bf16[8,2,384,1024]{3,2,1,0:T(8,128)(2,1)S(1)}) custom-call(s32[1]{0:T(128)} %bitcast.place.refs_8_, bf16[8,2,384,4096]{3,2,1,0:T(8,128)(2,1)} %refs_1_.3), custom_call_target="tpu_custom_call" | custom-call | bytes 50331648 | tf_op jit(solution)/shard_map/pallas_call | solution.py:133
  38.5 4.5 %copy-done = bf16[8,2,384,1024]{3,2,1,0:T(8,128)(2,1)} copy-done((bf16[8,2,384,1024]{3,2,1,0:T(8,128)(2,1)}, bf16[8,2,384,1024]{3,2,1,0:T(8,128)(2,1)S(1)}, u32[]{:S(2)}) %copy-start) | copy-done | bytes 12582936
  43.0 4.5 %copy-done.1 = bf16[8,2,384,1024]{3,2,1,0:T(8,128)(2,1)} copy-done((bf16[8,2,384,1024]{3,2,1,0:T(8,128)(2,1)}, bf16[8,2,384,1024]{3,2,1,0:T(8,128)(2,1)S(1)}, u32[]{:S(2)}) %copy-start.1) | copy-done | bytes 12582936
  47.5 1.1 shard_map.64
  48.6 4.7 %copy-done.2 = bf16[8,2,384,1024]{3,2,1,0:T(8,128)(2,1)S(1)} copy-done((bf16[8,2,384,1024]{3,2,1,0:T(8,128)(2,1)S(1)}, bf16[8,2,384,1024]{3,2,1,0:T(8,128)(2,1)}, u32[]{:S(2)}) %copy-start.2) | copy-done | bytes 12582936
  53.4 5.3 %shard_map.67 = (f32[8,2,64,384]{3,2,1,0:T(8,128)S(1)}, bf16[8,2,384,1024]{3,2,1,0:T(8,128)(2,1)S(1)}) custom-call(s32[1]{0:T(128)} %bitcast.place.refs_8_, bf16[4,128,64]{2,1,0:T(8,128)(2,1)S(1)} %get-tuple-element.26.placing, bf16[64,4096]{1,0:T(8,128)(2,1)S(1)} %get-tuple-element.27.normed, ...), custom_call_target="tpu_custom_call" | custom-call | flops 3221225472 | bytes 12582912 | tf_op jit(solution)/shard_map/pallas_call | solution.py:238
  59.5 1.2 %slice-done.2 = s8[4194304]{0:T(1024)(128)(4,1)S(1)} async-done(((s8[12582912]{0:T(1024)(128)(4,1)}), s8[4194304]{0:T(1024)(128)(4,1)S(1)}, s32[]{:S(2)}) %slice-start.2) | async-done | bytes 4194328
  60.7 5.3 %shard_map.68 = (f32[8,2,64,384]{3,2,1,0:T(8,128)S(1)}, bf16[8,2,384,1024]{3,2,1,0:T(8,128)(2,1)S(1)}) custom-call(s32[1]{0:T(128)} %bitcast.place.refs_8_, bf16[4,128,64]{2,1,0:T(8,128)(2,1)S(1)} %get-tuple-element.26.placing, bf16[64,4096]{1,0:T(8,128)(2,1)S(1)} %get-tuple-element.27.normed, bf16[192,1024]{1,0:T(8,128)(2,1)S(1)} %collective-permute-done.11.arrived, ...), custom_call_target="tpu_custom_call" | custom-call | flops 3221225472 | bytes 12582912 | tf_op jit(solution)/shard_map/pallas_call | solution.py:238
  66.0 5.3 %shard_map.69 = (f32[8,2,64,384]{3,2,1,0:T(8,128)S(1)}, bf16[8,384,1024]{2,1,0:T(8,128)(2,1)S(1)}, bf16[8,384,1024]{2,1,0:T(8,128)(2,1)S(1)}) custom-call(s32[1]{0:T(128)} %bitcast.place.refs_8_, bf16[4,128,64]{2,1,0:T(8,128)(2,1)S(1)} %get-tuple-element.26.placing, bf16[64,4096]{1,0:T(8,128)(2,1)S(1)} %get-tuple-element.27.normed, ...), custom_call_target="tpu_custom_call" | custom-call | flops 3221225472 | bytes 12582912 | tf_op jit(solution)/shard_map/pallas_call | solution.py:238
  71.3 2.6 %copy-done.3 = bf16[8,384,1024]{2,1,0:T(8,128)(2,1)} copy-done((bf16[8,384,1024]{2,1,0:T(8,128)(2,1)}, bf16[8,384,1024]{2,1,0:T(8,128)(2,1)S(1)}, u32[]{:S(2)}) %copy-start.3) | copy-done | bytes 6291480
  74.0 5.3 %shard_map.70 = (bf16[8,64,384]{2,1,0:T(8,128)(2,1)S(1)}, bf16[8,384,1024]{2,1,0:T(8,128)(2,1)S(1)}, bf16[8,384,1024]{2,1,0:T(8,128)(2,1)S(1)}) custom-call(s32[1]{0:T(128)} %bitcast.place.refs_8_, bf16[4,128,64]{2,1,0:T(8,128)(2,1)S(1)} %get-tuple-element.26.placing, bf16[64,4096]{1,0:T(8,128)(2,1)S(1)} %get-tuple-element.27.normed, ...), custom_call_target="tpu_custom_call" | custom-call | flops 3221225472 | bytes 12582912 | tf_op jit(solution)/shard_map/pallas_call | solution.py:238
  79.9 9.6 %collective-permute-done.12.refs_0_ = bf16[8,64,384]{2,1,0:T(8,128)(2,1)S(1)} collective-permute-done((bf16[8,64,384]{2,1,0:T(8,128)(2,1)S(1)}, bf16[8,64,384]{2,1,0:T(8,128)(2,1)S(1)}, u32[]{:S(2)}, u32[]{:S(2)}) %collective-permute-start.12) | collective-permute-done | bytes 393248 | tf_op jit(solution)/shard_map/ppermute | solution.py:35
  89.6 3.2 %shard_map.71.refs_4_ = f32[8,64,1024]{2,1,0:T(8,128)S(1)} custom-call(bf16[8,64,384]{2,1,0:T(8,128)(2,1)S(1)} %get-tuple-element.36.refs_0_, bf16[8,64,384]{2,1,0:T(8,128)(2,1)S(1)} %collective-permute-done.14.refs_1_, bf16[8,384,1024]{2,1,0:T(8,128)(2,1)S(1)} %get-tuple-element.39.refs_2_, bf16[8,384,1024]{2,1,0:T(8,128)(2,1)S(1)} %copy-done.4), custom_call_target="tpu_custom_call" | custom-call | flops 3221225472 | bytes 12582912 | tf_op jit(solution)/shard_map/pallas_call | solution.py:313
  92.8 3.7 %shard_map.72 = (bf16[64,1024]{1,0:T(8,128)(2,1)S(1)}, bf16[64,1024]{1,0:T(8,128)(2,1)S(1)}, bf16[64,1024]{1,0:T(8,128)(2,1)S(1)}, bf16[64,1024]{1,0:T(8,128)(2,1)S(1)}) custom-call(bf16[8,64,384]{2,1,0:T(8,128)(2,1)S(1)} %collective-permute-done.12.refs_0_, bf16[8,64,384]{2,1,0:T(8,128)(2,1)S(1)} %collective-permute-done.13.refs_1_, ...), custom_call_target="tpu_custom_call" | custom-call | flops 3221225472 | bytes 12582912 | tf_op jit(solution)/shard_map/pallas_call | solution.py:313
  96.5 1.6 %collective-permute-start.15 = (bf16[64,1024]{1,0:T(8,128)(2,1)S(1)}, bf16[64,1024]{1,0:T(8,128)(2,1)S(1)}, u32[]{:S(2)}, u32[]{:S(2)}) collective-permute-start(bf16[64,1024]{1,0:T(8,128)(2,1)S(1)} %get-tuple-element.43), channel_id=1, source_target_pairs={{0,16},{1,17},{2,18},{3,19},{16,0},{17,1},{18,2},{19,3},{4,20},{5,... | collective-permute-start | bytes 393224 | tf_op jit(solution)/shard_map/ppermute | solution.py:392
  98.1 1.2 %collective-permute-start.16 = (bf16[64,1024]{1,0:T(8,128)(2,1)S(1)}, bf16[64,1024]{1,0:T(8,128)(2,1)S(1)}, u32[]{:S(2)}, u32[]{:S(2)}) collective-permute-start(bf16[64,1024]{1,0:T(8,128)(2,1)S(1)} %get-tuple-element.44), channel_id=1, source_target_pairs={{0,19},{1,16},{2,17},{3,18},{16,3},{17,0},{18,1},{19,2},{4,23},{5,... | collective-permute-start | bytes 393224 | tf_op jit(solution)/shard_map/ppermute | solution.py:392
  99.3 1.2 %collective-permute-start.17 = (bf16[64,1024]{1,0:T(8,128)(2,1)S(1)}, bf16[64,1024]{1,0:T(8,128)(2,1)S(1)}, u32[]{:S(2)}, u32[]{:S(2)}) collective-permute-start(bf16[64,1024]{1,0:T(8,128)(2,1)S(1)} %get-tuple-element.45), channel_id=1, source_target_pairs={{0,18},{1,19},{2,16},{3,17},{16,2},{17,3},{18,0},{19,1},{4,22},{5,... | collective-permute-start | bytes 393224 | tf_op jit(solution)/shard_map/ppermute | solution.py:392
  100.5 1.3 %collective-permute-start.18 = (bf16[64,1024]{1,0:T(8,128)(2,1)S(1)}, bf16[64,1024]{1,0:T(8,128)(2,1)S(1)}, u32[]{:S(2)}, u32[]{:S(2)}) collective-permute-start(bf16[64,1024]{1,0:T(8,128)(2,1)S(1)} %get-tuple-element.46), channel_id=1, source_target_pairs={{0,17},{1,18},{2,19},{3,16},{16,1},{17,2},{18,3},{19,0},{4,21},{5,... | collective-permute-start | bytes 393224 | tf_op jit(solution)/shard_map/ppermute | solution.py:392
  101.8 4.4 %collective-permute-done.15.refs_0_ = bf16[64,1024]{1,0:T(8,128)(2,1)S(1)} collective-permute-done((bf16[64,1024]{1,0:T(8,128)(2,1)S(1)}, bf16[64,1024]{1,0:T(8,128)(2,1)S(1)}, u32[]{:S(2)}, u32[]{:S(2)}) %collective-permute-start.15) | collective-permute-done | bytes 131104 | tf_op jit(solution)/shard_map/ppermute | solution.py:392
  106.2 6.3 %collective-permute-done.17.refs_2_ = bf16[64,1024]{1,0:T(8,128)(2,1)S(1)} collective-permute-done((bf16[64,1024]{1,0:T(8,128)(2,1)S(1)}, bf16[64,1024]{1,0:T(8,128)(2,1)S(1)}, u32[]{:S(2)}, u32[]{:S(2)}) %collective-permute-start.17) | collective-permute-done | bytes 131104 | tf_op jit(solution)/shard_map/ppermute | solution.py:392
  (43 shorter events, 6.2 us)
Async XLA Ops:
  0.7 1.0 copy-start.5
  2.1 9.5 %collective-permute-start.6 = (bf16[64,1024]{1,0:T(8,128)(2,1)S(1)}, bf16[64,1024]{1,0:T(8,128)(2,1)S(1)}, u32[]{:S(2)}, u32[]{:S(2)}) collective-permute-start(bf16[64,1024]{1,0:T(8,128)(2,1)S(1)} %get-tuple-element.28), channel_id=1, source_target_pairs={{3,0},{0,1},{1,2},{2,3},{7,4},{4,5},{5,6},{6,7},{11,8},{8,9},{9,10... | collective-permute-start | bytes 393224 | tf_op jit(solution)/shard_map/ppermute | solution.py:31
  5.1 11.2 %collective-permute-start.7 = (bf16[64,1024]{1,0:T(8,128)(2,1)S(1)}, bf16[64,1024]{1,0:T(8,128)(2,1)S(1)}, u32[]{:S(2)}, u32[]{:S(2)}) collective-permute-start(bf16[64,1024]{1,0:T(8,128)(2,1)S(1)} %get-tuple-element.28), channel_id=1, source_target_pairs={{2,0},{3,1},{0,2},{1,3},{6,4},{7,5},{4,6},{5,7},{10,8},{11,9},{8,1... | collective-permute-start | bytes 393224 | tf_op jit(solution)/shard_map/ppermute | solution.py:31
  7.7 8.7 %collective-permute-start.8 = (bf16[64,1024]{1,0:T(8,128)(2,1)S(1)}, bf16[64,1024]{1,0:T(8,128)(2,1)S(1)}, u32[]{:S(2)}, u32[]{:S(2)}) collective-permute-start(bf16[64,1024]{1,0:T(8,128)(2,1)S(1)} %get-tuple-element.28), channel_id=1, source_target_pairs={{1,0},{2,1},{3,2},{0,3},{5,4},{6,5},{7,6},{4,7},{9,8},{10,9},{11,1... | collective-permute-start | bytes 393224 | tf_op jit(solution)/shard_map/ppermute | solution.py:31
  16.4 42.2 %collective-permute-start.9 = (bf16[192,1024]{1,0:T(8,128)(2,1)S(1)}, bf16[192,1024]{1,0:T(8,128)(2,1)S(1)}, u32[]{:S(2)}, u32[]{:S(2)}) collective-permute-start(bf16[192,1024]{1,0:T(8,128)(2,1)S(1)} %constant_dynamic-update-slice_fusion.arrived), channel_id=1, source_target_pairs={{0,8},{4,12},{8,0},{12,4},{1,9},{5,13},{9,1},{13,5},{2,10},{6,14},... | collective-permute-start | bytes 1179656 | tf_op jit(solution)/shard_map/ppermute | solution.py:35
  18.0 40.8 %collective-permute-start.11 = (bf16[192,1024]{1,0:T(8,128)(2,1)S(1)}, bf16[192,1024]{1,0:T(8,128)(2,1)S(1)}, u32[]{:S(2)}, u32[]{:S(2)}) collective-permute-start(bf16[192,1024]{1,0:T(8,128)(2,1)S(1)} %constant_dynamic-update-slice_fusion.arrived), channel_id=1, source_target_pairs={{0,4},{4,0},{8,12},{12,8},{1,5},{5,1},{9,13},{13,9},{2,6},{6,2},{1... | collective-permute-start | bytes 1179656 | tf_op jit(solution)/shard_map/ppermute | solution.py:35
  18.7 6.5 %collective-permute-start = (s32[64,8]{1,0:T(8,128)S(1)}, s32[64,8]{1,0:T(8,128)S(1)}, u32[]{:S(2)}, u32[]{:S(2)}) collective-permute-start(s32[64,8]{1,0:T(8,128)S(1)} %bitcast.9), channel_id=1, source_target_pairs={{3,0},{0,1},{1,2},{2,3},{7,4},{4,5},{5,6},{6,7},{11,8},{8,9},{9,10... | collective-permute-start | bytes 6152 | tf_op jit(solution)/shard_map/ppermute | solution.py:31
  22.0 5.2 %collective-permute-start.1 = (s32[64,8]{1,0:T(8,128)S(1)}, s32[64,8]{1,0:T(8,128)S(1)}, u32[]{:S(2)}, u32[]{:S(2)}) collective-permute-start(s32[64,8]{1,0:T(8,128)S(1)} %bitcast.10), channel_id=1, source_target_pairs={{2,0},{3,1},{0,2},{1,3},{6,4},{7,5},{4,6},{5,7},{10,8},{11,9},{8,1... | collective-permute-start | bytes 6152 | tf_op jit(solution)/shard_map/ppermute | solution.py:31
  23.7 5.1 %collective-permute-start.2 = (s32[64,8]{1,0:T(8,128)S(1)}, s32[64,8]{1,0:T(8,128)S(1)}, u32[]{:S(2)}, u32[]{:S(2)}) collective-permute-start(s32[64,8]{1,0:T(8,128)S(1)} %bitcast.11), channel_id=1, source_target_pairs={{1,0},{2,1},{3,2},{0,3},{5,4},{6,5},{7,6},{4,7},{9,8},{10,9},{11,1... | collective-permute-start | bytes 6152 | tf_op jit(solution)/shard_map/ppermute | solution.py:31
  25.2 22.3 %collective-permute-start.3 = (f32[64,8]{1,0:T(8,128)S(1)}, f32[64,8]{1,0:T(8,128)S(1)}, u32[]{:S(2)}, u32[]{:S(2)}) collective-permute-start(f32[64,8]{1,0:T(8,128)S(1)} %bitcast.13), channel_id=1, source_target_pairs={{3,0},{0,1},{1,2},{2,3},{7,4},{4,5},{5,6},{6,7},{11,8},{8,9},{9,10... | collective-permute-start | bytes 6152 | tf_op jit(solution)/shard_map/ppermute | solution.py:31
  27.2 20.3 %collective-permute-start.4 = (f32[64,8]{1,0:T(8,128)S(1)}, f32[64,8]{1,0:T(8,128)S(1)}, u32[]{:S(2)}, u32[]{:S(2)}) collective-permute-start(f32[64,8]{1,0:T(8,128)S(1)} %bitcast.14), channel_id=1, source_target_pairs={{2,0},{3,1},{0,2},{1,3},{6,4},{7,5},{4,6},{5,7},{10,8},{11,9},{8,1... | collective-permute-start | bytes 6152 | tf_op jit(solution)/shard_map/ppermute | solution.py:31
  28.8 18.7 %collective-permute-start.5 = (f32[64,8]{1,0:T(8,128)S(1)}, f32[64,8]{1,0:T(8,128)S(1)}, u32[]{:S(2)}, u32[]{:S(2)}) collective-permute-start(f32[64,8]{1,0:T(8,128)S(1)} %bitcast.15), channel_id=1, source_target_pairs={{1,0},{2,1},{3,2},{0,3},{5,4},{6,5},{7,6},{4,7},{9,8},{10,9},{11,1... | collective-permute-start | bytes 6152 | tf_op jit(solution)/shard_map/ppermute | solution.py:31
  38.4 4.5 %copy-start = (bf16[8,2,384,1024]{3,2,1,0:T(8,128)(2,1)}, bf16[8,2,384,1024]{3,2,1,0:T(8,128)(2,1)S(1)}, u32[]{:S(2)}) copy-start(bf16[8,2,384,1024]{3,2,1,0:T(8,128)(2,1)S(1)} %get-tuple-element.29.weights) | copy-start | bytes 37748740
  43.0 4.5 %copy-start.1 = (bf16[8,2,384,1024]{3,2,1,0:T(8,128)(2,1)}, bf16[8,2,384,1024]{3,2,1,0:T(8,128)(2,1)S(1)}, u32[]{:S(2)}) copy-start(bf16[8,2,384,1024]{3,2,1,0:T(8,128)(2,1)S(1)} %get-tuple-element.30.weights) | copy-start | bytes 37748740
  48.6 10.1 %slice-start = ((s8[12582912]{0:T(1024)(128)(4,1)}), s8[4194304]{0:T(1024)(128)(4,1)S(1)}, s32[]{:S(2)}) async-start(s8[12582912]{0:T(1024)(128)(4,1)} %bitcast.5), calls=%async_computation | async-start | bytes 8388608
  48.6 4.7 %copy-start.2 = (bf16[8,2,384,1024]{3,2,1,0:T(8,128)(2,1)S(1)}, bf16[8,2,384,1024]{3,2,1,0:T(8,128)(2,1)}, u32[]{:S(2)}) copy-start(bf16[8,2,384,1024]{3,2,1,0:T(8,128)(2,1)} %copy-done.1) | copy-start | bytes 37748740
  53.4 6.1 %slice-start.1 = ((s8[12582912]{0:T(1024)(128)(4,1)}), s8[4194304]{0:T(1024)(128)(4,1)S(1)}, s32[]{:S(2)}) async-start(s8[12582912]{0:T(1024)(128)(4,1)} %bitcast.5), calls=%async_computation.1 | async-start | bytes 8388608
  53.4 7.3 %slice-start.2 = ((s8[12582912]{0:T(1024)(128)(4,1)}), s8[4194304]{0:T(1024)(128)(4,1)S(1)}, s32[]{:S(2)}) async-start(s8[12582912]{0:T(1024)(128)(4,1)} %bitcast.5), calls=%async_computation.2 | async-start | bytes 8388608
  58.7 15.3 %collective-permute-start.10 = (bf16[192,1024]{1,0:T(8,128)(2,1)S(1)}, bf16[192,1024]{1,0:T(8,128)(2,1)S(1)}, u32[]{:S(2)}, u32[]{:S(2)}) collective-permute-start(bf16[192,1024]{1,0:T(8,128)(2,1)S(1)} %collective-permute-done.9.arrived), channel_id=1, source_target_pairs={{0,4},{4,0},{8,12},{12,8},{1,5},{5,1},{9,13},{13,9},{2,6},{6,2},{1... | collective-permute-start | bytes 1179656 | tf_op jit(solution)/shard_map/ppermute | solution.py:35
  71.3 2.6 %copy-start.3 = (bf16[8,384,1024]{2,1,0:T(8,128)(2,1)}, bf16[8,384,1024]{2,1,0:T(8,128)(2,1)S(1)}, u32[]{:S(2)}) copy-start(bf16[8,384,1024]{2,1,0:T(8,128)(2,1)S(1)} %get-tuple-element.40.refs_3_) | copy-start | bytes 18874372
  74.0 15.6 %copy-start.4 = (bf16[8,384,1024]{2,1,0:T(8,128)(2,1)S(1)}, bf16[8,384,1024]{2,1,0:T(8,128)(2,1)}, u32[]{:S(2)}) copy-start(bf16[8,384,1024]{2,1,0:T(8,128)(2,1)} %copy-done.3) | copy-start | bytes 18874372
  79.3 10.3 %collective-permute-start.12 = (bf16[8,64,384]{2,1,0:T(8,128)(2,1)S(1)}, bf16[8,64,384]{2,1,0:T(8,128)(2,1)S(1)}, u32[]{:S(2)}, u32[]{:S(2)}) collective-permute-start(bf16[8,64,384]{2,1,0:T(8,128)(2,1)S(1)} %get-tuple-element.36.refs_0_), channel_id=1, source_target_pairs={{0,8},{4,12},{8,0},{12,4},{1,9},{5,13},{9,1},{13,5},{2,10},{6,14},... | collective-permute-start | bytes 1179656 | tf_op jit(solution)/shard_map/ppermute | solution.py:35
  79.9 9.6 %collective-permute-start.14 = (bf16[8,64,384]{2,1,0:T(8,128)(2,1)S(1)}, bf16[8,64,384]{2,1,0:T(8,128)(2,1)S(1)}, u32[]{:S(2)}, u32[]{:S(2)}) collective-permute-start(bf16[8,64,384]{2,1,0:T(8,128)(2,1)S(1)} %get-tuple-element.36.refs_0_), channel_id=1, source_target_pairs={{0,4},{4,0},{8,12},{12,8},{1,5},{5,1},{9,13},{13,9},{2,6},{6,2},{1... | collective-permute-start | bytes 1179656 | tf_op jit(solution)/shard_map/ppermute | solution.py:35
  89.5 3.2 %collective-permute-start.13 = (bf16[8,64,384]{2,1,0:T(8,128)(2,1)S(1)}, bf16[8,64,384]{2,1,0:T(8,128)(2,1)S(1)}, u32[]{:S(2)}, u32[]{:S(2)}) collective-permute-start(bf16[8,64,384]{2,1,0:T(8,128)(2,1)S(1)} %collective-permute-done.12.refs_0_), channel_id=1, source_target_pairs={{0,4},{4,0},{8,12},{12,8},{1,5},{5,1},{9,13},{13,9},{2,6},{6,2},{1... | collective-permute-start | bytes 1179656 | tf_op jit(solution)/shard_map/ppermute | solution.py:35
  89.5 3.2 %copy-start.6 = (bf16[1,64,4096]{2,1,0:T(8,128)(2,1)S(1)}, bf16[1,64,4096]{2,1,0:T(8,128)(2,1)}, u32[]{:S(2)}) copy-start(bf16[1,64,4096]{2,1,0:T(8,128)(2,1)} %param.6) | copy-start | bytes 1572868
  96.5 9.7 %collective-permute-start.15 = (bf16[64,1024]{1,0:T(8,128)(2,1)S(1)}, bf16[64,1024]{1,0:T(8,128)(2,1)S(1)}, u32[]{:S(2)}, u32[]{:S(2)}) collective-permute-start(bf16[64,1024]{1,0:T(8,128)(2,1)S(1)} %get-tuple-element.43), channel_id=1, source_target_pairs={{0,16},{1,17},{2,18},{3,19},{16,0},{17,1},{18,2},{19,3},{4,20},{5,... | collective-permute-start | bytes 393224 | tf_op jit(solution)/shard_map/ppermute | solution.py:392
  98.1 8.1 %collective-permute-start.16 = (bf16[64,1024]{1,0:T(8,128)(2,1)S(1)}, bf16[64,1024]{1,0:T(8,128)(2,1)S(1)}, u32[]{:S(2)}, u32[]{:S(2)}) collective-permute-start(bf16[64,1024]{1,0:T(8,128)(2,1)S(1)} %get-tuple-element.44), channel_id=1, source_target_pairs={{0,19},{1,16},{2,17},{3,18},{16,3},{17,0},{18,1},{19,2},{4,23},{5,... | collective-permute-start | bytes 393224 | tf_op jit(solution)/shard_map/ppermute | solution.py:392
  99.3 13.3 %collective-permute-start.17 = (bf16[64,1024]{1,0:T(8,128)(2,1)S(1)}, bf16[64,1024]{1,0:T(8,128)(2,1)S(1)}, u32[]{:S(2)}, u32[]{:S(2)}) collective-permute-start(bf16[64,1024]{1,0:T(8,128)(2,1)S(1)} %get-tuple-element.45), channel_id=1, source_target_pairs={{0,18},{1,19},{2,16},{3,17},{16,2},{17,3},{18,0},{19,1},{4,22},{5,... | collective-permute-start | bytes 393224 | tf_op jit(solution)/shard_map/ppermute | solution.py:392
  100.5 12.1 %collective-permute-start.18 = (bf16[64,1024]{1,0:T(8,128)(2,1)S(1)}, bf16[64,1024]{1,0:T(8,128)(2,1)S(1)}, u32[]{:S(2)}, u32[]{:S(2)}) collective-permute-start(bf16[64,1024]{1,0:T(8,128)(2,1)S(1)} %get-tuple-element.46), channel_id=1, source_target_pairs={{0,17},{1,18},{2,19},{3,16},{16,1},{17,2},{18,3},{19,0},{4,21},{5,... | collective-permute-start | bytes 393224 | tf_op jit(solution)/shard_map/ppermute | solution.py:392

commit v2 on v0

--- a/solution.py
+++ b/solution.py
@@ -1,16 +1,566 @@
+import functools
+
 import jax
 import jax.numpy as jnp
 from jax import lax
+from jax.experimental import pallas as pl
+from jax.experimental.pallas import tpu as pltpu
 from jax.sharding import PartitionSpec as P
 
-
-def passed_along(block, axis, distance):
-    devices = range(lax.axis_size(axis))
-    route = [((i - distance) % len(devices), i) for i in devices]
-    return lax.ppermute(block, axis, route)
-
-
-def body(activations, routes, gate_weights, norm_gain, gate_up_weights, down_weights):
+CONTRACT_LAST = (((1,), (1,)), ((), ()))
+IN_VMEM = pl.BlockSpec(memory_space=pltpu.VMEM)
+IN_SMEM = pl.BlockSpec(memory_space=pltpu.SMEM)
+IN_HBM = pl.BlockSpec(memory_space=pltpu.HBM)
+MIB = 1 << 20
+LANES = 128
+
+
+def params(mib):
+    return pltpu.CompilerParams(vmem_limit_bytes=mib * MIB)
+
+
+def cost(flops, moved):
+    return pl.CostEstimate(flops=int(flops), bytes_accessed=int(moved), transcendentals=0)
+
+
+def pinned(array):
+    return pltpu.with_memory_space_constraint(array, pltpu.VMEM)
+
+
+def in_hbm(array):
+    return pltpu.with_memory_space_constraint(array, pltpu.HBM)
+
+
+def shifted(block, axis, distance):
+    count = lax.axis_size(axis)
+    return lax.ppermute(block, axis, [((i - distance) % count, i) for i in range(count)])
+
+
+def flipped(block, axis, bit):
+    return lax.ppermute(block, axis, [(i, i ^ bit) for i in range(lax.axis_size(axis))])
+
+
+def norm_kernel(ids, *refs):
+    sources, (normed, sent), landed, semaphores = refs[:4], refs[4:6], refs[6:10], refs[10]
+    copies = [
+        pltpu.make_async_copy(source, target, semaphores.at[i])
+        for i, (source, target) in enumerate(zip(sources, landed))
+    ]
+    for copy in copies:
+        copy.start()
+    for copy in copies:
+        copy.wait()
+    tokens, gain, routes, weights = landed
+    widened = tokens[...].astype(jnp.float32)
+    mean_square = jnp.mean(widened * widened, axis=-1, keepdims=True)
+    rows = widened * lax.rsqrt(mean_square + 1e-06)
+    rows = rows * gain[...].astype(jnp.float32).reshape(1, rows.shape[1])
+    normed[...] = rows.astype(jnp.bfloat16)
+    count, features = normed.shape
+    pieces = sent.shape[0] // count
+    start = pl.multiple_of(ids[0] * pieces * LANES, pieces * LANES)
+    for i in range(pieces):
+        at = pl.ds(pl.multiple_of(start + i * LANES, LANES), LANES)
+        sent[i * count : (i + 1) * count] = normed[:, at]
+    whole = weights[...]
+    coarse = whole.astype(jnp.bfloat16).astype(jnp.float32)
+    middle = (whole - coarse).astype(jnp.bfloat16).astype(jnp.float32)
+    fine = whole - coarse - middle
+    upper = jnp.concatenate([routes[...].astype(jnp.float32), coarse])
+    lower = jnp.concatenate([middle, fine])
+    sent[pieces * count :] = jnp.concatenate([upper, lower], axis=1).astype(jnp.bfloat16)
+
+
+def normalize(ids, tokens, gain, routes, weights, width):
+    count, features = tokens.shape
+    top = routes.shape[0]
+    operands = (tokens, gain, routes, weights)
+    return pl.pallas_call(
+        norm_kernel,
+        out_shape=(
+            jax.ShapeDtypeStruct((count, features), jnp.bfloat16),
+            jax.ShapeDtypeStruct((count * width // LANES + 2 * top, LANES), jnp.bfloat16),
+        ),
+        in_specs=[IN_SMEM] + [IN_HBM] * 4,
+        out_specs=(IN_VMEM, IN_VMEM),
+        scratch_shapes=[pltpu.VMEM(x.shape, x.dtype) for x in operands]
+        + [pltpu.SemaphoreType.DMA((4,))],
+        compiler_params=params(8),
+    )(ids, *(in_hbm(x) for x in operands))
+
+
+def relay_kernel(block, after, result):
+    result[...] = block[...]
+
+
+def relayed(block, after):
+    return pl.pallas_call(
+        relay_kernel,
+        out_shape=jax.ShapeDtypeStruct(block.shape, block.dtype),
+        in_specs=[IN_VMEM, IN_VMEM],
+        out_specs=IN_VMEM,
+        compiler_params=params(8),
+    )(block, after)
+
+
+def collect_kernel(*refs):
+    *blocks, staged, result = refs
+    count = result.shape[0] // len(blocks)
+    for i, block in enumerate(blocks):
+        for j in range(result.shape[1] // LANES):
+            result[i * count : (i + 1) * count, j * LANES : (j + 1) * LANES] = block[
+                j * count : (j + 1) * count
+            ]
+
+
+def collect(blocks, count, width, staged):
+    return pl.pallas_call(
+        collect_kernel,
+        out_shape=jax.ShapeDtypeStruct((len(blocks) * count, width), jnp.bfloat16),
+        in_specs=[IN_VMEM] * (len(blocks) + 1),
+        out_specs=IN_VMEM,
+        compiler_params=params(8),
+    )(*blocks, pinned(staged))
+
+
+def plan_kernel(capacity, top, ids, *refs):
+    blocks = refs[:-3]
+    placing, high, low = refs[-3:]
+    tokens, slots = high.shape[1:]
+    lane = lax.broadcasted_iota(jnp.int32, (tokens, slots), 1)
+    expert = (ids[1] + lane // capacity).astype(jnp.float32)
+    rank_of_lane = lane % capacity
+    row = lax.broadcasted_iota(jnp.int32, (tokens, tokens), 0)
+    column = lax.broadcasted_iota(jnp.int32, (tokens, tokens), 1)
+    earlier = jnp.where(column < row, 1.0, 0.0).astype(jnp.bfloat16)
+    for i, block in enumerate(blocks):
+        named = jnp.zeros((tokens, slots), jnp.float32)
+        weight = jnp.zeros((tokens, slots), jnp.float32)
+        sent = block[block.shape[0] - 2 * top :].astype(jnp.float32)
+        sent = jnp.concatenate(
+            [
+                sent[:, :tokens],
+                sent[:, LANES // 2 : LANES // 2 + tokens],
+                jnp.zeros((LANES - 4 * top, tokens), jnp.float32),
+            ]
+        ).T
+        for k in range(top):
+            hit = sent[:, k : k + 1] == expert
+            value = sum(sent[:, part * top + k : part * top + k + 1] for part in (1, 2, 3))
+            named = jnp.where(hit, 1.0, named)
+            weight = jnp.where(hit, value, weight)
+        ranks = jnp.dot(earlier, named.astype(jnp.bfloat16), preferred_element_type=jnp.float32)
+        here = jnp.where((named > 0.5) & (ranks.astype(jnp.int32) == rank_of_lane), 1.0, 0.0)
+        placing[i] = here.T.astype(jnp.bfloat16)
+        scaled = here * weight
+        coarse = scaled.astype(jnp.bfloat16)
+        high[i] = coarse
+        low[i] = (scaled - coarse.astype(jnp.float32)).astype(jnp.bfloat16)
+
+
+def plan(ids, blocks, tokens, slots, capacity, top):
+    count = len(blocks)
+    return pl.pallas_call(
+        functools.partial(plan_kernel, capacity, top),
+        out_shape=(
+            jax.ShapeDtypeStruct((count, slots, tokens), jnp.bfloat16),
+            jax.ShapeDtypeStruct((count, tokens, slots), jnp.bfloat16),
+            jax.ShapeDtypeStruct((count, tokens, slots), jnp.bfloat16),
+        ),
+        in_specs=[IN_SMEM] + [IN_VMEM] * count,
+        out_specs=(IN_VMEM,) * 3,
+        compiler_params=params(8),
+    )(ids, *blocks)
+
+
+def up_part(weights, store, semaphores, place, expert, slot, quarter):
+    width = store.shape[-1]
+    start = pl.multiple_of((place ^ quarter) * width, width)
+    source = weights.at[expert, :, :, pl.ds(start, width)]
+    return [pltpu.make_async_copy(source, store.at[slot, expert], semaphores.at[slot, 0, expert])]
+
+
+def down_part(weights, store, semaphores, place, expert, slot):
+    rows = store.shape[-2]
+    copies = []
+    for side in range(2):
+        start = pl.multiple_of((place ^ (2 * slot + side)) * rows, rows)
+        source = weights.at[expert, pl.ds(start, rows), :]
+        target = store.at[slot, expert, side]
+        copies.append(pltpu.make_async_copy(source, target, semaphores.at[slot, side, expert]))
+    return copies
+
+
+def stage_kernel(ids, weights, store, semaphores):
+    slots, local_experts = store.shape[:2]
+    copies = [
+        copy
+        for slot in range(slots)
+        for expert in range(local_experts)
+        for copy in up_part(weights, store, semaphores, ids[0], expert, slot, slot)
+    ]
+    for copy in copies:
+        copy.start()
+    for copy in copies:
+        copy.wait()
+
+
+def stage(ids, weights, width):
+    shape = (2,) + weights.shape[:-1] + (width,)
+    return pl.pallas_call(
+        stage_kernel,
+        out_shape=pltpu.VMEM(shape, weights.dtype),
+        in_specs=[IN_SMEM, IN_HBM],
+        out_specs=IN_VMEM,
+        scratch_shapes=[pltpu.SemaphoreType.DMA((2, 1, weights.shape[0]))],
+        compiler_params=params(8),
+        cost_estimate=cost(0, weights.size),
+    )(ids, in_hbm(weights))
+
+
+def refill(source, store, semaphores, place, expert, quarters, down):
+    copies = []
+    for quarter in quarters:
+        slot = quarter % 2
+        if down:
+            copies += down_part(source, store, semaphores, place, expert, slot)
+        else:
+            copies += up_part(source, store, semaphores, place, expert, slot, quarter + 2)
+    return copies
+
+
+def up_kernel(opts, ids, placing, normed, *refs):
+    quarters, has_total, finish, experts, late = opts
+    refs = list(refs)
+    arrived = [refs.pop(0) for _ in quarters]
+    total_in = refs.pop(0) if has_total else None
+    source, before, _, result, store, gathered, rows, semaphores, at_start = refs
+    blocks, slots, tokens = placing.shape
+    _, local_experts, _, hidden, width = store.shape
+    capacity = slots // local_experts
+    place = ids[0]
+    first_copies = []
+    if late:
+        for expert in late[0]:
+            first_copies += refill(before, store, at_start, place, expert, late[1], late[2])
+    for copy in first_copies:
+        copy.start()
+
+    for i, quarter in enumerate(quarters):
+        start = pl.multiple_of((place ^ quarter) * width, width)
+        rows[0:tokens] = normed[:, pl.ds(start, width)]
+        rows[tokens:] = arrived[i][...]
+        for block in range(blocks):
+            picked = jnp.dot(
+                placing[block, experts[0] * capacity : experts[1] * capacity],
+                rows[block * tokens : (block + 1) * tokens],
+                preferred_element_type=jnp.float32,
+            ).astype(jnp.bfloat16)
+            at = slice(block * capacity, (block + 1) * capacity)
+            gathered[i, :, at, :] = picked.reshape(experts[1] - experts[0], capacity, width)
+
+    def pair(first):
+        for expert in (first, first + 1):
+            value = total_in[expert] if has_total else None
+            for i, quarter in enumerate(quarters):
+                part = lax.dot_general(
+                    gathered[i, expert - experts[0]],
+                    store[quarter % 2, expert].reshape(2 * hidden, width),
+                    CONTRACT_LAST,
+                    preferred_element_type=jnp.float32,
+                )
+                value = part if value is None else value + part
+            if finish:
+                gate, up = value[:, :hidden], value[:, hidden:]
+                value = (gate / (1.0 + jnp.exp(-gate)) * up).astype(jnp.bfloat16)
+                result[expert - experts[0]] = value
+            else:
+                result[expert] = value
+
+    def replaced(expert):
+        return refill(source, store, semaphores, place, expert, quarters, finish)
+
+    def some(step, carry):
+        first = experts[0] + 2 * step
+        pair(first)
+
+        @pl.when(step < (experts[1] - experts[0]) // 2 - 1)
+        def _():
+            for expert in (first, first + 1):
+                for copy in replaced(expert):
+                    copy.start()
+
+        return carry
+
+    lax.fori_loop(0, (experts[1] - experts[0]) // 2, some, 0)
+    for expert in range(experts[0], experts[1] - 2):
+        for copy in replaced(expert):
+            copy.wait()
+    for copy in first_copies:
+        copy.wait()
+
+
+def up_step(ids, placing, normed, arrived, total, quarters, finish, experts, source, before, late, store):
+    blocks, slots, tokens = placing.shape
+    _, local_experts, _, hidden, width = store.shape
+    depth = blocks * (slots // local_experts)
+    operands = [ids, placing, normed] + list(arrived)
+    if total is not None:
+        operands.append(total)
+    operands += [in_hbm(source), in_hbm(before), pinned(store)]
+    in_specs = [IN_SMEM] + [IN_VMEM] * (len(operands) - 4) + [IN_HBM, IN_HBM, IN_VMEM]
+    count = experts[1] - experts[0]
+    if finish:
+        shape = jax.ShapeDtypeStruct((count, depth, hidden), jnp.bfloat16)
+    else:
+        shape = jax.ShapeDtypeStruct((local_experts, depth, 2 * hidden), jnp.float32)
+    return pl.pallas_call(
+        functools.partial(up_kernel, (quarters, total is not None, finish, experts, late)),
+        out_shape=(shape, pltpu.VMEM(store.shape, store.dtype)),
+        in_specs=in_specs,
+        out_specs=(IN_VMEM, IN_VMEM),
+        input_output_aliases={len(operands) - 1: 1},
+        scratch_shapes=[
+            pltpu.VMEM((len(quarters), count, depth, width), jnp.bfloat16),
+            pltpu.VMEM((blocks * tokens, width), jnp.bfloat16),
+            pltpu.SemaphoreType.DMA((2, 2, local_experts)),
+            pltpu.SemaphoreType.DMA((2, 2, local_experts)),
+        ],
+        compiler_params=params(8),
+        cost_estimate=cost(0, 3 * source.size // 4),
+    )(*operands)
+
+
+def down_kernel(groups, pieces, has_total, late, *refs):
+    refs = list(refs)
+    acts = [[refs.pop(0) for _ in group] for group in pieces]
+    total_in = refs.pop(0) if has_total else None
+    copies = []
+    if late:
+        ids, source, _, result, store, semaphores = refs
+        for expert in late:
+            copies += refill(source, store, semaphores, ids[0], expert, (2, 3), True)
+        for copy in copies:
+            copy.start()
+    else:
+        store, result = refs
+
+    def one(group, index, carry):
+        expert = groups[group][0] + index
+        value = total_in[expert] if has_total else None
+        for act, q in zip(acts[group], pieces[group]):
+            weights = store[q // 2, expert, q % 2]
+            part = jnp.dot(act[index], weights, preferred_element_type=jnp.float32)
+            value = part if value is None else value + part
+        result[expert] = value
+        return carry
+
+    for group, (low, high) in enumerate(groups):
+        if group == len(groups) - 1:
+            for copy in copies:
+                copy.wait()
+        lax.fori_loop(0, high - low, functools.partial(one, group), 0, unroll=2)
+
+
+def down_step(groups, acts, store, total, late=None):
+    pieces = [tuple(sorted(group)) for group in acts]
+    _, local_experts, _, hidden, width = store.shape
+    depth = acts[0][pieces[0][0]].shape[1]
+    operands = [group[q] for group, piece in zip(acts, pieces) for q in piece]
+    in_specs = [IN_VMEM] * len(operands)
+    aliases, scratch = {}, []
+    if total is not None:
+        aliases = {len(operands): 0}
+        operands.append(total)
+        in_specs.append(IN_VMEM)
+    shapes = (jax.ShapeDtypeStruct((local_experts, depth, width), jnp.float32),)
+    if late:
+        experts, ids, source = late
+        operands += [ids, in_hbm(source)]
+        in_specs += [IN_SMEM, IN_HBM]
+        aliases[len(operands)] = 1
+        shapes += (pltpu.VMEM(store.shape, store.dtype),)
+        scratch = [pltpu.SemaphoreType.DMA((2, 2, local_experts))]
+    operands.append(pinned(store))
+    in_specs.append(IN_VMEM)
+    return pl.pallas_call(
+        functools.partial(
+            down_kernel, groups, pieces, total is not None, experts if late else None
+        ),
+        out_shape=shapes,
+        in_specs=in_specs,
+        out_specs=(IN_VMEM,) * len(shapes),
+        input_output_aliases=aliases,
+        scratch_shapes=scratch,
+        compiler_params=params(8),
+        cost_estimate=cost(0, store.size // 2),
+    )(*operands)
+
+
+def finish_kernel(opts, ids, *refs):
+    group, quarters, part, parts = opts
+    refs = list(refs)
+    acts = [refs.pop(0) for _ in quarters]
+    store, total, high, low, tokens = [refs.pop(0) for _ in range(5)]
+    kept, given, slots_out = refs
+    local_experts, depth, whole = total.shape
+    width = whole // parts
+    lanes = slice(part * width, (part + 1) * width)
+    blocks = high.shape[0]
+    capacity = depth // blocks
+
+    def place(expert, value):
+        rounded = value.astype(jnp.bfloat16)
+        at = pl.ds(pl.multiple_of(expert * capacity, capacity), capacity)
+        for block in range(blocks):
+            slots_out[block, at, :] = rounded[block * capacity : (block + 1) * capacity]
+
+    def known(expert, carry):
+        place(expert, total[expert, :, lanes])
+        return carry
+
+    def one(expert, carry):
+        value = total[expert, :, lanes]
+        for act, q in zip(acts, quarters):
+            weights = store[q // 2, expert, q % 2, :, lanes]
+            value = value + jnp.dot(
+                act[expert - group[0]], weights, preferred_element_type=jnp.float32
+            )
+        place(expert, value)
+        return carry
+
+    lax.fori_loop(0, group[0], known, 0)
+    lax.fori_loop(group[0], group[1], one, 0)
+    start = pl.multiple_of(ids[0] * whole + part * width, LANES)
+    for block in range(blocks):
+        value = jnp.dot(
+            high[block], slots_out[block], preferred_element_type=jnp.float32
+        ) + jnp.dot(low[block], slots_out[block], preferred_element_type=jnp.float32)
+        if block == 0:
+            value = value + tokens[:, pl.ds(start, width)].astype(jnp.float32)
+        target = given if block % 2 else kept
+        target[block // 2] = value.astype(jnp.bfloat16)
+
+
+def finish_step(ids, group, acts, store, total, high, low, tokens, part, parts):
+    quarters = tuple(sorted(acts))
+    blocks, count, slots = high.shape
+    width = total.shape[2] // parts
+    operands = [ids] + [acts[q] for q in quarters]
+    operands += [pinned(store), total, high, low, tokens]
+    shape = jax.ShapeDtypeStruct((blocks // 2, count, width), jnp.bfloat16)
+    return pl.pallas_call(
+        functools.partial(finish_kernel, (group, quarters, part, parts)),
+        out_shape=(shape, shape),
+        in_specs=[IN_SMEM] + [IN_VMEM] * (len(operands) - 1),
+        out_specs=(IN_VMEM, IN_VMEM),
+        scratch_shapes=[pltpu.VMEM((blocks, slots, width), jnp.bfloat16)],
+        compiler_params=params(8),
+        cost_estimate=cost(0, store.size // 8),
+    )(*operands)
+
+
+def add_kernel(own, other, *results):
+    size = own.shape[0] // len(results)
+    for i, result in enumerate(results):
+        for j in range(size):
+            value = own[j * len(results) + i].astype(jnp.float32)
+            value = value + other[j * len(results) + i].astype(jnp.float32)
+            result[j] = value.astype(jnp.bfloat16)
+
+
+def add_up(own, other):
+    count = own.shape[0]
+    sides = min(2, count)
+    shape = jax.ShapeDtypeStruct((count // sides,) + own.shape[1:], own.dtype)
+    return pl.pallas_call(
+        add_kernel,
+        out_shape=(shape,) * sides,
+        in_specs=[IN_VMEM, IN_VMEM],
+        out_specs=(IN_VMEM,) * sides,
+        compiler_params=params(8),
+    )(own, other)
+
+
+def sum_kernel(*refs):
+    *parts, result = refs
+    width = parts[0].shape[2]
+    for i in range(result.shape[2] // width):
+        value = parts[2 * i][0].astype(jnp.float32) + parts[2 * i + 1][0].astype(jnp.float32)
+        result[0, :, i * width : (i + 1) * width] = value.astype(jnp.bfloat16)
+
+
+def gathered_tokens(activations, routes, gate_weights, norm_gain, gate_up_weights, down_weights):
+    tokens = activations[0]
+    token_count, features = tokens.shape
+    local_experts = gate_up_weights.shape[0]
+    rows = lax.axis_size("expert")
+    dp_devices = lax.axis_size("dp")
+    sections = lax.axis_size("section")
+    capacity = token_count * routes.shape[2] // (local_experts * rows)
+    slots = local_experts * capacity
+    width = features // dp_devices
+    ids = jnp.stack([lax.axis_index("dp"), lax.axis_index("expert") * local_experts])
+    ids = ids.astype(jnp.int32)
+
+    normed, own = normalize(ids, tokens, norm_gain, routes[0].T, gate_weights[0].T, width)
+    blocks = [flipped(own, "expert", j) for j in range(1, rows)]
+    store = stage(ids, gate_up_weights, width)
+    mine = collect(blocks, token_count, width, store)
+    across = flipped(mine, "dp", 2)
+    beside = flipped(mine, "dp", 1)
+    placing, high, low = plan(
+        ids, [own] + blocks, token_count, slots, capacity, routes.shape[2]
+    )
+    everyone = (0, local_experts)
+    half = local_experts // 2
+    groups = ((0, half), (half, local_experts))
+    step = functools.partial(up_step, ids, placing, normed)
+    wide, tall = gate_up_weights, down_weights
+    left = (local_experts - 2, local_experts - 1)
+    total, store = step([mine], None, (0,), False, everyone, wide, wide, None, store)
+    across = relayed(across, total)
+    far = flipped(across, "dp", 1)
+    late = (left, (0,), False)
+    total, store = step([beside], total, (1,), False, everyone, wide, wide, late, store)
+    step = functools.partial(step, [across, far], total, (2, 3), True)
+    late = (left, (1,), False)
+    act, store = step(groups[0], tall, wide, late, store)
+    acts = [{0: act, 1: flipped(act, "dp", 1), 2: flipped(act, "dp", 2)}]
+    late = ((half - 2, half - 1), (2, 3), True)
+    act, store = step(groups[1], tall, tall, late, store)
+    acts.append({0: act, 1: flipped(act, "dp", 1), 2: flipped(act, "dp", 2)})
+    near = [{q: act[q] for q in (0, 1)} for act in acts]
+    summed, store = down_step(groups, near, store, None, (left, ids, tall))
+    middle = relayed(acts[0][2], summed)
+    middle = {2: middle, 3: flipped(middle, "dp", 1)}
+    (summed,) = down_step(groups[:1], [middle], store, summed)
+    last = relayed(acts[1][2], summed)
+    last = {2: last, 3: flipped(last, "dp", 1)}
+    parts = 2
+    received = []
+    for part in range(parts):
+        kept, given = finish_step(
+            ids, groups[1], last, store, summed, high, low, tokens, part, parts
+        )
+        near, given = add_up(kept, flipped(given, "expert", 1))
+        for block, j in ((given, 2), (near, 0)):
+            route = [
+                (s * rows + e, ((s + 1) % sections) * rows + (e ^ j))
+                for s in range(sections)
+                for e in range(rows)
+            ]
+            received.append(lax.ppermute(block, ("section", "expert"), route))
+    return pl.pallas_call(
+        sum_kernel,
+        out_shape=jax.ShapeDtypeStruct((1, token_count, width), jnp.bfloat16),
+        in_specs=[IN_VMEM] * len(received),
+        out_specs=IN_VMEM,
+        compiler_params=params(8),
+    )(*received)
+
+
+def routed_rows(activations, routes, gate_weights, norm_gain, gate_up_weights, down_weights):
     tokens_here = activations[0]
     token_count, feature_count = tokens_here.shape
     top_count = routes.shape[2]
@@ -67,8 +617,22 @@
     branch = jnp.sum(picked.astype(jnp.float32) * gate_weights[0][:, :, None], axis=1)
     residual = lax.dynamic_slice_in_dim(widened, dp_place * slice_width, slice_width, 1)
     finished = (residual + branch).astype(jnp.bfloat16)
-    arrived = passed_along(finished, "section", 1)
+    arrived = shifted(finished, "section", 1)
     return arrived[None]
+
+
+def body(activations, routes, gate_weights, norm_gain, gate_up_weights, down_weights):
+    token_count, top_count = routes.shape[1], routes.shape[2]
+    local_experts = gate_up_weights.shape[0]
+    rows = lax.axis_size("expert")
+    capacity = token_count * top_count // (local_experts * rows)
+    few = token_count <= local_experts * capacity
+    aligned = capacity % 16 == 0 and token_count % 16 == 0
+    suits = rows == 4 and lax.axis_size("dp") == 4 and token_count * 2 == LANES
+    form = gathered_tokens if few and aligned and suits else routed_rows
+    return form(
+        activations, routes, gate_weights, norm_gain, gate_up_weights, down_weights
+    )
 
 
 def solution(mesh):

time: 185 us -> 84.5 us (0.46)
  waiting for transfers between devices: 82.7 us -> 15 us
  Pallas kernels: 0 us -> 50.1 us
  matrix products: 36.1 us -> 0 us
  blocking collectives: 31.8 us -> 0 us
  between operations: 13.5 us -> 0.19 us
  starting transfers between devices: 6.18 us -> 19 us
  local copies, waits for them, and re-layouts: 7.31 us -> 0.01 us
  other arithmetic: 6.67 us -> 0.07 us
    all_gather x2 -> x0, waiting for transfers between devices: 53.5 us -> none  [the longest x1 33.7 us: body(): lax.all_gather(arriving, 'dp', axis=3, tiled=True)]
    pallas_call x0 -> x18, Pallas kernels: none -> 50.1 us  [the longest x4 25.9 us: up_step(): pl.pallas_call(functools.partial(up_kernel, (quarters, total is not None,...]
    dot_general x3 -> x0, matrix products: 36.1 us -> none  [the longest x1 22.5 us: body(): jnp.einsum('seck,ejhk->jsech', lax.all_gather(arriving, 'dp', axis=3, til...]
    all_to_all x1 -> x0, blocking collectives: 31.8 us -> none  [body(): lax.all_to_all(outgoing, 'expert', split_axis=0, concat_axis=0, tiled=True)]
    all_to_all x1 -> x0, waiting for transfers between devices: 25.7 us -> none  [body(): lax.all_to_all(expert_out, 'expert', split_axis=0, concat_axis=0, tiled=T...]
    ppermute x1 -> x18, starting transfers between devices: 1.54 us -> 19 us  [the longest x14 13 us: flipped(): lax.ppermute(block, axis, [(i, i ^ bit) for i in range(lax.axis_size(axis...]
    ppermute x1 -> x18, waiting for transfers between devices: 3.49 us -> 15 us  [the longest x14 11 us: flipped(): lax.ppermute(block, axis, [(i, i ^ bit) for i in range(lax.axis_size(axis...]
    all_to_all x1 -> x0, starting transfers between devices: 4.6 us -> none  [body(): lax.all_to_all(expert_out, 'expert', split_axis=0, concat_axis=0, tiled=T...]
  transfers between devices with their start and end apart: 4 -> 18, of which waited for: 4 -> 10; matrix products, arithmetic and copies ran while one was open for 0% -> 0% of each run, Pallas kernels for 0% -> 39%
where the time goes in v2:
time: 84.5 us; the launch traced here: 84.4 us
  Pallas kernels  50.1 us (59%)
  starting transfers between devices  19 us (22%)
  waiting for transfers between devices  15 us (18%)
    pallas_call x4, Pallas kernels, up_step(): pl.pallas_call(functools.partial(up_kernel, (quarters, total is not None,...  25.9 us
    ppermute x14, starting transfers between devices, flipped(): lax.ppermute(block, axis, [(i, i ^ bit) for i in range(lax.axis_size(axis...  13 us
    ppermute x14, waiting for transfers between devices, flipped(): lax.ppermute(block, axis, [(i, i ^ bit) for i in range(lax.axis_size(axis...  11 us
    pallas_call x1, Pallas kernels, stage(): pl.pallas_call(stage_kernel, out_shape=pltpu.VMEM(shape, weights.dtype),...  8.99 us
    pallas_call x2, Pallas kernels, down_step(): pl.pallas_call(functools.partial(down_kernel, groups, pieces, total is no...  6.37 us
    ppermute x4, starting transfers between devices, gathered_tokens(): received.append(lax.ppermute(block, ('section', 'expert'), route))  5.98 us
    ppermute x4, waiting for transfers between devices, gathered_tokens(): received.append(lax.ppermute(block, ('section', 'expert'), route))  4.02 us
    pallas_call x2, Pallas kernels, finish_step(): pl.pallas_call(functools.partial(finish_kernel, (group, quarters, part, p...  3.87 us
  transfers between devices with their start and end apart: 18, of which 10 were waited for; matrix products, arithmetic and copies ran while one was open for 0% of the time, Pallas kernels for 39%

profile of v2, /device:TPU:0, one launch (start us, length us, event | category | flops | bytes accessed | tf_op | source)
XLA Modules:
  0.0 84.4 jit_solution(16199945842387322754)
XLA Ops:
  0.1 2.0 %shard_map.64 = (bf16[64,4096]{1,0:T(8,128)(2,1)S(1)}, bf16[528,128]{1,0:T(8,128)(2,1)S(1)}) custom-call(s32[2]{0:T(128)S(1)} %pad_add_fusion.ids.refs_4_, bf16[64,4096]{1,0:T(8,128)(2,1)} %bitcast.9, bf16[4096]{0:T(1024)(128)(2,1)} %refs_1_.2, s32[8,64]{1,0:T(8,128)} %bitcast.12, f32[8,64]{1,0:T(8,128)} %bitcast.13), custom_call_target="tpu_custom_call" | custom-call | tf_op jit(solution)/shard_map/pallas_call | solution.py:78
  2.0 5.1 %collective-permute-start.2 = (bf16[528,128]{1,0:T(8,128)(2,1)S(1)}, bf16[528,128]{1,0:T(8,128)(2,1)S(1)}, u32[]{:S(2)}, u32[]{:S(2)}) collective-permute-start(bf16[528,128]{1,0:T(8,128)(2,1)S(1)} %get-tuple-element.28.refs_0_), channel_id=1, source_target_pairs={{0,3},{1,2},{2,1},{3,0},{4,7},{5,6},{6,5},{7,4},{8,11},{9,10},{10,... | collective-permute-start | bytes 405512 | tf_op jit(solution)/shard_map/ppermute | solution.py:40
  7.2 0.6 collective-permute-start
  7.8 9.0 %shard_map.66.refs_3_ = bf16[2,8,2,384,1024]{4,3,2,1,0:T(8,128)(2,1)S(1)} custom-call(s32[2]{0:T(128)S(1)} %pad_add_fusion.ids.refs_4_, bf16[8,2,384,4096]{3,2,1,0:T(8,128)(2,1)} %refs_4_.2), custom_call_target="tpu_custom_call" | custom-call | bytes 25165824 | tf_op jit(solution)/shard_map/pallas_call | solution.py:210
  16.8 1.8 %collective-permute-done.1.refs_2_.refs_1_ = bf16[528,128]{1,0:T(8,128)(2,1)S(1)} collective-permute-done((bf16[528,128]{1,0:T(8,128)(2,1)S(1)}, bf16[528,128]{1,0:T(8,128)(2,1)S(1)}, u32[]{:S(2)}, u32[]{:S(2)}) %collective-permute-start.1) | collective-permute-done | bytes 135200 | tf_op jit(solution)/shard_map/ppermute | solution.py:40
  18.7 1.6 %collective-permute-start.3 = (bf16[192,1024]{1,0:T(8,128)(2,1)S(1)}, bf16[192,1024]{1,0:T(8,128)(2,1)S(1)}, u32[]{:S(2)}, u32[]{:S(2)}) collective-permute-start(bf16[192,1024]{1,0:T(8,128)(2,1)S(1)} %shard_map.67.refs_0_), channel_id=1, source_target_pairs={{0,8},{4,12},{8,0},{12,4},{1,9},{5,13},{9,1},{13,5},{2,10},{6,14},... | collective-permute-start | bytes 1179656 | tf_op jit(solution)/shard_map/ppermute | solution.py:40
  20.2 2.1 %shard_map.65 = (bf16[4,128,64]{2,1,0:T(8,128)(2,1)S(1)}, bf16[4,64,128]{2,1,0:T(8,128)(2,1)S(1)}, bf16[4,64,128]{2,1,0:T(8,128)(2,1)S(1)}) custom-call(s32[2]{0:T(128)S(1)} %pad_add_fusion.ids.refs_4_, bf16[528,128]{1,0:T(8,128)(2,1)S(1)} %get-tuple-element.28.refs_0_, bf16[528,128]{1,0:T(8,128)(2,1)S(1)} %collective-permute-done.refs_1_.refs_0_, ...), custom_call_target="tpu_custom_call" | custom-call | tf_op jit(solution)/shard_map/pallas_call | solution.py:163
  22.3 6.7 %shard_map.68 = (f32[8,64,768]{2,1,0:T(8,128)S(1)}, bf16[2,8,2,384,1024]{4,3,2,1,0:T(8,128)(2,1)S(1)}) custom-call(s32[2]{0:T(128)S(1)} %pad_add_fusion.ids.refs_4_, bf16[4,128,64]{2,1,0:T(8,128)(2,1)S(1)} %get-tuple-element.29.placing, bf16[64,4096]{1,0:T(8,128)(2,1)S(1)} %get-tuple-element.30.normed, ...), custom_call_target="tpu_custom_call", output_to_operand_aliasing={{1}: (6, {})} | custom-call | bytes 18874368 | tf_op jit(solution)/shard_map/pallas_call | solution.py:317
  29.1 0.6 collective-permute-start.4
  29.6 6.7 %shard_map.70 = (f32[8,64,768]{2,1,0:T(8,128)S(1)}, bf16[2,8,2,384,1024]{4,3,2,1,0:T(8,128)(2,1)S(1)}) custom-call(s32[2]{0:T(128)S(1)} %pad_add_fusion.ids.refs_4_, bf16[4,128,64]{2,1,0:T(8,128)(2,1)S(1)} %get-tuple-element.29.placing, bf16[64,4096]{1,0:T(8,128)(2,1)S(1)} %get-tuple-element.30.normed, ...), custom_call_target="tpu_custom_call", output_to_operand_aliasing={{1}: (7, {})} | custom-call | bytes 18874368 | tf_op jit(solution)/shard_map/pallas_call | solution.py:317
  36.4 6.2 %shard_map.71 = (bf16[4,64,384]{2,1,0:T(8,128)(2,1)S(1)}, bf16[2,8,2,384,1024]{4,3,2,1,0:T(8,128)(2,1)S(1)}) custom-call(s32[2]{0:T(128)S(1)} %pad_add_fusion.ids.refs_4_, bf16[4,128,64]{2,1,0:T(8,128)(2,1)S(1)} %get-tuple-element.29.placing, bf16[64,4096]{1,0:T(8,128)(2,1)S(1)} %get-tuple-element.30.normed, ...), custom_call_target="tpu_custom_call", output_to_operand_aliasing={{1}: (8, {})} | custom-call | bytes 9437184 | tf_op jit(solution)/shard_map/pallas_call | solution.py:317
  42.6 6.3 %shard_map.72 = (bf16[4,64,384]{2,1,0:T(8,128)(2,1)S(1)}, bf16[2,8,2,384,1024]{4,3,2,1,0:T(8,128)(2,1)S(1)}) custom-call(s32[2]{0:T(128)S(1)} %pad_add_fusion.ids.refs_4_, bf16[4,128,64]{2,1,0:T(8,128)(2,1)S(1)} %get-tuple-element.29.placing, bf16[64,4096]{1,0:T(8,128)(2,1)S(1)} %get-tuple-element.30.normed, ...), custom_call_target="tpu_custom_call", output_to_operand_aliasing={{1}: (8, {})} | custom-call | bytes 9437184 | tf_op jit(solution)/shard_map/pallas_call | solution.py:317
  49.0 0.5 collective-permute-start.8
  49.5 0.9 %collective-permute-start.7 = (bf16[4,64,384]{2,1,0:T(8,128)(2,1)S(1)}, bf16[4,64,384]{2,1,0:T(8,128)(2,1)S(1)}, u32[]{:S(2)}, u32[]{:S(2)}) collective-permute-start(bf16[4,64,384]{2,1,0:T(8,128)(2,1)S(1)} %get-tuple-element.37.refs_0_), channel_id=1, source_target_pairs={{0,8},{4,12},{8,0},{12,4},{1,9},{5,13},{9,1},{13,5},{2,10},{6,14},... | collective-permute-start | bytes 589832 | tf_op jit(solution)/shard_map/ppermute | solution.py:40
  50.4 0.3 collective-permute-done.8.refs_1_
  50.7 5.0 %shard_map.73 = (f32[8,64,1024]{2,1,0:T(8,128)S(1)}, bf16[2,8,2,384,1024]{4,3,2,1,0:T(8,128)(2,1)S(1)}) custom-call(bf16[4,64,384]{2,1,0:T(8,128)(2,1)S(1)} %get-tuple-element.37.refs_0_, bf16[4,64,384]{2,1,0:T(8,128)(2,1)S(1)} %collective-permute-done.8.refs_1_, bf16[4,64,384]{2,1,0:T(8,128)(2,1)S(1)} %get-tuple-element.36.refs_2_, ...), custom_call_target="tpu_custom_call", output_to_operand_aliasing={{1}: (6, {})} | custom-call | bytes 6291456 | tf_op jit(solution)/shard_map/pallas_call | solution.py:386
  55.7 0.7 collective-permute-done.7.block
  56.5 1.4 %collective-permute-start.6 = (bf16[4,64,384]{2,1,0:T(8,128)(2,1)S(1)}, bf16[4,64,384]{2,1,0:T(8,128)(2,1)S(1)}, u32[]{:S(2)}, u32[]{:S(2)}) collective-permute-start(bf16[4,64,384]{2,1,0:T(8,128)(2,1)S(1)} %get-tuple-element.36.refs_2_), channel_id=1, source_target_pairs={{0,8},{4,12},{8,0},{12,4},{1,9},{5,13},{9,1},{13,5},{2,10},{6,14},... | collective-permute-start | bytes 589832 | tf_op jit(solution)/shard_map/ppermute | solution.py:40
  57.9 1.4 %shard_map.75.after.refs_3_ = f32[8,64,1024]{2,1,0:T(8,128)S(1)} custom-call(bf16[4,64,384]{2,1,0:T(8,128)(2,1)S(1)} %shard_map.74.refs_0_, bf16[4,64,384]{2,1,0:T(8,128)(2,1)S(1)} %collective-permute-done.10.refs_1_, f32[8,64,1024]{2,1,0:T(8,128)S(1)} %get-tuple-element.39.after.refs_2_, ...), custom_call_target="tpu_custom_call", output_to_operand_aliasing={{}: (2, {})} | custom-call | bytes 6291456 | tf_op jit(solution)/shard_map/pallas_call | solution.py:386
  59.3 4.5 %collective-permute-done.6.block = bf16[4,64,384]{2,1,0:T(8,128)(2,1)S(1)} collective-permute-done((bf16[4,64,384]{2,1,0:T(8,128)(2,1)S(1)}, bf16[4,64,384]{2,1,0:T(8,128)(2,1)S(1)}, u32[]{:S(2)}, u32[]{:S(2)}) %collective-permute-start.6) | collective-permute-done | bytes 196640 | tf_op jit(solution)/shard_map/ppermute | solution.py:40
  63.9 1.4 %collective-permute-done.11.refs_1_ = bf16[4,64,384]{2,1,0:T(8,128)(2,1)S(1)} collective-permute-done((bf16[4,64,384]{2,1,0:T(8,128)(2,1)S(1)}, bf16[4,64,384]{2,1,0:T(8,128)(2,1)S(1)}, u32[]{:S(2)}, u32[]{:S(2)}) %collective-permute-start.11) | collective-permute-done | bytes 196640 | tf_op jit(solution)/shard_map/ppermute | solution.py:40
  65.3 1.9 %shard_map.79 = (bf16[2,64,512]{2,1,0:T(8,128)(2,1)S(1)}, bf16[2,64,512]{2,1,0:T(8,128)(2,1)S(1)}) custom-call(s32[2]{0:T(128)S(1)} %pad_add_fusion.ids.refs_4_, bf16[4,64,384]{2,1,0:T(8,128)(2,1)S(1)} %shard_map.76.refs_0_, bf16[4,64,384]{2,1,0:T(8,128)(2,1)S(1)} %collective-permute-done.11.refs_1_, ...), custom_call_target="tpu_custom_call" | custom-call | bytes 1572864 | tf_op jit(solution)/shard_map/pallas_call | solution.py:452
  67.3 1.9 %shard_map.77 = (bf16[2,64,512]{2,1,0:T(8,128)(2,1)S(1)}, bf16[2,64,512]{2,1,0:T(8,128)(2,1)S(1)}) custom-call(s32[2]{0:T(128)S(1)} %pad_add_fusion.ids.refs_4_, bf16[4,64,384]{2,1,0:T(8,128)(2,1)S(1)} %shard_map.76.refs_0_, bf16[4,64,384]{2,1,0:T(8,128)(2,1)S(1)} %collective-permute-done.11.refs_1_, ...), custom_call_target="tpu_custom_call" | custom-call | bytes 1572864 | tf_op jit(solution)/shard_map/pallas_call | solution.py:452
  69.3 2.1 %collective-permute-start.12 = (bf16[2,64,512]{2,1,0:T(8,128)(2,1)S(1)}, bf16[2,64,512]{2,1,0:T(8,128)(2,1)S(1)}, u32[]{:S(2)}, u32[]{:S(2)}) collective-permute-start(bf16[2,64,512]{2,1,0:T(8,128)(2,1)S(1)} %get-tuple-element.44), channel_id=1, source_target_pairs={{0,1},{1,0},{2,3},{3,2},{4,5},{5,4},{6,7},{7,6},{8,9},{9,8},{10,11... | collective-permute-start | bytes 393224 | tf_op jit(solution)/shard_map/ppermute | solution.py:40
  71.4 2.3 %collective-permute-done.15.other = bf16[2,64,512]{2,1,0:T(8,128)(2,1)S(1)} collective-permute-done((bf16[2,64,512]{2,1,0:T(8,128)(2,1)S(1)}, bf16[2,64,512]{2,1,0:T(8,128)(2,1)S(1)}, u32[]{:S(2)}, u32[]{:S(2)}) %collective-permute-start.15) | collective-permute-done | bytes 131104 | tf_op jit(solution)/shard_map/ppermute | solution.py:40
  73.6 1.6 %collective-permute-start.16 = (bf16[1,64,512]{2,1,0:T(8,128)(2,1)S(1)}, bf16[1,64,512]{2,1,0:T(8,128)(2,1)S(1)}, u32[]{:S(2)}, u32[]{:S(2)}) collective-permute-start(bf16[1,64,512]{2,1,0:T(8,128)(2,1)S(1)} %get-tuple-element.49), channel_id=1, source_target_pairs={{0,18},{1,19},{2,16},{3,17},{16,2},{17,3},{18,0},{19,1},{4,22},{5,... | collective-permute-start | bytes 196616 | tf_op jit(solution)/shard_map/ppermute | solution.py:553
  75.2 0.5 collective-permute-start.17
  75.8 3.6 %collective-permute-start.13 = (bf16[1,64,512]{2,1,0:T(8,128)(2,1)S(1)}, bf16[1,64,512]{2,1,0:T(8,128)(2,1)S(1)}, u32[]{:S(2)}, u32[]{:S(2)}) collective-permute-start(bf16[1,64,512]{2,1,0:T(8,128)(2,1)S(1)} %get-tuple-element.45), channel_id=1, source_target_pairs={{0,18},{1,19},{2,16},{3,17},{16,2},{17,3},{18,0},{19,1},{4,22},{5,... | collective-permute-start | bytes 196616 | tf_op jit(solution)/shard_map/ppermute | solution.py:553
  79.7 1.9 %collective-permute-done.16.refs_2_ = bf16[1,64,512]{2,1,0:T(8,128)(2,1)S(1)} collective-permute-done((bf16[1,64,512]{2,1,0:T(8,128)(2,1)S(1)}, bf16[1,64,512]{2,1,0:T(8,128)(2,1)S(1)}, u32[]{:S(2)}, u32[]{:S(2)}) %collective-permute-start.16) | collective-permute-done | bytes 65568 | tf_op jit(solution)/shard_map/ppermute | solution.py:553
  81.6 0.8 collective-permute-done.13.refs_0_
  82.3 1.4 %collective-permute-done.14.refs_1_ = bf16[1,64,512]{2,1,0:T(8,128)(2,1)S(1)} collective-permute-done((bf16[1,64,512]{2,1,0:T(8,128)(2,1)S(1)}, bf16[1,64,512]{2,1,0:T(8,128)(2,1)S(1)}, u32[]{:S(2)}, u32[]{:S(2)}) %collective-permute-start.14) | collective-permute-done | bytes 65568 | tf_op jit(solution)/shard_map/ppermute | solution.py:553
  83.7 0.7 shard_map.81
  (25 shorter events, 0.9 us)
Async XLA Ops:
  2.0 14.8 %collective-permute-start.2 = (bf16[528,128]{1,0:T(8,128)(2,1)S(1)}, bf16[528,128]{1,0:T(8,128)(2,1)S(1)}, u32[]{:S(2)}, u32[]{:S(2)}) collective-permute-start(bf16[528,128]{1,0:T(8,128)(2,1)S(1)} %get-tuple-element.28.refs_0_), channel_id=1, source_target_pairs={{0,3},{1,2},{2,1},{3,0},{4,7},{5,6},{6,5},{7,4},{8,11},{9,10},{10,... | collective-permute-start | bytes 405512 | tf_op jit(solution)/shard_map/ppermute | solution.py:40
  7.2 11.4 %collective-permute-start.1 = (bf16[528,128]{1,0:T(8,128)(2,1)S(1)}, bf16[528,128]{1,0:T(8,128)(2,1)S(1)}, u32[]{:S(2)}, u32[]{:S(2)}) collective-permute-start(bf16[528,128]{1,0:T(8,128)(2,1)S(1)} %get-tuple-element.28.refs_0_), channel_id=1, source_target_pairs={{0,2},{1,3},{2,0},{3,1},{4,6},{5,7},{6,4},{7,5},{8,10},{9,11},{10,... | collective-permute-start | bytes 405512 | tf_op jit(solution)/shard_map/ppermute | solution.py:40
  7.2 11.4 %collective-permute-start = (bf16[528,128]{1,0:T(8,128)(2,1)S(1)}, bf16[528,128]{1,0:T(8,128)(2,1)S(1)}, u32[]{:S(2)}, u32[]{:S(2)}) collective-permute-start(bf16[528,128]{1,0:T(8,128)(2,1)S(1)} %get-tuple-element.28.refs_0_), channel_id=1, source_target_pairs={{0,1},{1,0},{2,3},{3,2},{4,5},{5,4},{6,7},{7,6},{8,9},{9,8},{10,11... | collective-permute-start | bytes 405512 | tf_op jit(solution)/shard_map/ppermute | solution.py:40
  18.7 10.4 %collective-permute-start.3 = (bf16[192,1024]{1,0:T(8,128)(2,1)S(1)}, bf16[192,1024]{1,0:T(8,128)(2,1)S(1)}, u32[]{:S(2)}, u32[]{:S(2)}) collective-permute-start(bf16[192,1024]{1,0:T(8,128)(2,1)S(1)} %shard_map.67.refs_0_), channel_id=1, source_target_pairs={{0,8},{4,12},{8,0},{12,4},{1,9},{5,13},{9,1},{13,5},{2,10},{6,14},... | collective-permute-start | bytes 1179656 | tf_op jit(solution)/shard_map/ppermute | solution.py:40
  20.2 9.4 %collective-permute-start.5 = (bf16[192,1024]{1,0:T(8,128)(2,1)S(1)}, bf16[192,1024]{1,0:T(8,128)(2,1)S(1)}, u32[]{:S(2)}, u32[]{:S(2)}) collective-permute-start(bf16[192,1024]{1,0:T(8,128)(2,1)S(1)} %shard_map.67.refs_0_), channel_id=1, source_target_pairs={{0,4},{4,0},{8,12},{12,8},{1,5},{5,1},{9,13},{13,9},{2,6},{6,2},{1... | collective-permute-start | bytes 1179656 | tf_op jit(solution)/shard_map/ppermute | solution.py:40
  29.1 7.3 %collective-permute-start.4 = (bf16[192,1024]{1,0:T(8,128)(2,1)S(1)}, bf16[192,1024]{1,0:T(8,128)(2,1)S(1)}, u32[]{:S(2)}, u32[]{:S(2)}) collective-permute-start(bf16[192,1024]{1,0:T(8,128)(2,1)S(1)} %shard_map.69.refs_0_), channel_id=1, source_target_pairs={{0,4},{4,0},{8,12},{12,8},{1,5},{5,1},{9,13},{13,9},{2,6},{6,2},{1... | collective-permute-start | bytes 1179656 | tf_op jit(solution)/shard_map/ppermute | solution.py:40
  48.9 1.5 %collective-permute-start.9 = (bf16[4,64,384]{2,1,0:T(8,128)(2,1)S(1)}, bf16[4,64,384]{2,1,0:T(8,128)(2,1)S(1)}, u32[]{:S(2)}, u32[]{:S(2)}) collective-permute-start(bf16[4,64,384]{2,1,0:T(8,128)(2,1)S(1)} %get-tuple-element.36.refs_2_), channel_id=1, source_target_pairs={{0,4},{4,0},{8,12},{12,8},{1,5},{5,1},{9,13},{13,9},{2,6},{6,2},{1... | collective-permute-start | bytes 589832 | tf_op jit(solution)/shard_map/ppermute | solution.py:40
  49.0 1.7 %collective-permute-start.8 = (bf16[4,64,384]{2,1,0:T(8,128)(2,1)S(1)}, bf16[4,64,384]{2,1,0:T(8,128)(2,1)S(1)}, u32[]{:S(2)}, u32[]{:S(2)}) collective-permute-start(bf16[4,64,384]{2,1,0:T(8,128)(2,1)S(1)} %get-tuple-element.37.refs_0_), channel_id=1, source_target_pairs={{0,4},{4,0},{8,12},{12,8},{1,5},{5,1},{9,13},{13,9},{2,6},{6,2},{1... | collective-permute-start | bytes 589832 | tf_op jit(solution)/shard_map/ppermute | solution.py:40
  49.5 6.9 %collective-permute-start.7 = (bf16[4,64,384]{2,1,0:T(8,128)(2,1)S(1)}, bf16[4,64,384]{2,1,0:T(8,128)(2,1)S(1)}, u32[]{:S(2)}, u32[]{:S(2)}) collective-permute-start(bf16[4,64,384]{2,1,0:T(8,128)(2,1)S(1)} %get-tuple-element.37.refs_0_), channel_id=1, source_target_pairs={{0,8},{4,12},{8,0},{12,4},{1,9},{5,13},{9,1},{13,5},{2,10},{6,14},... | collective-permute-start | bytes 589832 | tf_op jit(solution)/shard_map/ppermute | solution.py:40
  55.7 9.6 %copy-start = (bf16[1,64,4096]{2,1,0:T(8,128)(2,1)S(1)}, bf16[1,64,4096]{2,1,0:T(8,128)(2,1)}, u32[]{:S(2)}) copy-start(bf16[1,64,4096]{2,1,0:T(8,128)(2,1)} %param.6) | copy-start | bytes 1572868
  56.4 1.5 %collective-permute-start.10 = (bf16[4,64,384]{2,1,0:T(8,128)(2,1)S(1)}, bf16[4,64,384]{2,1,0:T(8,128)(2,1)S(1)}, u32[]{:S(2)}, u32[]{:S(2)}) collective-permute-start(bf16[4,64,384]{2,1,0:T(8,128)(2,1)S(1)} %shard_map.74.refs_0_), channel_id=1, source_target_pairs={{0,4},{4,0},{8,12},{12,8},{1,5},{5,1},{9,13},{13,9},{2,6},{6,2},{1... | collective-permute-start | bytes 589832 | tf_op jit(solution)/shard_map/ppermute | solution.py:40
  56.5 7.3 %collective-permute-start.6 = (bf16[4,64,384]{2,1,0:T(8,128)(2,1)S(1)}, bf16[4,64,384]{2,1,0:T(8,128)(2,1)S(1)}, u32[]{:S(2)}, u32[]{:S(2)}) collective-permute-start(bf16[4,64,384]{2,1,0:T(8,128)(2,1)S(1)} %get-tuple-element.36.refs_2_), channel_id=1, source_target_pairs={{0,8},{4,12},{8,0},{12,4},{1,9},{5,13},{9,1},{13,5},{2,10},{6,14},... | collective-permute-start | bytes 589832 | tf_op jit(solution)/shard_map/ppermute | solution.py:40
  63.8 1.5 %collective-permute-start.11 = (bf16[4,64,384]{2,1,0:T(8,128)(2,1)S(1)}, bf16[4,64,384]{2,1,0:T(8,128)(2,1)S(1)}, u32[]{:S(2)}, u32[]{:S(2)}) collective-permute-start(bf16[4,64,384]{2,1,0:T(8,128)(2,1)S(1)} %shard_map.76.refs_0_), channel_id=1, source_target_pairs={{0,4},{4,0},{8,12},{12,8},{1,5},{5,1},{9,13},{13,9},{2,6},{6,2},{1... | collective-permute-start | bytes 589832 | tf_op jit(solution)/shard_map/ppermute | solution.py:40
  67.3 6.3 %collective-permute-start.15 = (bf16[2,64,512]{2,1,0:T(8,128)(2,1)S(1)}, bf16[2,64,512]{2,1,0:T(8,128)(2,1)S(1)}, u32[]{:S(2)}, u32[]{:S(2)}) collective-permute-start(bf16[2,64,512]{2,1,0:T(8,128)(2,1)S(1)} %get-tuple-element.48), channel_id=1, source_target_pairs={{0,1},{1,0},{2,3},{3,2},{4,5},{5,4},{6,7},{7,6},{8,9},{9,8},{10,11... | collective-permute-start | bytes 393224 | tf_op jit(solution)/shard_map/ppermute | solution.py:40
  69.3 6.5 %collective-permute-start.12 = (bf16[2,64,512]{2,1,0:T(8,128)(2,1)S(1)}, bf16[2,64,512]{2,1,0:T(8,128)(2,1)S(1)}, u32[]{:S(2)}, u32[]{:S(2)}) collective-permute-start(bf16[2,64,512]{2,1,0:T(8,128)(2,1)S(1)} %get-tuple-element.44), channel_id=1, source_target_pairs={{0,1},{1,0},{2,3},{3,2},{4,5},{5,4},{6,7},{7,6},{8,9},{9,8},{10,11... | collective-permute-start | bytes 393224 | tf_op jit(solution)/shard_map/ppermute | solution.py:40
  73.6 7.9 %collective-permute-start.16 = (bf16[1,64,512]{2,1,0:T(8,128)(2,1)S(1)}, bf16[1,64,512]{2,1,0:T(8,128)(2,1)S(1)}, u32[]{:S(2)}, u32[]{:S(2)}) collective-permute-start(bf16[1,64,512]{2,1,0:T(8,128)(2,1)S(1)} %get-tuple-element.49), channel_id=1, source_target_pairs={{0,18},{1,19},{2,16},{3,17},{16,2},{17,3},{18,0},{19,1},{4,22},{5,... | collective-permute-start | bytes 196616 | tf_op jit(solution)/shard_map/ppermute | solution.py:553
  75.2 6.3 %collective-permute-start.17 = (bf16[1,64,512]{2,1,0:T(8,128)(2,1)S(1)}, bf16[1,64,512]{2,1,0:T(8,128)(2,1)S(1)}, u32[]{:S(2)}, u32[]{:S(2)}) collective-permute-start(bf16[1,64,512]{2,1,0:T(8,128)(2,1)S(1)} %get-tuple-element.50), channel_id=1, source_target_pairs={{0,16},{1,17},{2,18},{3,19},{16,0},{17,1},{18,2},{19,3},{4,20},{5,... | collective-permute-start | bytes 196616 | tf_op jit(solution)/shard_map/ppermute | solution.py:553
  75.8 6.5 %collective-permute-start.13 = (bf16[1,64,512]{2,1,0:T(8,128)(2,1)S(1)}, bf16[1,64,512]{2,1,0:T(8,128)(2,1)S(1)}, u32[]{:S(2)}, u32[]{:S(2)}) collective-permute-start(bf16[1,64,512]{2,1,0:T(8,128)(2,1)S(1)} %get-tuple-element.45), channel_id=1, source_target_pairs={{0,18},{1,19},{2,16},{3,17},{16,2},{17,3},{18,0},{19,1},{4,22},{5,... | collective-permute-start | bytes 196616 | tf_op jit(solution)/shard_map/ppermute | solution.py:553
  79.4 4.3 %collective-permute-start.14 = (bf16[1,64,512]{2,1,0:T(8,128)(2,1)S(1)}, bf16[1,64,512]{2,1,0:T(8,128)(2,1)S(1)}, u32[]{:S(2)}, u32[]{:S(2)}) collective-permute-start(bf16[1,64,512]{2,1,0:T(8,128)(2,1)S(1)} %get-tuple-element.46), channel_id=1, source_target_pairs={{0,16},{1,17},{2,18},{3,19},{16,0},{17,1},{18,2},{19,3},{4,20},{5,... | collective-permute-start | bytes 196616 | tf_op jit(solution)/shard_map/ppermute | solution.py:553

commit v3 on v2

v3 whole, which is shorter than its diff:
```python
import functools

import jax
import jax.numpy as jnp
from jax import lax
from jax.experimental import pallas as pl
from jax.experimental.pallas import tpu as pltpu
from jax.sharding import PartitionSpec as P

CONTRACT_LAST = (((1,), (1,)), ((), ()))
IN_VMEM = pl.BlockSpec(memory_space=pltpu.VMEM)
IN_SMEM = pl.BlockSpec(memory_space=pltpu.SMEM)
IN_HBM = pl.BlockSpec(memory_space=pltpu.HBM)
MIB = 1 << 20
LANES = 128
SPARE = 1


def params(mib):
    return pltpu.CompilerParams(vmem_limit_bytes=mib * MIB)


def cost(flops, moved):
    return pl.CostEstimate(flops=int(flops), bytes_accessed=int(moved), transcendentals=0)


def pinned(array):
    return pltpu.with_memory_space_constraint(array, pltpu.VMEM)


def in_hbm(array):
    return pltpu.with_memory_space_constraint(array, pltpu.HBM)


def shifted(block, axis, distance):
    count = lax.axis_size(axis)
    return lax.ppermute(block, axis, [((i - distance) % count, i) for i in range(count)])


def flipped(block, axis, bit):
    return lax.ppermute(block, axis, [(i, i ^ bit) for i in range(lax.axis_size(axis))])


def norm_kernel(ids, *refs):
    sources, (normed, sent), landed, semaphores = refs[:4], refs[4:6], refs[6:10], refs[10]
    copies = [
        pltpu.make_async_copy(source, target, semaphores.at[i])
        for i, (source, target) in enumerate(zip(sources, landed))
    ]
    for copy in copies:
        copy.start()
    for copy in copies:
        copy.wait()
    tokens, gain, routes, weights = landed
    widened = tokens[...].astype(jnp.float32)
    mean_square = jnp.mean(widened * widened, axis=-1, keepdims=True)
    rows = widened * lax.rsqrt(mean_square + 1e-06)
    rows = rows * gain[...].astype(jnp.float32).reshape(1, rows.shape[1])
    normed[...] = rows.astype(jnp.bfloat16)
    count, features = normed.shape
    pieces = sent.shape[0] // count
    start = pl.multiple_of(ids[0] * pieces * LANES, pieces * LANES)
    for i in range(pieces):
        at = pl.ds(pl.multiple_of(start + i * LANES, LANES), LANES)
        sent[i * count : (i + 1) * count] = normed[:, at]
    whole = weights[...]
    coarse = whole.astype(jnp.bfloat16).astype(jnp.float32)
    middle = (whole - coarse).astype(jnp.bfloat16).astype(jnp.float32)
    fine = whole - coarse - middle
    upper = jnp.concatenate([routes[...].astype(jnp.float32), coarse])
    lower = jnp.concatenate([middle, fine])
    sent[pieces * count :] = jnp.concatenate([upper, lower], axis=1).astype(jnp.bfloat16)


def normalize(ids, tokens, gain, routes, weights, width):
    count, features = tokens.shape
    top = routes.shape[0]
    operands = (tokens, gain, routes, weights)
    return pl.pallas_call(
        norm_kernel,
        out_shape=(
            jax.ShapeDtypeStruct((count, features), jnp.bfloat16),
            jax.ShapeDtypeStruct((count * width // LANES + 2 * top, LANES), jnp.bfloat16),
        ),
        in_specs=[IN_SMEM] + [IN_HBM] * 4,
        out_specs=(IN_VMEM, IN_VMEM),
        scratch_shapes=[pltpu.VMEM(x.shape, x.dtype) for x in operands]
        + [pltpu.SemaphoreType.DMA((4,))],
        compiler_params=params(5),
    )(ids, *(in_hbm(x) for x in operands))


def relay_kernel(block, after, result):
    result[...] = block[...]


def relayed(block, after):
    return pl.pallas_call(
        relay_kernel,
        out_shape=jax.ShapeDtypeStruct(block.shape, block.dtype),
        in_specs=[IN_VMEM, IN_VMEM],
        out_specs=IN_VMEM,
        compiler_params=params(5),
        cost_estimate=cost(0, MIB),
    )(block, after)


def collect_kernel(*refs):
    *blocks, staged, result = refs
    count = result.shape[0] // len(blocks)
    for i, block in enumerate(blocks):
        for j in range(result.shape[1] // LANES):
            result[i * count : (i + 1) * count, j * LANES : (j + 1) * LANES] = block[
                j * count : (j + 1) * count
            ]


def collect(blocks, count, width, staged):
    return pl.pallas_call(
        collect_kernel,
        out_shape=jax.ShapeDtypeStruct((len(blocks) * count, width), jnp.bfloat16),
        in_specs=[IN_VMEM] * (len(blocks) + 1),
        out_specs=IN_VMEM,
        compiler_params=params(5),
    )(*blocks, pinned(staged))


def write_plan(capacity, top, first_expert, blocks, placing, high, low):
    tokens, slots = high.shape[1:]
    count = len(blocks) * tokens
    lane = lax.broadcasted_iota(jnp.int32, (count, slots), 1)
    expert = (first_expert + lane // capacity).astype(jnp.float32)
    rank_of_lane = (lane % capacity).astype(jnp.float32)
    row = lax.broadcasted_iota(jnp.int32, (tokens, tokens), 0)
    column = lax.broadcasted_iota(jnp.int32, (tokens, tokens), 1)
    earlier = jnp.where(column < row, 1.0, 0.0).astype(jnp.bfloat16)
    sent = [block[block.shape[0] - 2 * top :].astype(jnp.float32) for block in blocks]
    upper = jnp.concatenate([part[:, :tokens] for part in sent], axis=1)
    lower = jnp.concatenate([part[:, LANES // 2 : LANES // 2 + tokens] for part in sent], axis=1)
    names = upper[:top]
    values = upper[top:] + lower[:top] + lower[top:]
    rest = jnp.zeros((LANES - 2 * top, count), jnp.float32)
    table = jnp.concatenate([names, values, rest]).T
    weight = jnp.zeros((count, slots), jnp.float32)
    for k in range(top):
        hit = table[:, k : k + 1] == expert
        weight = jnp.where(hit, table[:, top + k : top + k + 1], weight)
    named = jnp.where(weight > 0, 1.0, 0.0)
    for i in range(len(blocks)):
        own = slice(i * tokens, (i + 1) * tokens)
        ranks = jnp.dot(earlier, named[own].astype(jnp.bfloat16), preferred_element_type=jnp.float32)
        fits = (named[own] > 0) & (ranks == rank_of_lane[own])
        placing[i] = jnp.where(fits, 1.0, 0.0).T.astype(jnp.bfloat16)
        scaled = jnp.where(fits, weight[own], 0.0)
        coarse = scaled.astype(jnp.bfloat16)
        high[i] = coarse
        low[i] = (scaled - coarse.astype(jnp.float32)).astype(jnp.bfloat16)


def ring_place(store, kind, expert):
    _, places, _, _, _ = store.shape
    local_experts = places - SPARE
    return (kind * local_experts + expert) % places


def moves_of(store, moves):
    cut = []
    for when, kind, first, count, slot in moves:
        for expert in range(first, first + count):
            if expert > first and ring_place(store, kind, expert) > 0:
                cut[-1][3] += 1
            else:
                cut.append([when, kind, expert, 1, slot])
    return cut


def move(wide, tall, store, semaphore, place, kind, first, count, slot):
    experts = pl.ds(first, count)
    if kind == 2:
        source = tall.at[experts, pl.ds(2 * ((place >> 1) ^ slot), 2)]
    else:
        width = store.shape[-1]
        start = pl.multiple_of((place ^ (2 * kind + slot)) * width, width)
        source = wide.at[experts, :, :, pl.ds(start, width)]
    target = store.at[slot, pl.ds(ring_place(store, kind, first), count)]
    return pltpu.make_async_copy(source, target, semaphore)


def down_at(store, place, quarter, expert):
    return quarter // 2, ring_place(store, 2, expert), (quarter ^ place) & 1


def stage_kernel(ids, wide, tall, store, semaphores):
    count = store.shape[1] - SPARE
    copies = [
        move(wide, tall, store, semaphores.at[slot], ids[0], 0, 0, count, slot) for slot in range(2)
    ]
    for copy in copies:
        copy.start()
    for copy in copies:
        copy.wait()


def stage(ids, wide, tall, width):
    shape = (2, wide.shape[0] + SPARE) + wide.shape[1:-1] + (width,)
    return pl.pallas_call(
        stage_kernel,
        out_shape=pltpu.VMEM(shape, wide.dtype),
        in_specs=[IN_SMEM, IN_HBM, IN_HBM],
        out_specs=IN_VMEM,
        scratch_shapes=[pltpu.SemaphoreType.DMA((2,))],
        compiler_params=params(5),
        cost_estimate=cost(0, wide.size),
    )(ids, in_hbm(wide), in_hbm(tall))


def up_kernel(opts, ids, *refs):
    quarters, experts, total_first, finish, planned, moves = opts
    refs = list(refs)
    if planned:
        top, payloads = planned[0], [refs.pop(0) for _ in range(planned[1])]
    else:
        placing = refs.pop(0)
    normed = refs.pop(0)
    arrived = [refs.pop(0) for _ in quarters]
    total_in = refs.pop(0) if total_first is not None else None
    wide, tall, _, result, store = [refs.pop(0) for _ in range(5)]
    if planned:
        placing, high, low = [refs.pop(0) for _ in range(3)]
    gathered, rows, semaphores = refs
    blocks, slots, tokens = placing.shape
    _, places, _, hidden, width = store.shape
    capacity = slots // (places - SPARE)
    place = ids[0]
    copies = [
        move(wide, tall, store, semaphores.at[i], place, *what)
        for i, (_, *what) in enumerate(moves)
    ]
    for copy, (when, *_) in zip(copies, moves):
        if when is None:
            copy.start()
    if planned:
        write_plan(capacity, top, ids[1], payloads, placing, high, low)
    for i, quarter in enumerate(quarters):
        start = pl.multiple_of((place ^ quarter) * width, width)
        rows[0:tokens] = normed[:, pl.ds(start, width)]
        rows[tokens:] = arrived[i][...]
        for block in range(blocks):
            picked = jnp.dot(
                placing[block, experts[0] * capacity : experts[1] * capacity],
                rows[block * tokens : (block + 1) * tokens],
                preferred_element_type=jnp.float32,
            ).astype(jnp.bfloat16)
            at = slice(block * capacity, (block + 1) * capacity)
            gathered[i, :, at, :] = picked.reshape(experts[1] - experts[0], capacity, width)

    for expert in range(*experts):
        for copy, (when, *_) in zip(copies, moves):
            if when == expert:
                copy.start()
        value = total_in[expert - total_first] if total_in is not None else None
        for i, quarter in enumerate(quarters):
            part = lax.dot_general(
                gathered[i, expert - experts[0]],
                store[quarter % 2, ring_place(store, quarter // 2, expert)].reshape(2 * hidden, width),
                CONTRACT_LAST,
                preferred_element_type=jnp.float32,
            )
            value = part if value is None else value + part
        if finish:
            gate, up = value[:, :hidden], value[:, hidden:]
            value = (gate / (1.0 + jnp.exp(-gate)) * up).astype(jnp.bfloat16)
        result[expert - experts[0]] = value
    for copy in copies:
        copy.wait()


def up_step(ids, plan, normed, arrived, total, quarters, finish, experts, moves, wide, tall, store):
    _, places, _, hidden, width = store.shape
    moves = moves_of(store, moves)
    if isinstance(plan, dict):
        planned = (plan["top"], len(plan["payloads"]))
        blocks, slots, tokens = plan["shape"]
        operands = [ids] + list(plan["payloads"])
    else:
        planned = None
        blocks, slots, tokens = plan.shape
        operands = [ids, plan]
    depth = blocks * (slots // (places - SPARE))
    operands += [normed] + list(arrived)
    total_first = None
    if total is not None:
        total_first = total[1]
        operands.append(total[0])
    in_specs = [IN_SMEM] + [IN_VMEM] * (len(operands) - 1) + [IN_HBM, IN_HBM, IN_VMEM]
    operands += [in_hbm(wide), in_hbm(tall), pinned(store)]
    count = experts[1] - experts[0]
    if finish:
        shape = jax.ShapeDtypeStruct((count, depth, hidden), jnp.bfloat16)
    else:
        shape = jax.ShapeDtypeStruct((count, depth, 2 * hidden), jnp.float32)
    shapes = (shape, pltpu.VMEM(store.shape, store.dtype))
    if planned:
        shapes += (jax.ShapeDtypeStruct((blocks, slots, tokens), jnp.bfloat16),)
        shapes += (jax.ShapeDtypeStruct((blocks, tokens, slots), jnp.bfloat16),) * 2
    opts = (quarters, experts, total_first, finish, planned, moves)
    return pl.pallas_call(
        functools.partial(up_kernel, opts),
        out_shape=shapes,
        in_specs=in_specs,
        out_specs=(IN_VMEM,) * len(shapes),
        input_output_aliases={len(operands) - 1: 1},
        scratch_shapes=[
            pltpu.VMEM((len(quarters), count, depth, width), jnp.bfloat16),
            pltpu.VMEM((blocks * tokens, width), jnp.bfloat16),
            pltpu.SemaphoreType.DMA((len(moves),)),
        ],
        compiler_params=params(5),
        cost_estimate=cost(0, wide.size * len(quarters) * count // 8),
    )(*operands)


def down_kernel(groups, pieces, has_total, moves, ids, *refs):
    refs = list(refs)
    acts = [[refs.pop(0) for _ in group] for group in pieces]
    total_in = refs.pop(0) if has_total else None
    copies = []
    if moves:
        wide, tall, _, result, store, semaphores = refs
        for i, (_, *what) in enumerate(moves):
            copies.append(move(wide, tall, store, semaphores.at[i], ids[0], *what))
        for copy in copies:
            copy.start()
    else:
        store, result = refs
    for group, (low, high) in enumerate(groups):
        for expert in range(low, high):
            for copy, (when, *_) in zip(copies, moves):
                if when == expert:
                    copy.wait()
            value = total_in[expert] if has_total else None
            for act, q in zip(acts[group], pieces[group]):
                weights = store[down_at(store, ids[0], q, expert)]
                part = jnp.dot(act[expert - low], weights, preferred_element_type=jnp.float32)
                value = part if value is None else value + part
            result[expert] = value
    for copy, (when, *_) in zip(copies, moves):
        if when is None:
            copy.wait()


def down_step(ids, groups, acts, store, total, moves=(), wide=None, tall=None):
    pieces = [tuple(sorted(group)) for group in acts]
    local_experts, width = store.shape[1] - SPARE, store.shape[-1]
    moves = moves_of(store, moves)
    depth = acts[0][pieces[0][0]].shape[1]
    operands = [ids] + [group[q] for group, piece in zip(acts, pieces) for q in piece]
    in_specs = [IN_SMEM] + [IN_VMEM] * (len(operands) - 1)
    aliases, scratch = {}, []
    if total is not None:
        aliases = {len(operands): 0}
        operands.append(total)
        in_specs.append(IN_VMEM)
    shapes = (jax.ShapeDtypeStruct((local_experts, depth, width), jnp.float32),)
    if moves:
        operands += [in_hbm(wide), in_hbm(tall)]
        in_specs += [IN_HBM, IN_HBM]
        aliases[len(operands)] = 1
        shapes += (pltpu.VMEM(store.shape, store.dtype),)
        scratch = [pltpu.SemaphoreType.DMA((len(moves),))]
    operands.append(pinned(store))
    in_specs.append(IN_VMEM)
    return pl.pallas_call(
        functools.partial(down_kernel, groups, pieces, total is not None, moves),
        out_shape=shapes,
        in_specs=in_specs,
        out_specs=(IN_VMEM,) * len(shapes),
        input_output_aliases=aliases,
        scratch_shapes=scratch,
        compiler_params=params(5),
        cost_estimate=cost(0, 4 * MIB * len(acts)),
    )(*operands)


def finish_kernel(opts, ids, *refs):
    groups, quarter, part, parts = opts
    refs = list(refs)
    acts = [refs.pop(0) for _ in groups]
    store, total, high, low, tokens = [refs.pop(0) for _ in range(5)]
    kept, given, slots_out = refs
    local_experts, depth, whole = total.shape
    width = whole // parts
    lanes = slice(part * width, (part + 1) * width)
    blocks = high.shape[0]
    capacity = depth // blocks

    def place(expert, value):
        rounded = value.astype(jnp.bfloat16)
        at = slice(expert * capacity, (expert + 1) * capacity)
        for block in range(blocks):
            slots_out[block, at, :] = rounded[block * capacity : (block + 1) * capacity]

    for act, group in zip(acts, groups):
        for expert in range(*group):
            weights = store[*down_at(store, ids[0], quarter, expert), :, lanes]
            part_sum = jnp.dot(act[expert - group[0]], weights, preferred_element_type=jnp.float32)
            place(expert, total[expert, :, lanes] + part_sum)
    start = pl.multiple_of(ids[0] * whole + part * width, LANES)
    for block in range(blocks):
        value = jnp.dot(
            high[block], slots_out[block], preferred_element_type=jnp.float32
        ) + jnp.dot(low[block], slots_out[block], preferred_element_type=jnp.float32)
        if block == 0:
            value = value + tokens[:, pl.ds(start, width)].astype(jnp.float32)
        target = given if block % 2 else kept
        target[block // 2] = value.astype(jnp.bfloat16)


def finish_step(ids, groups, acts, quarter, store, total, high, low, tokens, part, parts):
    blocks, count, slots = high.shape
    width = total.shape[2] // parts
    operands = [ids] + list(acts)
    operands += [pinned(store), total, high, low, tokens]
    shape = jax.ShapeDtypeStruct((blocks // 2, count, width), jnp.bfloat16)
    return pl.pallas_call(
        functools.partial(finish_kernel, (groups, quarter, part, parts)),
        out_shape=(shape, shape),
        in_specs=[IN_SMEM] + [IN_VMEM] * (len(operands) - 1),
        out_specs=(IN_VMEM, IN_VMEM),
        scratch_shapes=[pltpu.VMEM((blocks, slots, width), jnp.bfloat16)],
        compiler_params=params(5),
        cost_estimate=cost(0, 0),
    )(*operands)


def add_kernel(own, other, *results):
    size = own.shape[0] // len(results)
    for i, result in enumerate(results):
        for j in range(size):
            value = own[j * len(results) + i].astype(jnp.float32)
            value = value + other[j * len(results) + i].astype(jnp.float32)
            result[j] = value.astype(jnp.bfloat16)


def add_up(own, other):
    count = own.shape[0]
    sides = min(2, count)
    shape = jax.ShapeDtypeStruct((count // sides,) + own.shape[1:], own.dtype)
    return pl.pallas_call(
        add_kernel,
        out_shape=(shape,) * sides,
        in_specs=[IN_VMEM, IN_VMEM],
        out_specs=(IN_VMEM,) * sides,
        compiler_params=params(5),
    )(own, other)


def sum_kernel(*refs):
    *parts, result = refs
    width = parts[0].shape[2]
    for i in range(result.shape[2] // width):
        value = parts[2 * i][0].astype(jnp.float32) + parts[2 * i + 1][0].astype(jnp.float32)
        result[0, :, i * width : (i + 1) * width] = value.astype(jnp.bfloat16)


def gathered_tokens(activations, routes, gate_weights, norm_gain, gate_up_weights, down_weights):
    tokens = activations[0]
    token_count, features = tokens.shape
    local_experts = gate_up_weights.shape[0]
    rows = lax.axis_size("expert")
    dp_devices = lax.axis_size("dp")
    sections = lax.axis_size("section")
    capacity = token_count * routes.shape[2] // (local_experts * rows)
    slots = local_experts * capacity
    width = features // dp_devices
    ids = jnp.stack([lax.axis_index("dp"), lax.axis_index("expert") * local_experts])
    ids = ids.astype(jnp.int32)

    normed, own = normalize(ids, tokens, norm_gain, routes[0].T, gate_weights[0].T, width)
    blocks = [flipped(own, "expert", j) for j in range(1, rows)]
    wide = gate_up_weights
    tall = down_weights.reshape(local_experts, dp_devices, -1, width)
    store = stage(ids, wide, tall, width)
    mine = collect(blocks, token_count, width, store)
    across = flipped(mine, "dp", 2)
    beside = flipped(mine, "dp", 1)
    cut = local_experts - 3 * local_experts // 8
    first, second = groups = ((0, cut), (cut, local_experts))

    end = local_experts
    moves = [(None, 1, 0, 1, slot) for slot in range(2)]
    moves += [(e, 1, e - 1, 2, slot) for e in range(2, end, 2) for slot in range(2)][:-1]
    payload = {
        "payloads": [own] + blocks,
        "top": routes.shape[2],
        "shape": (rows, slots, token_count),
    }

    total, store, placing, high, low = up_step(
        ids, payload, normed, [mine, beside], None, (0, 1), False, (0, local_experts),
        moves, wide, tall, store,
    )
    across = relayed(across, total)
    far = flipped(across, "dp", 1)

    step = functools.partial(up_step, ids, placing, normed)
    moves = [(None, 1, end - 3, 2, 1), (None, 1, end - 1, 1, 0), (None, 2, 0, 1, 0)]
    partial, store = step([across], (total, 0), (2,), False, first, moves, wide, tall, store)
    moves = [(None, 1, end - 1, 1, 1), (None, 2, 1, cut - 1, 0)]
    act, store = step([far], (partial, 0), (3,), True, first, moves, wide, tall, store)
    acts = [{0: act, 1: flipped(act, "dp", 1), 2: flipped(act, "dp", 2)}]
    moves = [(None, 2, cut, 1, 0), (None, 2, 0, cut - 1, 1)]
    moves += [(e, 2, e, 1, 0) for e in range(cut + 1, end - 1)]
    act, store = step(
        [across, far], (total, 0), (2, 3), True, second, moves, wide, tall, store
    )
    acts.append({0: act, 1: flipped(act, "dp", 1), 2: flipped(act, "dp", 2)})
    near = [{q: acts[0][q] for q in (0, 1)}, {0: acts[1][0]}]
    moves = [(end - 1, 2, end - 1, 1, 0), (None, 2, cut - 1, end - cut + 1, 1)]
    summed, store = down_step(ids, groups, near, store, None, moves, wide, tall)
    middle = relayed(acts[0][2], summed)
    last = relayed(acts[1][2], middle)
    far = [flipped(act, "dp", 1) for act in (middle, last)]
    pieces = [{2: middle}, {1: acts[1][1], 2: last}]
    (summed,) = down_step(ids, groups, pieces, store, summed)
    parts = 2
    received = []
    for part in range(parts):
        kept, given = finish_step(
            ids, groups, far, 3, store, summed, high, low, tokens, part, parts
        )
        near, given = add_up(kept, flipped(given, "expert", 1))
        for block, j in ((given, 2), (near, 0)):
            route = [
                (s * rows + e, ((s + 1) % sections) * rows + (e ^ j))
                for s in range(sections)
                for e in range(rows)
            ]
            received.append(lax.ppermute(block, ("section", "expert"), route))
    return pl.pallas_call(
        sum_kernel,
        out_shape=jax.ShapeDtypeStruct((1, token_count, width), jnp.bfloat16),
        in_specs=[IN_VMEM] * len(received),
        out_specs=IN_VMEM,
        compiler_params=params(5),
    )(*received)


def routed_rows(activations, routes, gate_weights, norm_gain, gate_up_weights, down_weights):
    tokens_here = activations[0]
    token_count, feature_count = tokens_here.shape
    top_count = routes.shape[2]
    local_experts = gate_up_weights.shape[0]
    expert_devices = lax.axis_size("expert")
    dp_devices = lax.axis_size("dp")
    total_experts = local_experts * expert_devices
    window = max(1, token_count * top_count // (total_experts * dp_devices))
    capacity = window * dp_devices
    slice_width = feature_count // dp_devices
    dp_place = lax.axis_index("dp")
    widened = tokens_here.astype(jnp.float32)
    mean_square = jnp.mean(widened * widened, axis=-1, keepdims=True)
    normed = (widened * lax.rsqrt(mean_square + 1e-06) * norm_gain.astype(jnp.float32)).astype(
        jnp.bfloat16
    )
    flat_routes = routes[0].reshape(-1)
    experts_iota = jnp.arange(total_experts, dtype=jnp.int32)
    onehot = (flat_routes[:, None] == experts_iota[None, :]).astype(jnp.int32)
    slot_ranks = jnp.sum((jnp.cumsum(onehot, axis=0) - onehot) * onehot, axis=1)
    targets = flat_routes * capacity + slot_ranks
    contract_rows = (((0,), (0,)), ((), ()))
    slot_iota = jnp.arange(total_experts * capacity, dtype=jnp.int32)
    matches = (targets[:, None] == slot_iota[None, :]).reshape(
        token_count, top_count, total_experts * capacity
    )
    placing = jnp.any(matches, axis=1).astype(jnp.bfloat16)
    normed_slice = lax.dynamic_slice_in_dim(normed, dp_place * slice_width, slice_width, 1)
    outgoing = lax.dot_general(
        placing, normed_slice, contract_rows, preferred_element_type=jnp.float32
    )
    outgoing = outgoing.astype(jnp.bfloat16).reshape(total_experts, capacity, slice_width)
    arriving = lax.all_to_all(outgoing, "expert", split_axis=0, concat_axis=0, tiled=True)
    arriving = arriving.reshape(expert_devices, local_experts, capacity, slice_width)
    weights_part = gate_up_weights
    gate_up = jnp.einsum(
        "seck,ejhk->jsech",
        lax.all_gather(arriving, "dp", axis=3, tiled=True),
        weights_part,
        preferred_element_type=jnp.float32,
    )
    hidden_act = (jax.nn.silu(gate_up[0]) * gate_up[1]).astype(jnp.bfloat16)
    weights_part = down_weights
    summed = jnp.einsum(
        "sech,ehf->secf",
        lax.all_gather(hidden_act, "dp", axis=3, tiled=True),
        weights_part,
        preferred_element_type=jnp.float32,
    )
    expert_out = summed.astype(jnp.bfloat16)
    returned = lax.all_to_all(expert_out, "expert", split_axis=0, concat_axis=0, tiled=True)
    returned_flat = returned.reshape(total_experts * capacity, slice_width)
    picked = jnp.take(returned_flat, targets, axis=0).reshape(token_count, top_count, slice_width)
    branch = jnp.sum(picked.astype(jnp.float32) * gate_weights[0][:, :, None], axis=1)
    residual = lax.dynamic_slice_in_dim(widened, dp_place * slice_width, slice_width, 1)
    finished = (residual + branch).astype(jnp.bfloat16)
    arrived = shifted(finished, "section", 1)
    return arrived[None]


def body(activations, routes, gate_weights, norm_gain, gate_up_weights, down_weights):
    token_count, top_count = routes.shape[1], routes.shape[2]
    local_experts = gate_up_weights.shape[0]
    rows = lax.axis_size("expert")
    capacity = token_count * top_count // (local_experts * rows)
    few = token_count <= local_experts * capacity and local_experts % 8 == 0
    aligned = capacity % 16 == 0 and token_count % 16 == 0
    suits = rows == 4 and lax.axis_size("dp") == 4 and token_count * 2 == LANES
    form = gathered_tokens if few and aligned and suits else routed_rows
    return form(
        activations, routes, gate_weights, norm_gain, gate_up_weights, down_weights
    )


def solution(mesh):
    placed = (
        P("section", "expert", None),
        P("section", "expert", None),
        P("section", "expert", None),
        P(),
        P("expert", None, "dp", None),
        P("expert", None, "dp"),
    )
    return jax.shard_map(
        body, mesh=mesh, in_specs=placed, out_specs=P("section", "expert", "dp"), check_vma=False
    )
```

time: 84.5 us -> 71.5 us (0.85)
  Pallas kernels: 50.1 us -> 42.4 us
  waiting for transfers between devices: 15 us -> 9.83 us
    pallas_call x8 -> x7, Pallas kernels: 40.9 us -> 33.4 us  [the longest x4 21.7 us: up_step(): pl.pallas_call(functools.partial(up_kernel, opts), out_shape=shapes, in_s...]
    ppermute x14, waiting for transfers between devices: 11 us -> 6.08 us  [flipped(): lax.ppermute(block, axis, [(i, i ^ bit) for i in range(lax.axis_size(axis...]
  transfers between devices with their start and end apart: 18 -> 18, of which waited for: 10 -> 8; matrix products, arithmetic and copies ran while one was open for 0% -> 0% of each run, Pallas kernels for 39% -> 48%
where the time goes in v3:
time: 71.5 us; the launch traced here: 71.4 us
  Pallas kernels  42.4 us (59%)
  starting transfers between devices  18.9 us (26%)
  waiting for transfers between devices  9.83 us (14%)
    pallas_call x4, Pallas kernels, up_step(): pl.pallas_call(functools.partial(up_kernel, opts), out_shape=shapes, in_s...  21.7 us
    ppermute x14, starting transfers between devices, flipped(): lax.ppermute(block, axis, [(i, i ^ bit) for i in range(lax.axis_size(axis...  12.9 us
    pallas_call x1, Pallas kernels, stage(): pl.pallas_call(stage_kernel, out_shape=pltpu.VMEM(shape, wide.dtype), in_...  8.73 us
    pallas_call x2, Pallas kernels, down_step(): pl.pallas_call(functools.partial(down_kernel, groups, pieces, total is no...  6.14 us
    ppermute x14, waiting for transfers between devices, flipped(): lax.ppermute(block, axis, [(i, i ^ bit) for i in range(lax.axis_size(axis...  6.08 us
    ppermute x4, starting transfers between devices, gathered_tokens(): received.append(lax.ppermute(block, ('section', 'expert'), route))  5.98 us
    ppermute x4, waiting for transfers between devices, gathered_tokens(): received.append(lax.ppermute(block, ('section', 'expert'), route))  3.75 us
    pallas_call x2, Pallas kernels, finish_step(): pl.pallas_call(functools.partial(finish_kernel, (groups, quarter, part, p...  3 us
  transfers between devices with their start and end apart: 18, of which 8 were waited for; matrix products, arithmetic and copies ran while one was open for 0% of the time, Pallas kernels for 48%

profile of v3, /device:TPU:0, one launch (start us, length us, event | category | flops | bytes accessed | tf_op | source)
XLA Modules:
  0.0 71.4 jit_solution(13593632906238589354)
XLA Ops:
  0.1 2.0 %shard_map.64 = (bf16[64,4096]{1,0:T(8,128)(2,1)S(1)}, bf16[528,128]{1,0:T(8,128)(2,1)S(1)}) custom-call(s32[2]{0:T(128)S(1)} %pad_add_fusion.ids, bf16[64,4096]{1,0:T(8,128)(2,1)} %bitcast.10, bf16[4096]{0:T(1024)(128)(2,1)} %refs_1_.1, s32[8,64]{1,0:T(8,128)} %bitcast.19, f32[8,64]{1,0:T(8,128)} %bitcast.20), custom_call_target="tpu_custom_call" | custom-call | tf_op jit(solution)/shard_map/pallas_call | solution.py:79
  2.0 5.1 %collective-permute-start.2 = (bf16[528,128]{1,0:T(8,128)(2,1)S(1)}, bf16[528,128]{1,0:T(8,128)(2,1)S(1)}, u32[]{:S(2)}, u32[]{:S(2)}) collective-permute-start(bf16[528,128]{1,0:T(8,128)(2,1)S(1)} %get-tuple-element.28.refs_0_), channel_id=1, source_target_pairs={{0,3},{1,2},{2,1},{3,0},{4,7},{5,6},{6,5},{7,4},{8,11},{9,10},{10,... | collective-permute-start | bytes 405512 | tf_op jit(solution)/shard_map/ppermute | solution.py:41
  7.2 0.6 collective-permute-start
  7.8 8.7 %shard_map.65.refs_3_.refs_9_ = bf16[2,9,2,384,1024]{4,3,2,1,0:T(8,128)(2,1)S(1)} custom-call(s32[2]{0:T(128)S(1)} %pad_add_fusion.ids, bf16[8,2,384,4096]{3,2,1,0:T(8,128)(2,1)} %refs_3_.1, bf16[8,4,384,1024]{3,2,1,0:T(8,128)(2,1)} %bitcast.13), custom_call_target="tpu_custom_call" | custom-call | bytes 25165824 | tf_op jit(solution)/shard_map/pallas_call | solution.py:206
  16.6 2.0 %collective-permute-done.1.refs_1_.refs_2_ = bf16[528,128]{1,0:T(8,128)(2,1)S(1)} collective-permute-done((bf16[528,128]{1,0:T(8,128)(2,1)S(1)}, bf16[528,128]{1,0:T(8,128)(2,1)S(1)}, u32[]{:S(2)}, u32[]{:S(2)}) %collective-permute-start.1) | collective-permute-done | bytes 135200 | tf_op jit(solution)/shard_map/ppermute | solution.py:41
  18.7 1.6 %collective-permute-start.4 = (bf16[192,1024]{1,0:T(8,128)(2,1)S(1)}, bf16[192,1024]{1,0:T(8,128)(2,1)S(1)}, u32[]{:S(2)}, u32[]{:S(2)}) collective-permute-start(bf16[192,1024]{1,0:T(8,128)(2,1)S(1)} %shard_map.66.refs_5_), channel_id=1, source_target_pairs={{0,8},{4,12},{8,0},{12,4},{1,9},{5,13},{9,1},{13,5},{2,10},{6,14},... | collective-permute-start | bytes 1179656 | tf_op jit(solution)/shard_map/ppermute | solution.py:41
  20.3 0.2 collective-permute-done.3.refs_6_
  20.5 9.8 %shard_map.67 = (f32[8,64,768]{2,1,0:T(8,128)S(1)}, bf16[2,9,2,384,1024]{4,3,2,1,0:T(8,128)(2,1)S(1)}, bf16[4,128,64]{2,1,0:T(8,128)(2,1)S(1)}, bf16[4,64,128]{2,1,0:T(8,128)(2,1)S(1)}, bf16[4,64,128]{2,1,0:T(8,128)(2,1)S(1)}) custom-call(s32[2]{0:T(128)S(1)} %pad_add_fusion.ids, ...), custom_call_target="tpu_custom_call", output_to_operand_aliasing={{1}: (10, {})} | custom-call | bytes 50331648 | tf_op jit(solution)/shard_map/pallas_call | solution.py:307
  30.3 0.2 collective-permute-start.5
  30.5 3.4 %shard_map.69 = (f32[5,64,768]{2,1,0:T(8,128)S(1)}, bf16[2,9,2,384,1024]{4,3,2,1,0:T(8,128)(2,1)S(1)}) custom-call(s32[2]{0:T(128)S(1)} %pad_add_fusion.ids, bf16[4,128,64]{2,1,0:T(8,128)(2,1)S(1)} %get-tuple-element.30.refs_0_, bf16[64,4096]{1,0:T(8,128)(2,1)S(1)} %get-tuple-element.29.refs_4_.refs_1_, ...), custom_call_target="tpu_custom_call", output_to_operand_aliasing={{1}: (7, {})} | custom-call | bytes 15728640 | tf_op jit(solution)/shard_map/pallas_call | solution.py:307
  34.0 3.9 %shard_map.70 = (bf16[5,64,384]{2,1,0:T(8,128)(2,1)S(1)}, bf16[2,9,2,384,1024]{4,3,2,1,0:T(8,128)(2,1)S(1)}) custom-call(s32[2]{0:T(128)S(1)} %pad_add_fusion.ids, bf16[4,128,64]{2,1,0:T(8,128)(2,1)S(1)} %get-tuple-element.30.refs_0_, bf16[64,4096]{1,0:T(8,128)(2,1)S(1)} %get-tuple-element.29.refs_4_.refs_1_, ...), custom_call_target="tpu_custom_call", output_to_operand_aliasing={{1}: (7, {})} | custom-call | bytes 15728640 | tf_op jit(solution)/shard_map/pallas_call | solution.py:307
  37.9 0.4 collective-permute-start.7
  38.3 1.5 %collective-permute-start.6 = (bf16[5,64,384]{2,1,0:T(8,128)(2,1)S(1)}, bf16[5,64,384]{2,1,0:T(8,128)(2,1)S(1)}, u32[]{:S(2)}, u32[]{:S(2)}) collective-permute-start(bf16[5,64,384]{2,1,0:T(8,128)(2,1)S(1)} %get-tuple-element.35.refs_0_), channel_id=1, source_target_pairs={{0,8},{4,12},{8,0},{12,4},{1,9},{5,13},{9,1},{13,5},{2,10},{6,14},... | collective-permute-start | bytes 737288 | tf_op jit(solution)/shard_map/ppermute | solution.py:41
  39.8 4.5 %shard_map.71 = (bf16[3,64,384]{2,1,0:T(8,128)(2,1)S(1)}, bf16[2,9,2,384,1024]{4,3,2,1,0:T(8,128)(2,1)S(1)}) custom-call(s32[2]{0:T(128)S(1)} %pad_add_fusion.ids, bf16[4,128,64]{2,1,0:T(8,128)(2,1)S(1)} %get-tuple-element.30.refs_0_, bf16[64,4096]{1,0:T(8,128)(2,1)S(1)} %get-tuple-element.29.refs_4_.refs_1_, ...), custom_call_target="tpu_custom_call", output_to_operand_aliasing={{1}: (8, {})} | custom-call | bytes 18874368 | tf_op jit(solution)/shard_map/pallas_call | solution.py:307
  44.3 0.6 collective-permute-start.9
  44.9 3.8 %shard_map.72 = (f32[8,64,1024]{2,1,0:T(8,128)S(1)}, bf16[2,9,2,384,1024]{4,3,2,1,0:T(8,128)(2,1)S(1)}) custom-call(s32[2]{0:T(128)S(1)} %pad_add_fusion.ids, bf16[5,64,384]{2,1,0:T(8,128)(2,1)S(1)} %get-tuple-element.35.refs_0_, bf16[5,64,384]{2,1,0:T(8,128)(2,1)S(1)} %collective-permute-done.7.refs_1_, ...), custom_call_target="tpu_custom_call", output_to_operand_aliasing={{1}: (6, {})} | custom-call | bytes 8388608 | tf_op jit(solution)/shard_map/pallas_call | solution.py:373
  48.9 0.5 collective-permute-start.11
  49.4 0.6 collective-permute-done.9.block
  50.1 0.5 collective-permute-done.11.refs_1_
  50.6 2.3 %shard_map.75.refs_3_ = f32[8,64,1024]{2,1,0:T(8,128)S(1)} custom-call(s32[2]{0:T(128)S(1)} %pad_add_fusion.ids, bf16[5,64,384]{2,1,0:T(8,128)(2,1)S(1)} %shard_map.73.after.refs_0_, bf16[3,64,384]{2,1,0:T(8,128)(2,1)S(1)} %collective-permute-done.11.refs_1_, bf16[3,64,384]{2,1,0:T(8,128)(2,1)S(1)} %shard_map.74.refs_2_, ...), custom_call_target="tpu_custom_call", output_to_operand_aliasing={{}: (4, {})} | custom-call | bytes 8388608 | tf_op jit(solution)/shard_map/pallas_call | solution.py:373
  53.0 1.5 %shard_map.78 = (bf16[2,64,512]{2,1,0:T(8,128)(2,1)S(1)}, bf16[2,64,512]{2,1,0:T(8,128)(2,1)S(1)}) custom-call(s32[2]{0:T(128)S(1)} %pad_add_fusion.ids, bf16[5,64,384]{2,1,0:T(8,128)(2,1)S(1)} %collective-permute-done.8.refs_0_, bf16[3,64,384]{2,1,0:T(8,128)(2,1)S(1)} %collective-permute-done.10.refs_1_, ...), custom_call_target="tpu_custom_call" | custom-call | tf_op jit(solution)/shard_map/pallas_call | solution.py:425
  54.6 1.5 %shard_map.76 = (bf16[2,64,512]{2,1,0:T(8,128)(2,1)S(1)}, bf16[2,64,512]{2,1,0:T(8,128)(2,1)S(1)}) custom-call(s32[2]{0:T(128)S(1)} %pad_add_fusion.ids, bf16[5,64,384]{2,1,0:T(8,128)(2,1)S(1)} %collective-permute-done.8.refs_0_, bf16[3,64,384]{2,1,0:T(8,128)(2,1)S(1)} %collective-permute-done.10.refs_1_, ...), custom_call_target="tpu_custom_call" | custom-call | tf_op jit(solution)/shard_map/pallas_call | solution.py:425
  56.1 2.1 %collective-permute-start.12 = (bf16[2,64,512]{2,1,0:T(8,128)(2,1)S(1)}, bf16[2,64,512]{2,1,0:T(8,128)(2,1)S(1)}, u32[]{:S(2)}, u32[]{:S(2)}) collective-permute-start(bf16[2,64,512]{2,1,0:T(8,128)(2,1)S(1)} %get-tuple-element.44), channel_id=1, source_target_pairs={{0,1},{1,0},{2,3},{3,2},{4,5},{5,4},{6,7},{7,6},{8,9},{9,8},{10,11... | collective-permute-start | bytes 393224 | tf_op jit(solution)/shard_map/ppermute | solution.py:41
  58.2 2.7 %collective-permute-done.15.other = bf16[2,64,512]{2,1,0:T(8,128)(2,1)S(1)} collective-permute-done((bf16[2,64,512]{2,1,0:T(8,128)(2,1)S(1)}, bf16[2,64,512]{2,1,0:T(8,128)(2,1)S(1)}, u32[]{:S(2)}, u32[]{:S(2)}) %collective-permute-start.15) | collective-permute-done | bytes 131104 | tf_op jit(solution)/shard_map/ppermute | solution.py:41
  60.9 1.6 %collective-permute-start.16 = (bf16[1,64,512]{2,1,0:T(8,128)(2,1)S(1)}, bf16[1,64,512]{2,1,0:T(8,128)(2,1)S(1)}, u32[]{:S(2)}, u32[]{:S(2)}) collective-permute-start(bf16[1,64,512]{2,1,0:T(8,128)(2,1)S(1)} %get-tuple-element.49), channel_id=1, source_target_pairs={{0,18},{1,19},{2,16},{3,17},{16,2},{17,3},{18,0},{19,1},{4,22},{5,... | collective-permute-start | bytes 196616 | tf_op jit(solution)/shard_map/ppermute | solution.py:539
  62.5 0.5 collective-permute-start.17
  63.1 3.4 %collective-permute-start.13 = (bf16[1,64,512]{2,1,0:T(8,128)(2,1)S(1)}, bf16[1,64,512]{2,1,0:T(8,128)(2,1)S(1)}, u32[]{:S(2)}, u32[]{:S(2)}) collective-permute-start(bf16[1,64,512]{2,1,0:T(8,128)(2,1)S(1)} %get-tuple-element.45), channel_id=1, source_target_pairs={{0,18},{1,19},{2,16},{3,17},{16,2},{17,3},{18,0},{19,1},{4,22},{5,... | collective-permute-start | bytes 196616 | tf_op jit(solution)/shard_map/ppermute | solution.py:539
  66.4 0.5 collective-permute-start.14
  66.9 1.9 %collective-permute-done.16.refs_2_ = bf16[1,64,512]{2,1,0:T(8,128)(2,1)S(1)} collective-permute-done((bf16[1,64,512]{2,1,0:T(8,128)(2,1)S(1)}, bf16[1,64,512]{2,1,0:T(8,128)(2,1)S(1)}, u32[]{:S(2)}, u32[]{:S(2)}) %collective-permute-start.16) | collective-permute-done | bytes 65568 | tf_op jit(solution)/shard_map/ppermute | solution.py:539
  68.8 0.8 %collective-permute-done.13.refs_0_ = bf16[1,64,512]{2,1,0:T(8,128)(2,1)S(1)} collective-permute-done((bf16[1,64,512]{2,1,0:T(8,128)(2,1)S(1)}, bf16[1,64,512]{2,1,0:T(8,128)(2,1)S(1)}, u32[]{:S(2)}, u32[]{:S(2)}) %collective-permute-start.13) | collective-permute-done | bytes 65568 | tf_op jit(solution)/shard_map/ppermute | solution.py:539
  69.6 1.1 %collective-permute-done.14.refs_1_ = bf16[1,64,512]{2,1,0:T(8,128)(2,1)S(1)} collective-permute-done((bf16[1,64,512]{2,1,0:T(8,128)(2,1)S(1)}, bf16[1,64,512]{2,1,0:T(8,128)(2,1)S(1)}, u32[]{:S(2)}, u32[]{:S(2)}) %collective-permute-start.14) | collective-permute-done | bytes 65568 | tf_op jit(solution)/shard_map/ppermute | solution.py:539
  70.7 0.7 shard_map.80
  (24 shorter events, 0.6 us)
Async XLA Ops:
  2.0 14.5 %collective-permute-start.2 = (bf16[528,128]{1,0:T(8,128)(2,1)S(1)}, bf16[528,128]{1,0:T(8,128)(2,1)S(1)}, u32[]{:S(2)}, u32[]{:S(2)}) collective-permute-start(bf16[528,128]{1,0:T(8,128)(2,1)S(1)} %get-tuple-element.28.refs_0_), channel_id=1, source_target_pairs={{0,3},{1,2},{2,1},{3,0},{4,7},{5,6},{6,5},{7,4},{8,11},{9,10},{10,... | collective-permute-start | bytes 405512 | tf_op jit(solution)/shard_map/ppermute | solution.py:41
  7.2 11.4 %collective-permute-start.1 = (bf16[528,128]{1,0:T(8,128)(2,1)S(1)}, bf16[528,128]{1,0:T(8,128)(2,1)S(1)}, u32[]{:S(2)}, u32[]{:S(2)}) collective-permute-start(bf16[528,128]{1,0:T(8,128)(2,1)S(1)} %get-tuple-element.28.refs_0_), channel_id=1, source_target_pairs={{0,2},{1,3},{2,0},{3,1},{4,6},{5,7},{6,4},{7,5},{8,10},{9,11},{10,... | collective-permute-start | bytes 405512 | tf_op jit(solution)/shard_map/ppermute | solution.py:41
  7.2 11.4 %collective-permute-start = (bf16[528,128]{1,0:T(8,128)(2,1)S(1)}, bf16[528,128]{1,0:T(8,128)(2,1)S(1)}, u32[]{:S(2)}, u32[]{:S(2)}) collective-permute-start(bf16[528,128]{1,0:T(8,128)(2,1)S(1)} %get-tuple-element.28.refs_0_), channel_id=1, source_target_pairs={{0,1},{1,0},{2,3},{3,2},{4,5},{5,4},{6,7},{7,6},{8,9},{9,8},{10,11... | collective-permute-start | bytes 405512 | tf_op jit(solution)/shard_map/ppermute | solution.py:41
  18.7 1.8 %collective-permute-start.3 = (bf16[192,1024]{1,0:T(8,128)(2,1)S(1)}, bf16[192,1024]{1,0:T(8,128)(2,1)S(1)}, u32[]{:S(2)}, u32[]{:S(2)}) collective-permute-start(bf16[192,1024]{1,0:T(8,128)(2,1)S(1)} %shard_map.66.refs_5_), channel_id=1, source_target_pairs={{0,4},{4,0},{8,12},{12,8},{1,5},{5,1},{9,13},{13,9},{2,6},{6,2},{1... | collective-permute-start | bytes 1179656 | tf_op jit(solution)/shard_map/ppermute | solution.py:41
  18.7 11.5 %collective-permute-start.4 = (bf16[192,1024]{1,0:T(8,128)(2,1)S(1)}, bf16[192,1024]{1,0:T(8,128)(2,1)S(1)}, u32[]{:S(2)}, u32[]{:S(2)}) collective-permute-start(bf16[192,1024]{1,0:T(8,128)(2,1)S(1)} %shard_map.66.refs_5_), channel_id=1, source_target_pairs={{0,8},{4,12},{8,0},{12,4},{1,9},{5,13},{9,1},{13,5},{2,10},{6,14},... | collective-permute-start | bytes 1179656 | tf_op jit(solution)/shard_map/ppermute | solution.py:41
  30.3 3.6 %collective-permute-start.5 = (bf16[192,1024]{1,0:T(8,128)(2,1)S(1)}, bf16[192,1024]{1,0:T(8,128)(2,1)S(1)}, u32[]{:S(2)}, u32[]{:S(2)}) collective-permute-start(bf16[192,1024]{1,0:T(8,128)(2,1)S(1)} %shard_map.68.refs_2_), channel_id=1, source_target_pairs={{0,4},{4,0},{8,12},{12,8},{1,5},{5,1},{9,13},{13,9},{2,6},{6,2},{1... | collective-permute-start | bytes 1179656 | tf_op jit(solution)/shard_map/ppermute | solution.py:41
  37.9 7.1 %collective-permute-start.7 = (bf16[5,64,384]{2,1,0:T(8,128)(2,1)S(1)}, bf16[5,64,384]{2,1,0:T(8,128)(2,1)S(1)}, u32[]{:S(2)}, u32[]{:S(2)}) collective-permute-start(bf16[5,64,384]{2,1,0:T(8,128)(2,1)S(1)} %get-tuple-element.35.refs_0_), channel_id=1, source_target_pairs={{0,4},{4,0},{8,12},{12,8},{1,5},{5,1},{9,13},{13,9},{2,6},{6,2},{1... | collective-permute-start | bytes 737288 | tf_op jit(solution)/shard_map/ppermute | solution.py:41
  38.3 10.5 %collective-permute-start.6 = (bf16[5,64,384]{2,1,0:T(8,128)(2,1)S(1)}, bf16[5,64,384]{2,1,0:T(8,128)(2,1)S(1)}, u32[]{:S(2)}, u32[]{:S(2)}) collective-permute-start(bf16[5,64,384]{2,1,0:T(8,128)(2,1)S(1)} %get-tuple-element.35.refs_0_), channel_id=1, source_target_pairs={{0,8},{4,12},{8,0},{12,4},{1,9},{5,13},{9,1},{13,5},{2,10},{6,14},... | collective-permute-start | bytes 737288 | tf_op jit(solution)/shard_map/ppermute | solution.py:41
  44.3 5.7 %collective-permute-start.9 = (bf16[3,64,384]{2,1,0:T(8,128)(2,1)S(1)}, bf16[3,64,384]{2,1,0:T(8,128)(2,1)S(1)}, u32[]{:S(2)}, u32[]{:S(2)}) collective-permute-start(bf16[3,64,384]{2,1,0:T(8,128)(2,1)S(1)} %get-tuple-element.37.refs_2_), channel_id=1, source_target_pairs={{0,8},{4,12},{8,0},{12,4},{1,9},{5,13},{9,1},{13,5},{2,10},{6,14},... | collective-permute-start | bytes 442376 | tf_op jit(solution)/shard_map/ppermute | solution.py:41
  48.8 4.2 %copy-start = (bf16[1,64,4096]{2,1,0:T(8,128)(2,1)S(1)}, bf16[1,64,4096]{2,1,0:T(8,128)(2,1)}, u32[]{:S(2)}) copy-start(bf16[1,64,4096]{2,1,0:T(8,128)(2,1)} %param.6) | copy-start | bytes 1572868
  48.8 4.1 %collective-permute-start.8 = (bf16[5,64,384]{2,1,0:T(8,128)(2,1)S(1)}, bf16[5,64,384]{2,1,0:T(8,128)(2,1)S(1)}, u32[]{:S(2)}, u32[]{:S(2)}) collective-permute-start(bf16[5,64,384]{2,1,0:T(8,128)(2,1)S(1)} %shard_map.73.after.refs_0_), channel_id=1, source_target_pairs={{0,4},{4,0},{8,12},{12,8},{1,5},{5,1},{9,13},{13,9},{2,6},{6,2},{1... | collective-permute-start | bytes 737288 | tf_op jit(solution)/shard_map/ppermute | solution.py:41
  48.9 1.7 %collective-permute-start.11 = (bf16[3,64,384]{2,1,0:T(8,128)(2,1)S(1)}, bf16[3,64,384]{2,1,0:T(8,128)(2,1)S(1)}, u32[]{:S(2)}, u32[]{:S(2)}) collective-permute-start(bf16[3,64,384]{2,1,0:T(8,128)(2,1)S(1)} %get-tuple-element.37.refs_2_), channel_id=1, source_target_pairs={{0,4},{4,0},{8,12},{12,8},{1,5},{5,1},{9,13},{13,9},{2,6},{6,2},{1... | collective-permute-start | bytes 442376 | tf_op jit(solution)/shard_map/ppermute | solution.py:41
  50.0 2.9 %collective-permute-start.10 = (bf16[3,64,384]{2,1,0:T(8,128)(2,1)S(1)}, bf16[3,64,384]{2,1,0:T(8,128)(2,1)S(1)}, u32[]{:S(2)}, u32[]{:S(2)}) collective-permute-start(bf16[3,64,384]{2,1,0:T(8,128)(2,1)S(1)} %shard_map.74.refs_2_), channel_id=1, source_target_pairs={{0,4},{4,0},{8,12},{12,8},{1,5},{5,1},{9,13},{13,9},{2,6},{6,2},{1... | collective-permute-start | bytes 442376 | tf_op jit(solution)/shard_map/ppermute | solution.py:41
  54.5 6.4 %collective-permute-start.15 = (bf16[2,64,512]{2,1,0:T(8,128)(2,1)S(1)}, bf16[2,64,512]{2,1,0:T(8,128)(2,1)S(1)}, u32[]{:S(2)}, u32[]{:S(2)}) collective-permute-start(bf16[2,64,512]{2,1,0:T(8,128)(2,1)S(1)} %get-tuple-element.48), channel_id=1, source_target_pairs={{0,1},{1,0},{2,3},{3,2},{4,5},{5,4},{6,7},{7,6},{8,9},{9,8},{10,11... | collective-permute-start | bytes 393224 | tf_op jit(solution)/shard_map/ppermute | solution.py:41
  56.1 7.0 %collective-permute-start.12 = (bf16[2,64,512]{2,1,0:T(8,128)(2,1)S(1)}, bf16[2,64,512]{2,1,0:T(8,128)(2,1)S(1)}, u32[]{:S(2)}, u32[]{:S(2)}) collective-permute-start(bf16[2,64,512]{2,1,0:T(8,128)(2,1)S(1)} %get-tuple-element.44), channel_id=1, source_target_pairs={{0,1},{1,0},{2,3},{3,2},{4,5},{5,4},{6,7},{7,6},{8,9},{9,8},{10,11... | collective-permute-start | bytes 393224 | tf_op jit(solution)/shard_map/ppermute | solution.py:41
  60.9 7.9 %collective-permute-start.16 = (bf16[1,64,512]{2,1,0:T(8,128)(2,1)S(1)}, bf16[1,64,512]{2,1,0:T(8,128)(2,1)S(1)}, u32[]{:S(2)}, u32[]{:S(2)}) collective-permute-start(bf16[1,64,512]{2,1,0:T(8,128)(2,1)S(1)} %get-tuple-element.49), channel_id=1, source_target_pairs={{0,18},{1,19},{2,16},{3,17},{16,2},{17,3},{18,0},{19,1},{4,22},{5,... | collective-permute-start | bytes 196616 | tf_op jit(solution)/shard_map/ppermute | solution.py:539
  62.5 6.3 %collective-permute-start.17 = (bf16[1,64,512]{2,1,0:T(8,128)(2,1)S(1)}, bf16[1,64,512]{2,1,0:T(8,128)(2,1)S(1)}, u32[]{:S(2)}, u32[]{:S(2)}) collective-permute-start(bf16[1,64,512]{2,1,0:T(8,128)(2,1)S(1)} %get-tuple-element.50), channel_id=1, source_target_pairs={{0,16},{1,17},{2,18},{3,19},{16,0},{17,1},{18,2},{19,3},{4,20},{5,... | collective-permute-start | bytes 196616 | tf_op jit(solution)/shard_map/ppermute | solution.py:539
  63.1 6.5 %collective-permute-start.13 = (bf16[1,64,512]{2,1,0:T(8,128)(2,1)S(1)}, bf16[1,64,512]{2,1,0:T(8,128)(2,1)S(1)}, u32[]{:S(2)}, u32[]{:S(2)}) collective-permute-start(bf16[1,64,512]{2,1,0:T(8,128)(2,1)S(1)} %get-tuple-element.45), channel_id=1, source_target_pairs={{0,18},{1,19},{2,16},{3,17},{16,2},{17,3},{18,0},{19,1},{4,22},{5,... | collective-permute-start | bytes 196616 | tf_op jit(solution)/shard_map/ppermute | solution.py:539
  66.4 4.3 %collective-permute-start.14 = (bf16[1,64,512]{2,1,0:T(8,128)(2,1)S(1)}, bf16[1,64,512]{2,1,0:T(8,128)(2,1)S(1)}, u32[]{:S(2)}, u32[]{:S(2)}) collective-permute-start(bf16[1,64,512]{2,1,0:T(8,128)(2,1)S(1)} %get-tuple-element.46), channel_id=1, source_target_pairs={{0,16},{1,17},{2,18},{3,19},{16,0},{17,1},{18,2},{19,3},{4,20},{5,... | collective-permute-start | bytes 196616 | tf_op jit(solution)/shard_map/ppermute | solution.py:539

commit v4 on v3

--- a/solution.py
+++ b/solution.py
@@ -383,84 +383,52 @@
 
 
 def finish_kernel(opts, ids, *refs):
-    groups, quarter, part, parts = opts
+    groups, quarter = opts
     refs = list(refs)
     acts = [refs.pop(0) for _ in groups]
     store, total, high, low, tokens = [refs.pop(0) for _ in range(5)]
-    kept, given, slots_out = refs
+    *results, slots_out = refs
     local_experts, depth, whole = total.shape
-    width = whole // parts
-    lanes = slice(part * width, (part + 1) * width)
     blocks = high.shape[0]
     capacity = depth // blocks
-
-    def place(expert, value):
-        rounded = value.astype(jnp.bfloat16)
-        at = slice(expert * capacity, (expert + 1) * capacity)
-        for block in range(blocks):
-            slots_out[block, at, :] = rounded[block * capacity : (block + 1) * capacity]
-
     for act, group in zip(acts, groups):
         for expert in range(*group):
-            weights = store[*down_at(store, ids[0], quarter, expert), :, lanes]
-            part_sum = jnp.dot(act[expert - group[0]], weights, preferred_element_type=jnp.float32)
-            place(expert, total[expert, :, lanes] + part_sum)
-    start = pl.multiple_of(ids[0] * whole + part * width, LANES)
+            weights = store[down_at(store, ids[0], quarter, expert)]
+            value = jnp.dot(act[expert - group[0]], weights, preferred_element_type=jnp.float32)
+            value = (value + total[expert]).astype(jnp.bfloat16)
+            own = slice(expert * capacity, (expert + 1) * capacity)
+            for block in range(blocks):
+                slots_out[block, own, :] = value[block * capacity : (block + 1) * capacity]
+    start = pl.multiple_of(ids[0] * whole, LANES)
     for block in range(blocks):
         value = jnp.dot(
             high[block], slots_out[block], preferred_element_type=jnp.float32
         ) + jnp.dot(low[block], slots_out[block], preferred_element_type=jnp.float32)
         if block == 0:
-            value = value + tokens[:, pl.ds(start, width)].astype(jnp.float32)
-        target = given if block % 2 else kept
-        target[block // 2] = value.astype(jnp.bfloat16)
-
-
-def finish_step(ids, groups, acts, quarter, store, total, high, low, tokens, part, parts):
+            value = value + tokens[:, pl.ds(start, whole)].astype(jnp.float32)
+        results[block][...] = value.astype(jnp.bfloat16)
+
+
+def finish_step(ids, groups, acts, quarter, store, total, high, low, tokens):
     blocks, count, slots = high.shape
-    width = total.shape[2] // parts
+    whole = total.shape[2]
     operands = [ids] + list(acts)
     operands += [pinned(store), total, high, low, tokens]
-    shape = jax.ShapeDtypeStruct((blocks // 2, count, width), jnp.bfloat16)
-    return pl.pallas_call(
-        functools.partial(finish_kernel, (groups, quarter, part, parts)),
-        out_shape=(shape, shape),
+    shape = jax.ShapeDtypeStruct((count, whole), jnp.bfloat16)
+    return pl.pallas_call(
+        functools.partial(finish_kernel, (groups, quarter)),
+        out_shape=(shape,) * blocks,
         in_specs=[IN_SMEM] + [IN_VMEM] * (len(operands) - 1),
-        out_specs=(IN_VMEM, IN_VMEM),
-        scratch_shapes=[pltpu.VMEM((blocks, slots, width), jnp.bfloat16)],
+        out_specs=(IN_VMEM,) * blocks,
+        scratch_shapes=[pltpu.VMEM((blocks, slots, whole), jnp.bfloat16)],
         compiler_params=params(5),
         cost_estimate=cost(0, 0),
     )(*operands)
 
 
-def add_kernel(own, other, *results):
-    size = own.shape[0] // len(results)
-    for i, result in enumerate(results):
-        for j in range(size):
-            value = own[j * len(results) + i].astype(jnp.float32)
-            value = value + other[j * len(results) + i].astype(jnp.float32)
-            result[j] = value.astype(jnp.bfloat16)
-
-
-def add_up(own, other):
-    count = own.shape[0]
-    sides = min(2, count)
-    shape = jax.ShapeDtypeStruct((count // sides,) + own.shape[1:], own.dtype)
-    return pl.pallas_call(
-        add_kernel,
-        out_shape=(shape,) * sides,
-        in_specs=[IN_VMEM, IN_VMEM],
-        out_specs=(IN_VMEM,) * sides,
-        compiler_params=params(5),
-    )(own, other)
-
-
 def sum_kernel(*refs):
     *parts, result = refs
-    width = parts[0].shape[2]
-    for i in range(result.shape[2] // width):
-        value = parts[2 * i][0].astype(jnp.float32) + parts[2 * i + 1][0].astype(jnp.float32)
-        result[0, :, i * width : (i + 1) * width] = value.astype(jnp.bfloat16)
+    result[0] = sum(part[...].astype(jnp.float32) for part in parts).astype(jnp.bfloat16)
 
 
 def gathered_tokens(activations, routes, gate_weights, norm_gain, gate_up_weights, down_weights):
@@ -515,28 +483,23 @@
         [across, far], (total, 0), (2, 3), True, second, moves, wide, tall, store
     )
     acts.append({0: act, 1: flipped(act, "dp", 1), 2: flipped(act, "dp", 2)})
-    near = [{q: acts[0][q] for q in (0, 1)}, {0: acts[1][0]}]
-    moves = [(end - 1, 2, end - 1, 1, 0), (None, 2, cut - 1, end - cut + 1, 1)]
+    near = [acts[0], {0: acts[1][0]}]
+    moves = [(cut - 1, 2, cut - 1, 1, 1), (end - 1, 2, end - 1, 1, 0)]
+    moves.append((None, 2, cut, end - cut, 1))
     summed, store = down_step(ids, groups, near, store, None, moves, wide, tall)
-    middle = relayed(acts[0][2], summed)
-    last = relayed(acts[1][2], middle)
-    far = [flipped(act, "dp", 1) for act in (middle, last)]
-    pieces = [{2: middle}, {1: acts[1][1], 2: last}]
-    (summed,) = down_step(ids, groups, pieces, store, summed)
-    parts = 2
+    last = relayed(acts[1][2], summed)
+    far = [flipped(act, "dp", 1) for act in (acts[0][2], last)]
+    pieces = [{1: acts[1][1], 2: last}]
+    (summed,) = down_step(ids, (second,), pieces, store, summed)
+    sums = finish_step(ids, groups, far, 3, store, summed, high, low, tokens)
     received = []
-    for part in range(parts):
-        kept, given = finish_step(
-            ids, groups, far, 3, store, summed, high, low, tokens, part, parts
-        )
-        near, given = add_up(kept, flipped(given, "expert", 1))
-        for block, j in ((given, 2), (near, 0)):
-            route = [
-                (s * rows + e, ((s + 1) % sections) * rows + (e ^ j))
-                for s in range(sections)
-                for e in range(rows)
-            ]
-            received.append(lax.ppermute(block, ("section", "expert"), route))
+    for j in range(rows):
+        route = [
+            (s * rows + e, ((s + 1) % sections) * rows + (e ^ j))
+            for s in range(sections)
+            for e in range(rows)
+        ]
+        received.append(lax.ppermute(sums[j], ("section", "expert"), route))
     return pl.pallas_call(
         sum_kernel,
         out_shape=jax.ShapeDtypeStruct((1, token_count, width), jnp.bfloat16),

time: 71.5 us -> 70.9 us (level)
  waiting for transfers between devices: 9.83 us -> 12.4 us
  starting transfers between devices: 18.9 us -> 17.2 us
  Pallas kernels: 42.4 us -> 40.8 us
    ppermute x4, waiting for transfers between devices: 3.75 us -> 8.69 us  [gathered_tokens(): received.append(lax.ppermute(sums[j], ('section', 'expert'), route))]
    ppermute x14 -> x12, starting transfers between devices: 12.9 us -> 10.4 us  [flipped(): lax.ppermute(block, axis, [(i, i ^ bit) for i in range(lax.axis_size(axis...]
    ppermute x14 -> x12, waiting for transfers between devices: 6.08 us -> 3.73 us  [flipped(): lax.ppermute(block, axis, [(i, i ^ bit) for i in range(lax.axis_size(axis...]
    pallas_call x4 -> x1, Pallas kernels: 3.07 us -> 2.2 us  [finish_step(): pl.pallas_call(functools.partial(finish_kernel, (groups, quarter)), out_s...]
    ppermute x4, starting transfers between devices: 5.98 us -> 6.81 us  [gathered_tokens(): received.append(lax.ppermute(sums[j], ('section', 'expert'), route))]
    pallas_call x2, Pallas kernels: 6.14 us -> 5.4 us  [down_step(): pl.pallas_call(functools.partial(down_kernel, groups, pieces, total is no...]
  transfers between devices with their start and end apart: 18 -> 16, of which waited for: 8 -> 5; matrix products, arithmetic and copies ran while one was open for 0% -> 0% of each run, Pallas kernels for 48% -> 45%
where the time goes in v4:
time: 70.9 us; the launch traced here: 70.7 us
  Pallas kernels  40.8 us (58%)
  starting transfers between devices  17.2 us (24%)
  waiting for transfers between devices  12.4 us (17%)
    pallas_call x4, Pallas kernels, up_step(): pl.pallas_call(functools.partial(up_kernel, opts), out_shape=shapes, in_s...  21.7 us
    ppermute x12, starting transfers between devices, flipped(): lax.ppermute(block, axis, [(i, i ^ bit) for i in range(lax.axis_size(axis...  10.4 us
    pallas_call x1, Pallas kernels, stage(): pl.pallas_call(stage_kernel, out_shape=pltpu.VMEM(shape, wide.dtype), in_...  8.73 us
    ppermute x4, waiting for transfers between devices, gathered_tokens(): received.append(lax.ppermute(sums[j], ('section', 'expert'), route))  8.69 us
    ppermute x4, starting transfers between devices, gathered_tokens(): received.append(lax.ppermute(sums[j], ('section', 'expert'), route))  6.81 us
    pallas_call x2, Pallas kernels, down_step(): pl.pallas_call(functools.partial(down_kernel, groups, pieces, total is no...  5.4 us
    ppermute x12, waiting for transfers between devices, flipped(): lax.ppermute(block, axis, [(i, i ^ bit) for i in range(lax.axis_size(axis...  3.73 us
    pallas_call x1, Pallas kernels, finish_step(): pl.pallas_call(functools.partial(finish_kernel, (groups, quarter)), out_s...  2.2 us
  transfers between devices with their start and end apart: 16, of which 5 were waited for; matrix products, arithmetic and copies ran while one was open for 0% of the time, Pallas kernels for 45%

profile of v4, /device:TPU:0, one launch (start us, length us, event | category | flops | bytes accessed | tf_op | source)
XLA Modules:
  0.0 70.7 jit_solution(16092357969358910197)
XLA Ops:
  0.0 0.1 pad_add_fusion.ids
  0.1 2.0 %shard_map.64 = (bf16[64,4096]{1,0:T(8,128)(2,1)S(1)}, bf16[528,128]{1,0:T(8,128)(2,1)S(1)}) custom-call(s32[2]{0:T(128)S(1)} %pad_add_fusion.ids, bf16[64,4096]{1,0:T(8,128)(2,1)} %bitcast.10, bf16[4096]{0:T(1024)(128)(2,1)} %refs_1_.1, s32[8,64]{1,0:T(8,128)} %bitcast.18, f32[8,64]{1,0:T(8,128)} %bitcast.19), custom_call_target="tpu_custom_call" | custom-call | tf_op jit(solution)/shard_map/pallas_call | solution.py:79
  2.0 5.1 %collective-permute-start.2 = (bf16[528,128]{1,0:T(8,128)(2,1)S(1)}, bf16[528,128]{1,0:T(8,128)(2,1)S(1)}, u32[]{:S(2)}, u32[]{:S(2)}) collective-permute-start(bf16[528,128]{1,0:T(8,128)(2,1)S(1)} %get-tuple-element.24.refs_0_), channel_id=1, source_target_pairs={{0,3},{1,2},{2,1},{3,0},{4,7},{5,6},{6,5},{7,4},{8,11},{9,10},{10,... | collective-permute-start | bytes 405512 | tf_op jit(solution)/shard_map/ppermute | solution.py:41
  7.2 0.6 collective-permute-start
  7.8 8.7 %shard_map.65.refs_3_.refs_9_ = bf16[2,9,2,384,1024]{4,3,2,1,0:T(8,128)(2,1)S(1)} custom-call(s32[2]{0:T(128)S(1)} %pad_add_fusion.ids, bf16[8,2,384,4096]{3,2,1,0:T(8,128)(2,1)} %refs_4_.5, bf16[8,4,384,1024]{3,2,1,0:T(8,128)(2,1)} %bitcast.12), custom_call_target="tpu_custom_call" | custom-call | bytes 25165824 | tf_op jit(solution)/shard_map/pallas_call | solution.py:206
  16.6 2.0 %collective-permute-done.1.refs_1_.refs_2_ = bf16[528,128]{1,0:T(8,128)(2,1)S(1)} collective-permute-done((bf16[528,128]{1,0:T(8,128)(2,1)S(1)}, bf16[528,128]{1,0:T(8,128)(2,1)S(1)}, u32[]{:S(2)}, u32[]{:S(2)}) %collective-permute-start.1) | collective-permute-done | bytes 135200 | tf_op jit(solution)/shard_map/ppermute | solution.py:41
  18.6 0.1 shard_map.66.refs_5_
  18.7 0.1 collective-permute-start.3
  18.7 1.6 %collective-permute-start.4 = (bf16[192,1024]{1,0:T(8,128)(2,1)S(1)}, bf16[192,1024]{1,0:T(8,128)(2,1)S(1)}, u32[]{:S(2)}, u32[]{:S(2)}) collective-permute-start(bf16[192,1024]{1,0:T(8,128)(2,1)S(1)} %shard_map.66.refs_5_), channel_id=1, source_target_pairs={{0,8},{4,12},{8,0},{12,4},{1,9},{5,13},{9,1},{13,5},{2,10},{6,14},... | collective-permute-start | bytes 1179656 | tf_op jit(solution)/shard_map/ppermute | solution.py:41
  20.3 0.2 collective-permute-done.3.refs_6_
  20.5 9.8 %shard_map.67 = (f32[8,64,768]{2,1,0:T(8,128)S(1)}, bf16[2,9,2,384,1024]{4,3,2,1,0:T(8,128)(2,1)S(1)}, bf16[4,128,64]{2,1,0:T(8,128)(2,1)S(1)}, bf16[4,64,128]{2,1,0:T(8,128)(2,1)S(1)}, bf16[4,64,128]{2,1,0:T(8,128)(2,1)S(1)}) custom-call(s32[2]{0:T(128)S(1)} %pad_add_fusion.ids, ...), custom_call_target="tpu_custom_call", output_to_operand_aliasing={{1}: (10, {})} | custom-call | bytes 50331648 | tf_op jit(solution)/shard_map/pallas_call | solution.py:307
  30.2 0.0 collective-permute-done.4.block
  30.3 0.2 collective-permute-start.5
  30.5 3.4 %shard_map.69 = (f32[5,64,768]{2,1,0:T(8,128)S(1)}, bf16[2,9,2,384,1024]{4,3,2,1,0:T(8,128)(2,1)S(1)}) custom-call(s32[2]{0:T(128)S(1)} %pad_add_fusion.ids, bf16[4,128,64]{2,1,0:T(8,128)(2,1)S(1)} %get-tuple-element.26.refs_0_, bf16[64,4096]{1,0:T(8,128)(2,1)S(1)} %get-tuple-element.25.refs_4_.refs_1_, ...), custom_call_target="tpu_custom_call", output_to_operand_aliasing={{1}: (7, {})} | custom-call | bytes 15728640 | tf_op jit(solution)/shard_map/pallas_call | solution.py:307
  34.0 3.9 %shard_map.70 = (bf16[5,64,384]{2,1,0:T(8,128)(2,1)S(1)}, bf16[2,9,2,384,1024]{4,3,2,1,0:T(8,128)(2,1)S(1)}) custom-call(s32[2]{0:T(128)S(1)} %pad_add_fusion.ids, bf16[4,128,64]{2,1,0:T(8,128)(2,1)S(1)} %get-tuple-element.26.refs_0_, bf16[64,4096]{1,0:T(8,128)(2,1)S(1)} %get-tuple-element.25.refs_4_.refs_1_, ...), custom_call_target="tpu_custom_call", output_to_operand_aliasing={{1}: (7, {})} | custom-call | bytes 15728640 | tf_op jit(solution)/shard_map/pallas_call | solution.py:307
  37.9 1.6 %collective-permute-start.6 = (bf16[5,64,384]{2,1,0:T(8,128)(2,1)S(1)}, bf16[5,64,384]{2,1,0:T(8,128)(2,1)S(1)}, u32[]{:S(2)}, u32[]{:S(2)}) collective-permute-start(bf16[5,64,384]{2,1,0:T(8,128)(2,1)S(1)} %get-tuple-element.31.refs_0_), channel_id=1, source_target_pairs={{0,8},{4,12},{8,0},{12,4},{1,9},{5,13},{9,1},{13,5},{2,10},{6,14},... | collective-permute-start | bytes 737288 | tf_op jit(solution)/shard_map/ppermute | solution.py:41
  39.4 0.1 collective-permute-start.9
  39.5 4.5 %shard_map.71 = (bf16[3,64,384]{2,1,0:T(8,128)(2,1)S(1)}, bf16[2,9,2,384,1024]{4,3,2,1,0:T(8,128)(2,1)S(1)}) custom-call(s32[2]{0:T(128)S(1)} %pad_add_fusion.ids, bf16[4,128,64]{2,1,0:T(8,128)(2,1)S(1)} %get-tuple-element.26.refs_0_, bf16[64,4096]{1,0:T(8,128)(2,1)S(1)} %get-tuple-element.25.refs_4_.refs_1_, ...), custom_call_target="tpu_custom_call", output_to_operand_aliasing={{1}: (8, {})} | custom-call | bytes 18874368 | tf_op jit(solution)/shard_map/pallas_call | solution.py:307
  44.1 0.6 collective-permute-start.8
  44.7 1.5 %collective-permute-done.6.refs_2_ = bf16[5,64,384]{2,1,0:T(8,128)(2,1)S(1)} collective-permute-done((bf16[5,64,384]{2,1,0:T(8,128)(2,1)S(1)}, bf16[5,64,384]{2,1,0:T(8,128)(2,1)S(1)}, u32[]{:S(2)}, u32[]{:S(2)}) %collective-permute-start.6) | collective-permute-done | bytes 245792 | tf_op jit(solution)/shard_map/ppermute | solution.py:41
  46.2 0.5 collective-permute-start.11
  46.7 3.9 %shard_map.72 = (f32[8,64,1024]{2,1,0:T(8,128)S(1)}, bf16[2,9,2,384,1024]{4,3,2,1,0:T(8,128)(2,1)S(1)}) custom-call(s32[2]{0:T(128)S(1)} %pad_add_fusion.ids, bf16[5,64,384]{2,1,0:T(8,128)(2,1)S(1)} %get-tuple-element.31.refs_0_, bf16[5,64,384]{2,1,0:T(8,128)(2,1)S(1)} %collective-permute-done.9.refs_1_, ...), custom_call_target="tpu_custom_call", output_to_operand_aliasing={{1}: (7, {})} | custom-call | bytes 8388608 | tf_op jit(solution)/shard_map/pallas_call | solution.py:373
  50.6 0.0 copy-start
  50.6 0.1 collective-permute-start.10
  50.7 1.5 %shard_map.74.refs_3_ = f32[8,64,1024]{2,1,0:T(8,128)S(1)} custom-call(s32[2]{0:T(128)S(1)} %pad_add_fusion.ids, bf16[3,64,384]{2,1,0:T(8,128)(2,1)S(1)} %collective-permute-done.11.refs_0_, bf16[3,64,384]{2,1,0:T(8,128)(2,1)S(1)} %shard_map.73.refs_1_, f32[8,64,1024]{2,1,0:T(8,128)S(1)} %get-tuple-element.35.after.refs_2_, ...), custom_call_target="tpu_custom_call", output_to_operand_aliasing={{}: (3, {})} | custom-call | bytes 4194304 | tf_op jit(solution)/shard_map/pallas_call | solution.py:373
  52.3 2.2 %shard_map.75 = (bf16[64,1024]{1,0:T(8,128)(2,1)S(1)}, bf16[64,1024]{1,0:T(8,128)(2,1)S(1)}, bf16[64,1024]{1,0:T(8,128)(2,1)S(1)}, bf16[64,1024]{1,0:T(8,128)(2,1)S(1)}) custom-call(s32[2]{0:T(128)S(1)} %pad_add_fusion.ids, bf16[5,64,384]{2,1,0:T(8,128)(2,1)S(1)} %collective-permute-done.7.refs_0_, bf16[3,64,384]{2,1,0:T(8,128)(2,1)S(1)} %collective-permute-done.10.refs_1_, ...), custom_call_target="tpu_custom_call" | custom-call | tf_op jit(solution)/shard_map/pallas_call | solution.py:418
  54.5 1.6 %collective-permute-start.12 = (bf16[64,1024]{1,0:T(8,128)(2,1)S(1)}, bf16[64,1024]{1,0:T(8,128)(2,1)S(1)}, u32[]{:S(2)}, u32[]{:S(2)}) collective-permute-start(bf16[64,1024]{1,0:T(8,128)(2,1)S(1)} %get-tuple-element.39), channel_id=1, source_target_pairs={{0,16},{1,17},{2,18},{3,19},{16,0},{17,1},{18,2},{19,3},{4,20},{5,... | collective-permute-start | bytes 393224 | tf_op jit(solution)/shard_map/ppermute | solution.py:502
  56.1 4.0 %collective-permute-start.14 = (bf16[64,1024]{1,0:T(8,128)(2,1)S(1)}, bf16[64,1024]{1,0:T(8,128)(2,1)S(1)}, u32[]{:S(2)}, u32[]{:S(2)}) collective-permute-start(bf16[64,1024]{1,0:T(8,128)(2,1)S(1)} %get-tuple-element.41), channel_id=1, source_target_pairs={{0,18},{1,19},{2,16},{3,17},{16,2},{17,3},{18,0},{19,1},{4,22},{5,... | collective-permute-start | bytes 393224 | tf_op jit(solution)/shard_map/ppermute | solution.py:502
  60.0 1.3 %collective-permute-start.15 = (bf16[64,1024]{1,0:T(8,128)(2,1)S(1)}, bf16[64,1024]{1,0:T(8,128)(2,1)S(1)}, u32[]{:S(2)}, u32[]{:S(2)}) collective-permute-start(bf16[64,1024]{1,0:T(8,128)(2,1)S(1)} %get-tuple-element.42), channel_id=1, source_target_pairs={{0,19},{1,18},{2,17},{3,16},{16,3},{17,2},{18,1},{19,0},{4,23},{5,... | collective-permute-start | bytes 393224 | tf_op jit(solution)/shard_map/ppermute | solution.py:502
  61.3 3.6 %collective-permute-done.12.refs_0_ = bf16[64,1024]{1,0:T(8,128)(2,1)S(1)} collective-permute-done((bf16[64,1024]{1,0:T(8,128)(2,1)S(1)}, bf16[64,1024]{1,0:T(8,128)(2,1)S(1)}, u32[]{:S(2)}, u32[]{:S(2)}) %collective-permute-start.12) | collective-permute-done | bytes 131104 | tf_op jit(solution)/shard_map/ppermute | solution.py:502
  64.9 5.1 %collective-permute-done.14.refs_2_ = bf16[64,1024]{1,0:T(8,128)(2,1)S(1)} collective-permute-done((bf16[64,1024]{1,0:T(8,128)(2,1)S(1)}, bf16[64,1024]{1,0:T(8,128)(2,1)S(1)}, u32[]{:S(2)}, u32[]{:S(2)}) %collective-permute-start.14) | collective-permute-done | bytes 131104 | tf_op jit(solution)/shard_map/ppermute | solution.py:502
  70.0 0.7 %shard_map.76 = bf16[1,64,1024]{2,1,0:T(8,128)(2,1)} custom-call(bf16[64,1024]{1,0:T(8,128)(2,1)S(1)} %collective-permute-done.12.refs_0_, bf16[64,1024]{1,0:T(8,128)(2,1)S(1)} %collective-permute-done.13.refs_1_, bf16[64,1024]{1,0:T(8,128)(2,1)S(1)} %collective-permute-done.14.refs_2_, bf16[64,1024]{1,0:T(8,128)(2,1)S(1)} %collective-permute-done.15.refs_3_), custom_call_target="tpu_custom_call" | custom-call | tf_op jit(solution)/shard_map/pallas_call | solution.py:503
  (16 shorter events, 0.1 us)
Async XLA Ops:
  2.0 14.5 %collective-permute-start.2 = (bf16[528,128]{1,0:T(8,128)(2,1)S(1)}, bf16[528,128]{1,0:T(8,128)(2,1)S(1)}, u32[]{:S(2)}, u32[]{:S(2)}) collective-permute-start(bf16[528,128]{1,0:T(8,128)(2,1)S(1)} %get-tuple-element.24.refs_0_), channel_id=1, source_target_pairs={{0,3},{1,2},{2,1},{3,0},{4,7},{5,6},{6,5},{7,4},{8,11},{9,10},{10,... | collective-permute-start | bytes 405512 | tf_op jit(solution)/shard_map/ppermute | solution.py:41
  7.2 11.4 %collective-permute-start.1 = (bf16[528,128]{1,0:T(8,128)(2,1)S(1)}, bf16[528,128]{1,0:T(8,128)(2,1)S(1)}, u32[]{:S(2)}, u32[]{:S(2)}) collective-permute-start(bf16[528,128]{1,0:T(8,128)(2,1)S(1)} %get-tuple-element.24.refs_0_), channel_id=1, source_target_pairs={{0,2},{1,3},{2,0},{3,1},{4,6},{5,7},{6,4},{7,5},{8,10},{9,11},{10,... | collective-permute-start | bytes 405512 | tf_op jit(solution)/shard_map/ppermute | solution.py:41
  7.2 11.4 %collective-permute-start = (bf16[528,128]{1,0:T(8,128)(2,1)S(1)}, bf16[528,128]{1,0:T(8,128)(2,1)S(1)}, u32[]{:S(2)}, u32[]{:S(2)}) collective-permute-start(bf16[528,128]{1,0:T(8,128)(2,1)S(1)} %get-tuple-element.24.refs_0_), channel_id=1, source_target_pairs={{0,1},{1,0},{2,3},{3,2},{4,5},{5,4},{6,7},{7,6},{8,9},{9,8},{10,11... | collective-permute-start | bytes 405512 | tf_op jit(solution)/shard_map/ppermute | solution.py:41
  18.7 1.8 %collective-permute-start.3 = (bf16[192,1024]{1,0:T(8,128)(2,1)S(1)}, bf16[192,1024]{1,0:T(8,128)(2,1)S(1)}, u32[]{:S(2)}, u32[]{:S(2)}) collective-permute-start(bf16[192,1024]{1,0:T(8,128)(2,1)S(1)} %shard_map.66.refs_5_), channel_id=1, source_target_pairs={{0,4},{4,0},{8,12},{12,8},{1,5},{5,1},{9,13},{13,9},{2,6},{6,2},{1... | collective-permute-start | bytes 1179656 | tf_op jit(solution)/shard_map/ppermute | solution.py:41
  18.7 11.5 %collective-permute-start.4 = (bf16[192,1024]{1,0:T(8,128)(2,1)S(1)}, bf16[192,1024]{1,0:T(8,128)(2,1)S(1)}, u32[]{:S(2)}, u32[]{:S(2)}) collective-permute-start(bf16[192,1024]{1,0:T(8,128)(2,1)S(1)} %shard_map.66.refs_5_), channel_id=1, source_target_pairs={{0,8},{4,12},{8,0},{12,4},{1,9},{5,13},{9,1},{13,5},{2,10},{6,14},... | collective-permute-start | bytes 1179656 | tf_op jit(solution)/shard_map/ppermute | solution.py:41
  30.3 3.6 %collective-permute-start.5 = (bf16[192,1024]{1,0:T(8,128)(2,1)S(1)}, bf16[192,1024]{1,0:T(8,128)(2,1)S(1)}, u32[]{:S(2)}, u32[]{:S(2)}) collective-permute-start(bf16[192,1024]{1,0:T(8,128)(2,1)S(1)} %shard_map.68.refs_2_), channel_id=1, source_target_pairs={{0,4},{4,0},{8,12},{12,8},{1,5},{5,1},{9,13},{13,9},{2,6},{6,2},{1... | collective-permute-start | bytes 1179656 | tf_op jit(solution)/shard_map/ppermute | solution.py:41
  37.9 8.3 %collective-permute-start.6 = (bf16[5,64,384]{2,1,0:T(8,128)(2,1)S(1)}, bf16[5,64,384]{2,1,0:T(8,128)(2,1)S(1)}, u32[]{:S(2)}, u32[]{:S(2)}) collective-permute-start(bf16[5,64,384]{2,1,0:T(8,128)(2,1)S(1)} %get-tuple-element.31.refs_0_), channel_id=1, source_target_pairs={{0,8},{4,12},{8,0},{12,4},{1,9},{5,13},{9,1},{13,5},{2,10},{6,14},... | collective-permute-start | bytes 737288 | tf_op jit(solution)/shard_map/ppermute | solution.py:41
  39.4 7.2 %collective-permute-start.9 = (bf16[5,64,384]{2,1,0:T(8,128)(2,1)S(1)}, bf16[5,64,384]{2,1,0:T(8,128)(2,1)S(1)}, u32[]{:S(2)}, u32[]{:S(2)}) collective-permute-start(bf16[5,64,384]{2,1,0:T(8,128)(2,1)S(1)} %get-tuple-element.31.refs_0_), channel_id=1, source_target_pairs={{0,4},{4,0},{8,12},{12,8},{1,5},{5,1},{9,13},{13,9},{2,6},{6,2},{1... | collective-permute-start | bytes 737288 | tf_op jit(solution)/shard_map/ppermute | solution.py:41
  44.1 6.5 %collective-permute-start.8 = (bf16[3,64,384]{2,1,0:T(8,128)(2,1)S(1)}, bf16[3,64,384]{2,1,0:T(8,128)(2,1)S(1)}, u32[]{:S(2)}, u32[]{:S(2)}) collective-permute-start(bf16[3,64,384]{2,1,0:T(8,128)(2,1)S(1)} %get-tuple-element.33.refs_3_), channel_id=1, source_target_pairs={{0,8},{4,12},{8,0},{12,4},{1,9},{5,13},{9,1},{13,5},{2,10},{6,14},... | collective-permute-start | bytes 442376 | tf_op jit(solution)/shard_map/ppermute | solution.py:41
  46.2 6.1 %collective-permute-start.7 = (bf16[5,64,384]{2,1,0:T(8,128)(2,1)S(1)}, bf16[5,64,384]{2,1,0:T(8,128)(2,1)S(1)}, u32[]{:S(2)}, u32[]{:S(2)}) collective-permute-start(bf16[5,64,384]{2,1,0:T(8,128)(2,1)S(1)} %collective-permute-done.6.refs_2_), channel_id=1, source_target_pairs={{0,4},{4,0},{8,12},{12,8},{1,5},{5,1},{9,13},{13,9},{2,6},{6,2},{1... | collective-permute-start | bytes 737288 | tf_op jit(solution)/shard_map/ppermute | solution.py:41
  46.2 4.5 %collective-permute-start.11 = (bf16[3,64,384]{2,1,0:T(8,128)(2,1)S(1)}, bf16[3,64,384]{2,1,0:T(8,128)(2,1)S(1)}, u32[]{:S(2)}, u32[]{:S(2)}) collective-permute-start(bf16[3,64,384]{2,1,0:T(8,128)(2,1)S(1)} %get-tuple-element.33.refs_3_), channel_id=1, source_target_pairs={{0,4},{4,0},{8,12},{12,8},{1,5},{5,1},{9,13},{13,9},{2,6},{6,2},{1... | collective-permute-start | bytes 442376 | tf_op jit(solution)/shard_map/ppermute | solution.py:41
  50.6 1.7 %copy-start = (bf16[1,64,4096]{2,1,0:T(8,128)(2,1)S(1)}, bf16[1,64,4096]{2,1,0:T(8,128)(2,1)}, u32[]{:S(2)}) copy-start(bf16[1,64,4096]{2,1,0:T(8,128)(2,1)} %param.6) | copy-start | bytes 1572868
  50.6 1.6 %collective-permute-start.10 = (bf16[3,64,384]{2,1,0:T(8,128)(2,1)S(1)}, bf16[3,64,384]{2,1,0:T(8,128)(2,1)S(1)}, u32[]{:S(2)}, u32[]{:S(2)}) collective-permute-start(bf16[3,64,384]{2,1,0:T(8,128)(2,1)S(1)} %shard_map.73.refs_1_), channel_id=1, source_target_pairs={{0,4},{4,0},{8,12},{12,8},{1,5},{5,1},{9,13},{13,9},{2,6},{6,2},{1... | collective-permute-start | bytes 442376 | tf_op jit(solution)/shard_map/ppermute | solution.py:41
  54.5 10.4 %collective-permute-start.12 = (bf16[64,1024]{1,0:T(8,128)(2,1)S(1)}, bf16[64,1024]{1,0:T(8,128)(2,1)S(1)}, u32[]{:S(2)}, u32[]{:S(2)}) collective-permute-start(bf16[64,1024]{1,0:T(8,128)(2,1)S(1)} %get-tuple-element.39), channel_id=1, source_target_pairs={{0,16},{1,17},{2,18},{3,19},{16,0},{17,1},{18,2},{19,3},{4,20},{5,... | collective-permute-start | bytes 393224 | tf_op jit(solution)/shard_map/ppermute | solution.py:502
  56.1 8.8 %collective-permute-start.13 = (bf16[64,1024]{1,0:T(8,128)(2,1)S(1)}, bf16[64,1024]{1,0:T(8,128)(2,1)S(1)}, u32[]{:S(2)}, u32[]{:S(2)}) collective-permute-start(bf16[64,1024]{1,0:T(8,128)(2,1)S(1)} %get-tuple-element.40), channel_id=1, source_target_pairs={{0,17},{1,16},{2,19},{3,18},{16,1},{17,0},{18,3},{19,2},{4,21},{5,... | collective-permute-start | bytes 393224 | tf_op jit(solution)/shard_map/ppermute | solution.py:502
  56.1 13.9 %collective-permute-start.14 = (bf16[64,1024]{1,0:T(8,128)(2,1)S(1)}, bf16[64,1024]{1,0:T(8,128)(2,1)S(1)}, u32[]{:S(2)}, u32[]{:S(2)}) collective-permute-start(bf16[64,1024]{1,0:T(8,128)(2,1)S(1)} %get-tuple-element.41), channel_id=1, source_target_pairs={{0,18},{1,19},{2,16},{3,17},{16,2},{17,3},{18,0},{19,1},{4,22},{5,... | collective-permute-start | bytes 393224 | tf_op jit(solution)/shard_map/ppermute | solution.py:502
  60.0 10.0 %collective-permute-start.15 = (bf16[64,1024]{1,0:T(8,128)(2,1)S(1)}, bf16[64,1024]{1,0:T(8,128)(2,1)S(1)}, u32[]{:S(2)}, u32[]{:S(2)}) collective-permute-start(bf16[64,1024]{1,0:T(8,128)(2,1)S(1)} %get-tuple-element.42), channel_id=1, source_target_pairs={{0,19},{1,18},{2,17},{3,16},{16,3},{17,2},{18,1},{19,0},{4,23},{5,... | collective-permute-start | bytes 393224 | tf_op jit(solution)/shard_map/ppermute | solution.py:502

commit v5 on v4

--- a/solution.py
+++ b/solution.py
@@ -142,10 +142,11 @@
     rest = jnp.zeros((LANES - 2 * top, count), jnp.float32)
     table = jnp.concatenate([names, values, rest]).T
     weight = jnp.zeros((count, slots), jnp.float32)
+    named = jnp.zeros((count, slots), jnp.float32)
     for k in range(top):
         hit = table[:, k : k + 1] == expert
         weight = jnp.where(hit, table[:, top + k : top + k + 1], weight)
-    named = jnp.where(weight > 0, 1.0, 0.0)
+        named = jnp.where(hit, 1.0, named)
     for i in range(len(blocks)):
         own = slice(i * tokens, (i + 1) * tokens)
         ranks = jnp.dot(earlier, named[own].astype(jnp.bfloat16), preferred_element_type=jnp.float32)

time: 70.9 us -> 70.9 us (level)
  no operation moved by 1% of the time
where the time goes in v5:
time: 70.9 us; the launch traced here: 70.7 us
  Pallas kernels  40.8 us (58%)
  starting transfers between devices  17.2 us (24%)
  waiting for transfers between devices  12.5 us (18%)
    pallas_call x4, Pallas kernels, up_step(): pl.pallas_call(functools.partial(up_kernel, opts), out_shape=shapes, in_s...  21.6 us
    ppermute x12, starting transfers between devices, flipped(): lax.ppermute(block, axis, [(i, i ^ bit) for i in range(lax.axis_size(axis...  10.4 us
    pallas_call x1, Pallas kernels, stage(): pl.pallas_call(stage_kernel, out_shape=pltpu.VMEM(shape, wide.dtype), in_...  8.73 us
    ppermute x4, waiting for transfers between devices, gathered_tokens(): received.append(lax.ppermute(sums[j], ('section', 'expert'), route))  8.7 us
    ppermute x4, starting transfers between devices, gathered_tokens(): received.append(lax.ppermute(sums[j], ('section', 'expert'), route))  6.81 us
    pallas_call x2, Pallas kernels, down_step(): pl.pallas_call(functools.partial(down_kernel, groups, pieces, total is no...  5.4 us
    ppermute x12, waiting for transfers between devices, flipped(): lax.ppermute(block, axis, [(i, i ^ bit) for i in range(lax.axis_size(axis...  3.75 us
    pallas_call x1, Pallas kernels, finish_step(): pl.pallas_call(functools.partial(finish_kernel, (groups, quarter)), out_s...  2.2 us
  transfers between devices with their start and end apart: 16, of which 5 were waited for; matrix products, arithmetic and copies ran while one was open for 0% of the time, Pallas kernels for 45%

profile of v5, /device:TPU:0, one launch (start us, length us, event | category | flops | bytes accessed | tf_op | source)
XLA Modules:
  0.0 70.7 jit_solution(17454876738695765080)
XLA Ops:
  0.0 0.1 pad_add_fusion.ids
  0.1 2.0 %shard_map.64 = (bf16[64,4096]{1,0:T(8,128)(2,1)S(1)}, bf16[528,128]{1,0:T(8,128)(2,1)S(1)}) custom-call(s32[2]{0:T(128)S(1)} %pad_add_fusion.ids, bf16[64,4096]{1,0:T(8,128)(2,1)} %bitcast.10, bf16[4096]{0:T(1024)(128)(2,1)} %refs_1_.1, s32[8,64]{1,0:T(8,128)} %bitcast.18, f32[8,64]{1,0:T(8,128)} %bitcast.19), custom_call_target="tpu_custom_call" | custom-call | tf_op jit(solution)/shard_map/pallas_call | solution.py:79
  2.0 5.1 %collective-permute-start.2 = (bf16[528,128]{1,0:T(8,128)(2,1)S(1)}, bf16[528,128]{1,0:T(8,128)(2,1)S(1)}, u32[]{:S(2)}, u32[]{:S(2)}) collective-permute-start(bf16[528,128]{1,0:T(8,128)(2,1)S(1)} %get-tuple-element.24.refs_0_), channel_id=1, source_target_pairs={{0,3},{1,2},{2,1},{3,0},{4,7},{5,6},{6,5},{7,4},{8,11},{9,10},{10,... | collective-permute-start | bytes 405512 | tf_op jit(solution)/shard_map/ppermute | solution.py:41
  7.2 0.6 collective-permute-start
  7.8 8.7 %shard_map.65.refs_3_.refs_9_ = bf16[2,9,2,384,1024]{4,3,2,1,0:T(8,128)(2,1)S(1)} custom-call(s32[2]{0:T(128)S(1)} %pad_add_fusion.ids, bf16[8,2,384,4096]{3,2,1,0:T(8,128)(2,1)} %refs_4_.5, bf16[8,4,384,1024]{3,2,1,0:T(8,128)(2,1)} %bitcast.12), custom_call_target="tpu_custom_call" | custom-call | bytes 25165824 | tf_op jit(solution)/shard_map/pallas_call | solution.py:207
  16.6 2.0 %collective-permute-done.1.refs_1_.refs_2_ = bf16[528,128]{1,0:T(8,128)(2,1)S(1)} collective-permute-done((bf16[528,128]{1,0:T(8,128)(2,1)S(1)}, bf16[528,128]{1,0:T(8,128)(2,1)S(1)}, u32[]{:S(2)}, u32[]{:S(2)}) %collective-permute-start.1) | collective-permute-done | bytes 135200 | tf_op jit(solution)/shard_map/ppermute | solution.py:41
  18.6 0.1 shard_map.66.refs_5_
  18.7 0.1 collective-permute-start.3
  18.7 1.6 %collective-permute-start.4 = (bf16[192,1024]{1,0:T(8,128)(2,1)S(1)}, bf16[192,1024]{1,0:T(8,128)(2,1)S(1)}, u32[]{:S(2)}, u32[]{:S(2)}) collective-permute-start(bf16[192,1024]{1,0:T(8,128)(2,1)S(1)} %shard_map.66.refs_5_), channel_id=1, source_target_pairs={{0,8},{4,12},{8,0},{12,4},{1,9},{5,13},{9,1},{13,5},{2,10},{6,14},... | collective-permute-start | bytes 1179656 | tf_op jit(solution)/shard_map/ppermute | solution.py:41
  20.3 0.2 collective-permute-done.3.refs_6_
  20.5 9.8 %shard_map.67 = (f32[8,64,768]{2,1,0:T(8,128)S(1)}, bf16[2,9,2,384,1024]{4,3,2,1,0:T(8,128)(2,1)S(1)}, bf16[4,128,64]{2,1,0:T(8,128)(2,1)S(1)}, bf16[4,64,128]{2,1,0:T(8,128)(2,1)S(1)}, bf16[4,64,128]{2,1,0:T(8,128)(2,1)S(1)}) custom-call(s32[2]{0:T(128)S(1)} %pad_add_fusion.ids, ...), custom_call_target="tpu_custom_call", output_to_operand_aliasing={{1}: (10, {})} | custom-call | bytes 50331648 | tf_op jit(solution)/shard_map/pallas_call | solution.py:308
  30.2 0.0 collective-permute-done.4.block
  30.3 0.2 collective-permute-start.5
  30.5 3.4 %shard_map.69 = (f32[5,64,768]{2,1,0:T(8,128)S(1)}, bf16[2,9,2,384,1024]{4,3,2,1,0:T(8,128)(2,1)S(1)}) custom-call(s32[2]{0:T(128)S(1)} %pad_add_fusion.ids, bf16[4,128,64]{2,1,0:T(8,128)(2,1)S(1)} %get-tuple-element.26.refs_0_, bf16[64,4096]{1,0:T(8,128)(2,1)S(1)} %get-tuple-element.25.refs_4_.refs_1_, ...), custom_call_target="tpu_custom_call", output_to_operand_aliasing={{1}: (7, {})} | custom-call | bytes 15728640 | tf_op jit(solution)/shard_map/pallas_call | solution.py:308
  33.9 3.9 %shard_map.70 = (bf16[5,64,384]{2,1,0:T(8,128)(2,1)S(1)}, bf16[2,9,2,384,1024]{4,3,2,1,0:T(8,128)(2,1)S(1)}) custom-call(s32[2]{0:T(128)S(1)} %pad_add_fusion.ids, bf16[4,128,64]{2,1,0:T(8,128)(2,1)S(1)} %get-tuple-element.26.refs_0_, bf16[64,4096]{1,0:T(8,128)(2,1)S(1)} %get-tuple-element.25.refs_4_.refs_1_, ...), custom_call_target="tpu_custom_call", output_to_operand_aliasing={{1}: (7, {})} | custom-call | bytes 15728640 | tf_op jit(solution)/shard_map/pallas_call | solution.py:308
  37.8 1.5 %collective-permute-start.6 = (bf16[5,64,384]{2,1,0:T(8,128)(2,1)S(1)}, bf16[5,64,384]{2,1,0:T(8,128)(2,1)S(1)}, u32[]{:S(2)}, u32[]{:S(2)}) collective-permute-start(bf16[5,64,384]{2,1,0:T(8,128)(2,1)S(1)} %get-tuple-element.31.refs_0_), channel_id=1, source_target_pairs={{0,8},{4,12},{8,0},{12,4},{1,9},{5,13},{9,1},{13,5},{2,10},{6,14},... | collective-permute-start | bytes 737288 | tf_op jit(solution)/shard_map/ppermute | solution.py:41
  39.4 0.1 collective-permute-start.9
  39.5 4.5 %shard_map.71 = (bf16[3,64,384]{2,1,0:T(8,128)(2,1)S(1)}, bf16[2,9,2,384,1024]{4,3,2,1,0:T(8,128)(2,1)S(1)}) custom-call(s32[2]{0:T(128)S(1)} %pad_add_fusion.ids, bf16[4,128,64]{2,1,0:T(8,128)(2,1)S(1)} %get-tuple-element.26.refs_0_, bf16[64,4096]{1,0:T(8,128)(2,1)S(1)} %get-tuple-element.25.refs_4_.refs_1_, ...), custom_call_target="tpu_custom_call", output_to_operand_aliasing={{1}: (8, {})} | custom-call | bytes 18874368 | tf_op jit(solution)/shard_map/pallas_call | solution.py:308
  44.1 0.6 collective-permute-start.8
  44.7 1.5 %collective-permute-done.6.refs_2_ = bf16[5,64,384]{2,1,0:T(8,128)(2,1)S(1)} collective-permute-done((bf16[5,64,384]{2,1,0:T(8,128)(2,1)S(1)}, bf16[5,64,384]{2,1,0:T(8,128)(2,1)S(1)}, u32[]{:S(2)}, u32[]{:S(2)}) %collective-permute-start.6) | collective-permute-done | bytes 245792 | tf_op jit(solution)/shard_map/ppermute | solution.py:41
  46.2 0.5 collective-permute-start.11
  46.7 3.9 %shard_map.72 = (f32[8,64,1024]{2,1,0:T(8,128)S(1)}, bf16[2,9,2,384,1024]{4,3,2,1,0:T(8,128)(2,1)S(1)}) custom-call(s32[2]{0:T(128)S(1)} %pad_add_fusion.ids, bf16[5,64,384]{2,1,0:T(8,128)(2,1)S(1)} %get-tuple-element.31.refs_0_, bf16[5,64,384]{2,1,0:T(8,128)(2,1)S(1)} %collective-permute-done.9.refs_1_, ...), custom_call_target="tpu_custom_call", output_to_operand_aliasing={{1}: (7, {})} | custom-call | bytes 8388608 | tf_op jit(solution)/shard_map/pallas_call | solution.py:374
  50.6 0.0 copy-start
  50.6 0.1 collective-permute-start.10
  50.7 1.5 %shard_map.74.refs_3_ = f32[8,64,1024]{2,1,0:T(8,128)S(1)} custom-call(s32[2]{0:T(128)S(1)} %pad_add_fusion.ids, bf16[3,64,384]{2,1,0:T(8,128)(2,1)S(1)} %collective-permute-done.11.refs_0_, bf16[3,64,384]{2,1,0:T(8,128)(2,1)S(1)} %shard_map.73.refs_1_, f32[8,64,1024]{2,1,0:T(8,128)S(1)} %get-tuple-element.35.after.refs_2_, ...), custom_call_target="tpu_custom_call", output_to_operand_aliasing={{}: (3, {})} | custom-call | bytes 4194304 | tf_op jit(solution)/shard_map/pallas_call | solution.py:374
  52.3 2.2 %shard_map.75 = (bf16[64,1024]{1,0:T(8,128)(2,1)S(1)}, bf16[64,1024]{1,0:T(8,128)(2,1)S(1)}, bf16[64,1024]{1,0:T(8,128)(2,1)S(1)}, bf16[64,1024]{1,0:T(8,128)(2,1)S(1)}) custom-call(s32[2]{0:T(128)S(1)} %pad_add_fusion.ids, bf16[5,64,384]{2,1,0:T(8,128)(2,1)S(1)} %collective-permute-done.7.refs_0_, bf16[3,64,384]{2,1,0:T(8,128)(2,1)S(1)} %collective-permute-done.10.refs_1_, ...), custom_call_target="tpu_custom_call" | custom-call | tf_op jit(solution)/shard_map/pallas_call | solution.py:419
  54.5 1.6 %collective-permute-start.12 = (bf16[64,1024]{1,0:T(8,128)(2,1)S(1)}, bf16[64,1024]{1,0:T(8,128)(2,1)S(1)}, u32[]{:S(2)}, u32[]{:S(2)}) collective-permute-start(bf16[64,1024]{1,0:T(8,128)(2,1)S(1)} %get-tuple-element.39), channel_id=1, source_target_pairs={{0,16},{1,17},{2,18},{3,19},{16,0},{17,1},{18,2},{19,3},{4,20},{5,... | collective-permute-start | bytes 393224 | tf_op jit(solution)/shard_map/ppermute | solution.py:503
  56.1 4.0 %collective-permute-start.14 = (bf16[64,1024]{1,0:T(8,128)(2,1)S(1)}, bf16[64,1024]{1,0:T(8,128)(2,1)S(1)}, u32[]{:S(2)}, u32[]{:S(2)}) collective-permute-start(bf16[64,1024]{1,0:T(8,128)(2,1)S(1)} %get-tuple-element.41), channel_id=1, source_target_pairs={{0,18},{1,19},{2,16},{3,17},{16,2},{17,3},{18,0},{19,1},{4,22},{5,... | collective-permute-start | bytes 393224 | tf_op jit(solution)/shard_map/ppermute | solution.py:503
  60.0 1.3 %collective-permute-start.15 = (bf16[64,1024]{1,0:T(8,128)(2,1)S(1)}, bf16[64,1024]{1,0:T(8,128)(2,1)S(1)}, u32[]{:S(2)}, u32[]{:S(2)}) collective-permute-start(bf16[64,1024]{1,0:T(8,128)(2,1)S(1)} %get-tuple-element.42), channel_id=1, source_target_pairs={{0,19},{1,18},{2,17},{3,16},{16,3},{17,2},{18,1},{19,0},{4,23},{5,... | collective-permute-start | bytes 393224 | tf_op jit(solution)/shard_map/ppermute | solution.py:503
  61.3 3.5 %collective-permute-done.12.refs_0_ = bf16[64,1024]{1,0:T(8,128)(2,1)S(1)} collective-permute-done((bf16[64,1024]{1,0:T(8,128)(2,1)S(1)}, bf16[64,1024]{1,0:T(8,128)(2,1)S(1)}, u32[]{:S(2)}, u32[]{:S(2)}) %collective-permute-start.12) | collective-permute-done | bytes 131104 | tf_op jit(solution)/shard_map/ppermute | solution.py:503
  64.8 5.2 %collective-permute-done.14.refs_2_ = bf16[64,1024]{1,0:T(8,128)(2,1)S(1)} collective-permute-done((bf16[64,1024]{1,0:T(8,128)(2,1)S(1)}, bf16[64,1024]{1,0:T(8,128)(2,1)S(1)}, u32[]{:S(2)}, u32[]{:S(2)}) %collective-permute-start.14) | collective-permute-done | bytes 131104 | tf_op jit(solution)/shard_map/ppermute | solution.py:503
  70.0 0.7 %shard_map.76 = bf16[1,64,1024]{2,1,0:T(8,128)(2,1)} custom-call(bf16[64,1024]{1,0:T(8,128)(2,1)S(1)} %collective-permute-done.12.refs_0_, bf16[64,1024]{1,0:T(8,128)(2,1)S(1)} %collective-permute-done.13.refs_1_, bf16[64,1024]{1,0:T(8,128)(2,1)S(1)} %collective-permute-done.14.refs_2_, bf16[64,1024]{1,0:T(8,128)(2,1)S(1)} %collective-permute-done.15.refs_3_), custom_call_target="tpu_custom_call" | custom-call | tf_op jit(solution)/shard_map/pallas_call | solution.py:504
  (16 shorter events, 0.1 us)
Async XLA Ops:
  2.0 14.5 %collective-permute-start.2 = (bf16[528,128]{1,0:T(8,128)(2,1)S(1)}, bf16[528,128]{1,0:T(8,128)(2,1)S(1)}, u32[]{:S(2)}, u32[]{:S(2)}) collective-permute-start(bf16[528,128]{1,0:T(8,128)(2,1)S(1)} %get-tuple-element.24.refs_0_), channel_id=1, source_target_pairs={{0,3},{1,2},{2,1},{3,0},{4,7},{5,6},{6,5},{7,4},{8,11},{9,10},{10,... | collective-permute-start | bytes 405512 | tf_op jit(solution)/shard_map/ppermute | solution.py:41
  7.2 11.4 %collective-permute-start.1 = (bf16[528,128]{1,0:T(8,128)(2,1)S(1)}, bf16[528,128]{1,0:T(8,128)(2,1)S(1)}, u32[]{:S(2)}, u32[]{:S(2)}) collective-permute-start(bf16[528,128]{1,0:T(8,128)(2,1)S(1)} %get-tuple-element.24.refs_0_), channel_id=1, source_target_pairs={{0,2},{1,3},{2,0},{3,1},{4,6},{5,7},{6,4},{7,5},{8,10},{9,11},{10,... | collective-permute-start | bytes 405512 | tf_op jit(solution)/shard_map/ppermute | solution.py:41
  7.2 11.4 %collective-permute-start = (bf16[528,128]{1,0:T(8,128)(2,1)S(1)}, bf16[528,128]{1,0:T(8,128)(2,1)S(1)}, u32[]{:S(2)}, u32[]{:S(2)}) collective-permute-start(bf16[528,128]{1,0:T(8,128)(2,1)S(1)} %get-tuple-element.24.refs_0_), channel_id=1, source_target_pairs={{0,1},{1,0},{2,3},{3,2},{4,5},{5,4},{6,7},{7,6},{8,9},{9,8},{10,11... | collective-permute-start | bytes 405512 | tf_op jit(solution)/shard_map/ppermute | solution.py:41
  18.7 1.8 %collective-permute-start.3 = (bf16[192,1024]{1,0:T(8,128)(2,1)S(1)}, bf16[192,1024]{1,0:T(8,128)(2,1)S(1)}, u32[]{:S(2)}, u32[]{:S(2)}) collective-permute-start(bf16[192,1024]{1,0:T(8,128)(2,1)S(1)} %shard_map.66.refs_5_), channel_id=1, source_target_pairs={{0,4},{4,0},{8,12},{12,8},{1,5},{5,1},{9,13},{13,9},{2,6},{6,2},{1... | collective-permute-start | bytes 1179656 | tf_op jit(solution)/shard_map/ppermute | solution.py:41
  18.7 11.5 %collective-permute-start.4 = (bf16[192,1024]{1,0:T(8,128)(2,1)S(1)}, bf16[192,1024]{1,0:T(8,128)(2,1)S(1)}, u32[]{:S(2)}, u32[]{:S(2)}) collective-permute-start(bf16[192,1024]{1,0:T(8,128)(2,1)S(1)} %shard_map.66.refs_5_), channel_id=1, source_target_pairs={{0,8},{4,12},{8,0},{12,4},{1,9},{5,13},{9,1},{13,5},{2,10},{6,14},... | collective-permute-start | bytes 1179656 | tf_op jit(solution)/shard_map/ppermute | solution.py:41
  30.3 3.6 %collective-permute-start.5 = (bf16[192,1024]{1,0:T(8,128)(2,1)S(1)}, bf16[192,1024]{1,0:T(8,128)(2,1)S(1)}, u32[]{:S(2)}, u32[]{:S(2)}) collective-permute-start(bf16[192,1024]{1,0:T(8,128)(2,1)S(1)} %shard_map.68.refs_2_), channel_id=1, source_target_pairs={{0,4},{4,0},{8,12},{12,8},{1,5},{5,1},{9,13},{13,9},{2,6},{6,2},{1... | collective-permute-start | bytes 1179656 | tf_op jit(solution)/shard_map/ppermute | solution.py:41
  37.8 8.3 %collective-permute-start.6 = (bf16[5,64,384]{2,1,0:T(8,128)(2,1)S(1)}, bf16[5,64,384]{2,1,0:T(8,128)(2,1)S(1)}, u32[]{:S(2)}, u32[]{:S(2)}) collective-permute-start(bf16[5,64,384]{2,1,0:T(8,128)(2,1)S(1)} %get-tuple-element.31.refs_0_), channel_id=1, source_target_pairs={{0,8},{4,12},{8,0},{12,4},{1,9},{5,13},{9,1},{13,5},{2,10},{6,14},... | collective-permute-start | bytes 737288 | tf_op jit(solution)/shard_map/ppermute | solution.py:41
  39.4 7.3 %collective-permute-start.9 = (bf16[5,64,384]{2,1,0:T(8,128)(2,1)S(1)}, bf16[5,64,384]{2,1,0:T(8,128)(2,1)S(1)}, u32[]{:S(2)}, u32[]{:S(2)}) collective-permute-start(bf16[5,64,384]{2,1,0:T(8,128)(2,1)S(1)} %get-tuple-element.31.refs_0_), channel_id=1, source_target_pairs={{0,4},{4,0},{8,12},{12,8},{1,5},{5,1},{9,13},{13,9},{2,6},{6,2},{1... | collective-permute-start | bytes 737288 | tf_op jit(solution)/shard_map/ppermute | solution.py:41
  44.1 6.5 %collective-permute-start.8 = (bf16[3,64,384]{2,1,0:T(8,128)(2,1)S(1)}, bf16[3,64,384]{2,1,0:T(8,128)(2,1)S(1)}, u32[]{:S(2)}, u32[]{:S(2)}) collective-permute-start(bf16[3,64,384]{2,1,0:T(8,128)(2,1)S(1)} %get-tuple-element.33.refs_3_), channel_id=1, source_target_pairs={{0,8},{4,12},{8,0},{12,4},{1,9},{5,13},{9,1},{13,5},{2,10},{6,14},... | collective-permute-start | bytes 442376 | tf_op jit(solution)/shard_map/ppermute | solution.py:41
  46.2 6.1 %collective-permute-start.7 = (bf16[5,64,384]{2,1,0:T(8,128)(2,1)S(1)}, bf16[5,64,384]{2,1,0:T(8,128)(2,1)S(1)}, u32[]{:S(2)}, u32[]{:S(2)}) collective-permute-start(bf16[5,64,384]{2,1,0:T(8,128)(2,1)S(1)} %collective-permute-done.6.refs_2_), channel_id=1, source_target_pairs={{0,4},{4,0},{8,12},{12,8},{1,5},{5,1},{9,13},{13,9},{2,6},{6,2},{1... | collective-permute-start | bytes 737288 | tf_op jit(solution)/shard_map/ppermute | solution.py:41
  46.2 4.5 %collective-permute-start.11 = (bf16[3,64,384]{2,1,0:T(8,128)(2,1)S(1)}, bf16[3,64,384]{2,1,0:T(8,128)(2,1)S(1)}, u32[]{:S(2)}, u32[]{:S(2)}) collective-permute-start(bf16[3,64,384]{2,1,0:T(8,128)(2,1)S(1)} %get-tuple-element.33.refs_3_), channel_id=1, source_target_pairs={{0,4},{4,0},{8,12},{12,8},{1,5},{5,1},{9,13},{13,9},{2,6},{6,2},{1... | collective-permute-start | bytes 442376 | tf_op jit(solution)/shard_map/ppermute | solution.py:41
  50.6 1.7 %copy-start = (bf16[1,64,4096]{2,1,0:T(8,128)(2,1)S(1)}, bf16[1,64,4096]{2,1,0:T(8,128)(2,1)}, u32[]{:S(2)}) copy-start(bf16[1,64,4096]{2,1,0:T(8,128)(2,1)} %param.6) | copy-start | bytes 1572868
  50.6 1.6 %collective-permute-start.10 = (bf16[3,64,384]{2,1,0:T(8,128)(2,1)S(1)}, bf16[3,64,384]{2,1,0:T(8,128)(2,1)S(1)}, u32[]{:S(2)}, u32[]{:S(2)}) collective-permute-start(bf16[3,64,384]{2,1,0:T(8,128)(2,1)S(1)} %shard_map.73.refs_1_), channel_id=1, source_target_pairs={{0,4},{4,0},{8,12},{12,8},{1,5},{5,1},{9,13},{13,9},{2,6},{6,2},{1... | collective-permute-start | bytes 442376 | tf_op jit(solution)/shard_map/ppermute | solution.py:41
  54.5 10.3 %collective-permute-start.12 = (bf16[64,1024]{1,0:T(8,128)(2,1)S(1)}, bf16[64,1024]{1,0:T(8,128)(2,1)S(1)}, u32[]{:S(2)}, u32[]{:S(2)}) collective-permute-start(bf16[64,1024]{1,0:T(8,128)(2,1)S(1)} %get-tuple-element.39), channel_id=1, source_target_pairs={{0,16},{1,17},{2,18},{3,19},{16,0},{17,1},{18,2},{19,3},{4,20},{5,... | collective-permute-start | bytes 393224 | tf_op jit(solution)/shard_map/ppermute | solution.py:503
  56.1 8.8 %collective-permute-start.13 = (bf16[64,1024]{1,0:T(8,128)(2,1)S(1)}, bf16[64,1024]{1,0:T(8,128)(2,1)S(1)}, u32[]{:S(2)}, u32[]{:S(2)}) collective-permute-start(bf16[64,1024]{1,0:T(8,128)(2,1)S(1)} %get-tuple-element.40), channel_id=1, source_target_pairs={{0,17},{1,16},{2,19},{3,18},{16,1},{17,0},{18,3},{19,2},{4,21},{5,... | collective-permute-start | bytes 393224 | tf_op jit(solution)/shard_map/ppermute | solution.py:503
  56.1 13.9 %collective-permute-start.14 = (bf16[64,1024]{1,0:T(8,128)(2,1)S(1)}, bf16[64,1024]{1,0:T(8,128)(2,1)S(1)}, u32[]{:S(2)}, u32[]{:S(2)}) collective-permute-start(bf16[64,1024]{1,0:T(8,128)(2,1)S(1)} %get-tuple-element.41), channel_id=1, source_target_pairs={{0,18},{1,19},{2,16},{3,17},{16,2},{17,3},{18,0},{19,1},{4,22},{5,... | collective-permute-start | bytes 393224 | tf_op jit(solution)/shard_map/ppermute | solution.py:503
  60.0 10.0 %collective-permute-start.15 = (bf16[64,1024]{1,0:T(8,128)(2,1)S(1)}, bf16[64,1024]{1,0:T(8,128)(2,1)S(1)}, u32[]{:S(2)}, u32[]{:S(2)}) collective-permute-start(bf16[64,1024]{1,0:T(8,128)(2,1)S(1)} %get-tuple-element.42), channel_id=1, source_target_pairs={{0,19},{1,18},{2,17},{3,16},{16,3},{17,2},{18,1},{19,0},{4,23},{5,... | collective-permute-start | bytes 393224 | tf_op jit(solution)/shard_map/ppermute | solution.py:503
